TPU v7x, 32 devices: a whole 2x2x4 slice. The times are simulated.
32 devices in a mesh: dp: 4 (over z), context: 2 (over core), tensor: 4 (over y, x).
Axes of the slice: x: 2, y: 2, z: 4, core: 2. Of those that a mesh axis runs over, the one named last changes fastest.
Arguments:
- tokens: bfloat16 [8192, 2048], P(('dp', 'context')), may hold values from -6 to 6
- cotangent: bfloat16 [8192, 2048], P(('dp', 'context')), may hold values from -6 to 6
- lengths: int32 [4, 4], P('dp'), may hold values from 1 to 1024, as said below
- in_weight: float32 [2048, 7, 2048], P('dp', None, 'tensor'), may hold values from -0.125 to 0.125
- out_weight: float32 [5, 2048, 2048], P(None, 'tensor', 'dp')
- vectors: float32 [10, 2048], replicated
- in_first: float32 [2048, 7, 2048], P('dp', None, 'tensor'), may hold values from -27.1529 to 27.1529
- in_second: float32 [2048, 7, 2048], P('dp', None, 'tensor'), may hold values from 57.344 to 409.6
- out_first: float32 [5, 2048, 2048], P(None, 'tensor', 'dp'), may hold values from -27.1529 to 27.1529
- out_second: float32 [5, 2048, 2048], P(None, 'tensor', 'dp'), may hold values from 57.344 to 409.6
- vec_first: float32 [10, 2048], replicated, may hold values from -27.1529 to 27.1529
- vec_second: float32 [10, 2048], replicated, may hold values from 57.344 to 409.6
Outputs:
- result: bfloat16 [8192, 2048], P(('dp', 'context'), 'tensor')
- token_grad: float32 [8192, 2048], P(('dp', 'context'), 'tensor')
- new_in: float32 [2048, 7, 2048], P('dp', None, 'tensor')
- new_in_first: float32 [2048, 7, 2048], P('dp', None, 'tensor')
- new_in_second: float32 [2048, 7, 2048], P('dp', None, 'tensor')
- new_out: float32 [5, 2048, 2048], P(None, 'tensor', 'dp')
- new_out_first: float32 [5, 2048, 2048], P(None, 'tensor', 'dp')
- new_out_second: float32 [5, 2048, 2048], P(None, 'tensor', 'dp')
- new_vectors: float32 [10, 2048], replicated
- new_vec_first: float32 [10, 2048], replicated
- new_vec_second: float32 [10, 2048], replicated
Inputs may be any that keep to these rules, and one draw needn't show every extreme that they name: `lengths`: each row sums to 2048; its largest length is 1024.
All inputs are finite; a program needn't handle non-finite values.
Results may differ from a plain program's by a relative error of at most 0.0044.
The roundings to bfloat16 on the way count: a program that leaves them out, or rounds other values in their place, can miss the bound.
Values may be sent and summed in bfloat16 or wider, within the bound.
A program may use at most 384 MiB of HBM per device.

v0:
```python
import jax
import jax.numpy as jnp
from jax import lax
from jax.sharding import PartitionSpec as P

HD = 64
ROT = 32
STEP = 10
NIN = 7


norm_eps = 1e-05
beta_one = 0.9
beta_two = 0.95
adam_eps = 1e-08
weight_decay = 0.1
rate_matrix = 0.02
rate_vector = 0.4


def layout(lengths_row, row_span):
    seg_ends = jnp.cumsum(lengths_row)
    seg_starts = seg_ends - lengths_row
    places = jnp.arange(row_span, dtype=jnp.int32)
    segment = jnp.sum((places[:, None] >= seg_ends[None, :]).astype(jnp.int32), 1)
    numbers = jnp.arange(lengths_row.shape[0], dtype=jnp.int32)
    seg_begin = jnp.sum(jnp.where(segment[:, None] == numbers[None, :], seg_starts[None, :], 0), 1)
    return (segment, places - seg_begin)


def rotate(flat_in, places, turn_sign):
    row_count = flat_in.shape[0]
    per_head = flat_in.reshape(row_count, flat_in.shape[1] // HD, HD)
    half_rot = ROT // 2
    frequency = 10000.0 ** (-2.0 * jnp.arange(half_rot, dtype=jnp.float32) / ROT)
    angles = turn_sign * places.astype(jnp.float32)[:, None] * frequency[None, :]
    cosine = jnp.cos(angles)[:, None, :]
    sine_part = jnp.sin(angles)[:, None, :]
    first_half = per_head[:, :, :half_rot]
    second_half = per_head[:, :, half_rot:ROT]
    turned = jnp.concatenate(
        [
            first_half * cosine - second_half * sine_part,
            second_half * cosine + first_half * sine_part,
            per_head[:, :, ROT:],
        ],
        2,
    )
    return turned.reshape(row_count, flat_in.shape[1])


def gelu_tanh(hidden_in):
    return jax.nn.gelu(hidden_in, approximate=True)


def adamw(master, gradient, moment_one, moment_two, step_rate, decay_rate):
    first_new = beta_one * moment_one + (1.0 - beta_one) * gradient
    second_new = beta_two * moment_two + (1.0 - beta_two) * gradient * gradient
    first_hat = first_new / (1.0 - beta_one**STEP)
    second_hat = second_new / (1.0 - beta_two**STEP)
    updated = master - step_rate * (
        first_hat / (jnp.sqrt(second_hat) + adam_eps) + decay_rate * master
    )
    return (updated, first_new, second_new)


def block_masks(segment_block, index_block, key_segment):
    key_index = jnp.arange(key_segment.shape[0], dtype=jnp.int32)
    return (segment_block[:, None] == key_segment[None, :]) & (
        key_index[None, :] <= index_block[:, None]
    )


def attend_forward(queries, keys_all, values_all, query_segment, query_index, key_segment):
    local_rows = queries.shape[0]
    slice_width = queries.shape[1]
    head_count = slice_width // HD
    block_rows = min(512, local_rows)
    blocks = local_rows // block_rows
    row_span = keys_all.shape[0]
    key_heads = keys_all.reshape(row_span, head_count, HD)
    value_heads = values_all.reshape(row_span, head_count, HD)

    def one_block(block_item):
        query_block, segment_block, index_block = block_item
        scores = jnp.einsum(
            "qhe,khe->hqk", query_block, key_heads, preferred_element_type=jnp.float32
        ) * HD ** (-0.5)
        allowed = block_masks(segment_block, index_block, key_segment)
        scores = jnp.where(allowed[None], scores, -1e30)
        row_max = jnp.max(scores, -1, keepdims=True)
        exp_scores = jnp.exp(scores - row_max)
        exp_total = jnp.sum(exp_scores, -1, keepdims=True)
        probs_low = (exp_scores / exp_total).astype(jnp.bfloat16)
        block_out = jnp.einsum(
            "hqk,khe->qhe", probs_low, value_heads, preferred_element_type=jnp.float32
        )
        return (block_out, (row_max + jnp.log(exp_total))[..., 0])

    block_outs, log_total = lax.map(
        one_block,
        (
            queries.reshape(blocks, block_rows, head_count, HD),
            query_segment.reshape(blocks, block_rows),
            query_index.reshape(blocks, block_rows),
        ),
    )
    return (block_outs.reshape(local_rows, slice_width), log_total)


def attend_backward(
    queries, keys_all, values_all, grad_attended, log_total, query_segment, query_index, key_segment
):
    local_rows = queries.shape[0]
    slice_width = queries.shape[1]
    head_count = slice_width // HD
    block_rows = min(512, local_rows)
    blocks = local_rows // block_rows
    row_span = keys_all.shape[0]
    key_heads = keys_all.reshape(row_span, head_count, HD)
    value_heads = values_all.reshape(row_span, head_count, HD)
    scale_factor = HD ** (-0.5)

    def one_block(block_carry, block_item):
        key_acc, value_acc = block_carry
        query_block, grad_block, total_block, segment_block, index_block = block_item
        scores = (
            jnp.einsum("qhe,khe->hqk", query_block, key_heads, preferred_element_type=jnp.float32)
            * scale_factor
        )
        allowed = block_masks(segment_block, index_block, key_segment)
        scores = jnp.where(allowed[None], scores, -1e30)
        probs_full = jnp.exp(scores - total_block[..., None])
        grad_probs = jnp.einsum(
            "qhe,khe->hqk", grad_block, value_heads, preferred_element_type=jnp.float32
        )
        row_inner = jnp.sum(probs_full * grad_probs, -1, keepdims=True)
        grad_scores = (probs_full * (grad_probs - row_inner)).astype(jnp.bfloat16)
        grad_query = (
            jnp.einsum("hqk,khe->qhe", grad_scores, key_heads, preferred_element_type=jnp.float32)
            * scale_factor
        )
        key_acc = (
            key_acc
            + jnp.einsum(
                "hqk,qhe->khe", grad_scores, query_block, preferred_element_type=jnp.float32
            )
            * scale_factor
        )
        value_acc = value_acc + jnp.einsum(
            "hqk,qhe->khe",
            probs_full.astype(jnp.bfloat16),
            grad_block,
            preferred_element_type=jnp.float32,
        )
        return ((key_acc, value_acc), grad_query)

    zero_heads = jnp.zeros((row_span, head_count, HD), jnp.float32)
    block_items = (
        queries.reshape(blocks, block_rows, head_count, HD),
        grad_attended.reshape(blocks, block_rows, head_count, HD),
        log_total,
        query_segment.reshape(blocks, block_rows),
        query_index.reshape(blocks, block_rows),
    )
    sums_end, grad_queries = lax.scan(one_block, (zero_heads, zero_heads), block_items)
    return (
        grad_queries.reshape(local_rows, slice_width),
        sums_end[0].reshape(row_span, slice_width),
        sums_end[1].reshape(row_span, slice_width),
    )


def body(
    tokens,
    cotangent,
    lengths,
    in_weight,
    out_weight,
    vectors,
    in_first,
    in_second,
    out_first,
    out_second,
    vec_first,
    vec_second,
):
    local_rows = tokens.shape[0]
    model_width = tokens.shape[1]
    slice_width = in_weight.shape[2]
    context_count = lax.axis_size("context")
    context_index = lax.axis_index("context")
    tensor_count = lax.axis_size("tensor")
    tensor_index = lax.axis_index("tensor")
    row_span = local_rows * context_count
    segment_all, place_all = layout(lengths[0], row_span)
    first_row = context_index * local_rows
    query_segment = lax.dynamic_slice_in_dim(segment_all, first_row, local_rows, 0)
    query_place = lax.dynamic_slice_in_dim(place_all, first_row, local_rows, 0)
    query_index = first_row + jnp.arange(local_rows, dtype=jnp.int32)
    in_full, out_full = (
        lax.all_gather(in_weight.astype(jnp.bfloat16), "dp", axis=0, tiled=True),
        lax.all_gather(out_weight.astype(jnp.bfloat16), "dp", axis=2, tiled=True),
    )
    inputs = tokens.astype(jnp.float32)
    centered = inputs - jnp.mean(inputs, 1, keepdims=True)
    inv_dev = lax.rsqrt(jnp.mean(centered * centered, 1, keepdims=True) + norm_eps)
    unit_rows = centered * inv_dev
    norm_gain = vectors[NIN + 1]
    normed = (unit_rows * norm_gain + vectors[NIN + 2]).astype(jnp.bfloat16)
    column = tensor_index * slice_width
    in_bias = lax.dynamic_slice_in_dim(vectors[:NIN], column, slice_width, 1)
    projected = (
        jnp.einsum("td,dgc->tgc", normed, in_full, preferred_element_type=jnp.float32)
        + in_bias[None]
    )
    queries = rotate(projected[:, 0], query_place, 1.0).astype(jnp.bfloat16)
    keys_own = rotate(projected[:, 1], query_place, 1.0).astype(jnp.bfloat16)
    values_own = projected[:, 2].astype(jnp.bfloat16)
    hidden_pre = projected[:, 3:]
    activated = gelu_tanh(hidden_pre).astype(jnp.bfloat16)
    keys_all, values_all = (
        lax.all_gather(keys_own, "context", axis=0, tiled=True),
        lax.all_gather(values_own, "context", axis=0, tiled=True),
    )
    attended, log_total = attend_forward(
        queries, keys_all, values_all, query_segment, query_index, segment_all
    )
    branch_in = jnp.concatenate([attended.astype(jnp.bfloat16)[:, None], activated], 1)
    partial_out = jnp.einsum("tgc,gcd->td", branch_in, out_full, preferred_element_type=jnp.float32)
    branch = lax.psum_scatter(partial_out, "tensor", scatter_dimension=1, tiled=True)
    out_width = branch.shape[1]
    out_column = tensor_index * out_width
    residual = lax.dynamic_slice_in_dim(inputs, out_column, out_width, 1)
    out_bias = lax.dynamic_slice_in_dim(vectors[NIN], out_column, out_width, 0)
    result = (residual + (branch + out_bias[None])).astype(jnp.bfloat16)
    grad_mixed = jnp.einsum("td,gcd->tgc", cotangent, out_full, preferred_element_type=jnp.float32)
    out_partial = jnp.einsum(
        "tgc,td->gcd", branch_in, cotangent, preferred_element_type=jnp.float32
    )
    grad_attended = grad_mixed[:, 0].astype(jnp.bfloat16)
    gelu_pull = jax.vjp(gelu_tanh, hidden_pre)[1]
    grad_hidden = gelu_pull(grad_mixed[:, 1:])[0]
    grad_query, key_partial, value_partial = attend_backward(
        queries,
        keys_all,
        values_all,
        grad_attended,
        log_total,
        query_segment,
        query_index,
        segment_all,
    )
    key_grad, value_grad = (
        lax.psum_scatter(key_partial, "context", scatter_dimension=0, tiled=True),
        lax.psum_scatter(value_partial, "context", scatter_dimension=0, tiled=True),
    )
    grad_projected = jnp.concatenate(
        [
            rotate(grad_query, query_place, -1.0)[:, None],
            rotate(key_grad, query_place, -1.0)[:, None],
            value_grad[:, None],
            grad_hidden,
        ],
        1,
    ).astype(jnp.bfloat16)
    norm_partial = jnp.einsum(
        "tgc,dgc->td", grad_projected, in_full, preferred_element_type=jnp.float32
    )
    in_partial = jnp.einsum(
        "td,tgc->dgc", normed, grad_projected, preferred_element_type=jnp.float32
    )
    bias_grad = jnp.sum(grad_projected.astype(jnp.float32), 0)
    cot_row = jnp.sum(cotangent.astype(jnp.float32), 0) / tensor_count
    grad_normed = lax.psum(norm_partial, "tensor")
    grad_unit = grad_normed * norm_gain
    grad_inputs = inv_dev * (
        grad_unit
        - jnp.mean(grad_unit, 1, keepdims=True)
        - unit_rows * jnp.mean(grad_unit * unit_rows, 1, keepdims=True)
    ) + cotangent.astype(jnp.float32)
    token_grad = lax.dynamic_slice_in_dim(grad_inputs, out_column, out_width, 1)
    shared_rows = jnp.stack(
        [
            cot_row,
            jnp.sum(grad_normed * unit_rows, 0) / tensor_count,
            jnp.sum(grad_normed, 0) / tensor_count,
        ],
        0,
    )
    bias_rows = lax.dynamic_update_slice_in_dim(
        jnp.zeros((NIN, model_width), jnp.float32), bias_grad, column, 1
    )
    vector_grad = lax.psum(
        jnp.concatenate([bias_rows, shared_rows], 0), ("dp", "context", "tensor")
    )
    new_vectors, new_vec_first, new_vec_second = adamw(
        vectors, vector_grad, vec_first, vec_second, rate_vector, 0.0
    )
    in_context, out_context = lax.psum((in_partial, out_partial), "context")
    in_sum, out_sum = (
        lax.psum_scatter(in_context, "dp", scatter_dimension=0, tiled=True),
        lax.psum_scatter(out_context, "dp", scatter_dimension=2, tiled=True),
    )
    new_in, new_in_first, new_in_second = adamw(
        in_weight, in_sum, in_first, in_second, rate_matrix, weight_decay
    )
    new_out, new_out_first, new_out_second = adamw(
        out_weight, out_sum, out_first, out_second, rate_matrix, weight_decay
    )
    return (
        result,
        token_grad,
        new_in,
        new_in_first,
        new_in_second,
        new_out,
        new_out_first,
        new_out_second,
        new_vectors,
        new_vec_first,
        new_vec_second,
    )


def solution(mesh):
    return jax.shard_map(
        body,
        mesh=mesh,
        in_specs=(
            P(("dp", "context"), None),
            P(("dp", "context"), None),
            P("dp", None),
            P("dp", None, "tensor"),
            P(None, "tensor", "dp"),
            P(),
            P("dp", None, "tensor"),
            P("dp", None, "tensor"),
            P(None, "tensor", "dp"),
            P(None, "tensor", "dp"),
            P(),
            P(),
        ),
        out_specs=(
            P(("dp", "context"), "tensor"),
            P(("dp", "context"), "tensor"),
            P("dp", None, "tensor"),
            P("dp", None, "tensor"),
            P("dp", None, "tensor"),
            P(None, "tensor", "dp"),
            P(None, "tensor", "dp"),
            P(None, "tensor", "dp"),
            P(),
            P(),
            P(),
        ),
        check_vma=False,
    )
```

profile of v0, /device:TPU:0, one launch (start us, length us, event | category | flops | bytes accessed | tf_op | source)
XLA Modules:
  0.0 2219.8 jit_solution(14289239576846316016)
XLA Ops:
  27.6 242.0 %all-gather.6.cloned.1.call-done = bf16[2048,7,512]{0,2,1:T(8,128)(2,1)} async-done(((bf16[512,7,512]{0,2,1:T(8,128)(2,1)}), bf16[2048,7,512]{0,2,1:T(8,128)(2,1)}) %all-gather.6.cloned.1.call-update) | async-done | bytes 14680080 | tf_op jit(solution)/shard_map/all_gather | solution.py:202
  269.5 20.1 convolution_add_fusion
  298.6 155.2 %all-gather.10.cloned.1.call-done = bf16[5,512,2048]{2,1,0:T(8,128)(2,1)} async-done(((bf16[5,512,512]{2,1,0:T(8,128)(2,1)}), bf16[5,512,2048]{2,1,0:T(8,128)(2,1)}) %all-gather.10.cloned.1.call-update) | async-done | bytes 10485776 | tf_op jit(solution)/shard_map/all_gather | solution.py:203
  478.7 94.5 %while.27 = (s32[]{:T(128)}, bf16[2,512,8,64]{1,3,2,0:T(8,128)(2,1)}, f32[2,8,512]{2,1,0:T(8,128)S(1)}, s32[2,512]{1,0:T(2,128)S(1)}, s32[2048]{0:T(1024)S(1)}, ...) while((s32[]{:T(128)}, ...), condition=%wide.region_8.9_spmd, body=%wide.region_5.8_spmd.sunk | while | flops 2251288576 | bytes 119165080 | solution.py:100
  573.2 268.3 %while.28 = (s32[]{:T(128)}, f32[2048,8,64]{0,2,1:T(8,128)}, f32[2048,8,64]{0,2,1:T(8,128)}, f32[2,512,8,64]{1,0,3,2:T(2,128)}, bf16[2,512,8,64]{1,3,2,0:T(8,128...) while((s32[]{:T(128)}, f32[2048,8,64]{0,2,1:T(8,128)}, ...), condition=%wide.region_12.13_spmd.clone, body=%wide.region_10.12_spmd.clone.sunk | while | flops 5452853248 | bytes 296849600 | solution.py:166
  584.8 17.5 fusion.106
  603.6 24.7 %multiply_reduce_fusion.5 = (f32[8,512]{1,0:T(8,128)S(1)}, f32[8,512,2048]{2,1,0:T(8,128)}) fusion(f32[8,512,2048]{2,1,0:T(8,128)} %fusion.106, f32[8,512]{1,0:T(8,128)S(1)} %dynamic-slice_bitcast_fusion.2, bf16[2048,8,64]{0,2,1:T(8,128)(2,1)S(1)} %copy-done, bf16[2,512,8,64]{1,3,2,0:T(8,128)(2,1)} %get-tuple-element.525, s32[]{:T(128)S(6)} %copy.98, ...), kind=kOutput, calls=%fused_computation.20.clone.1 | convolution fusion | flops 1115680768 | bytes 70811648 | tf_op jit(solution)/shard_map/while/body/eval_jaxpr/qhe,khe->hqk/dot_general | solution.py:128
  628.3 27.4 %multiply_convert_fusion.3 = bf16[8,512,2048]{2,1,0:T(8,128)(2,1)} fusion(f32[8,512,2048]{2,1,0:T(8,128)} %get-tuple-element.461, f32[8,512,2048]{2,1,0:T(8,128)} %fusion.106, f32[8,512]{1,0:T(8,128)S(1)} %get-tuple-element.462), kind=kLoop, calls=%fused_computation.19.clone.1 | loop fusion | flops 25165824 | bytes 83902464 | tf_op jit(solution)/shard_map/while/body/eval_jaxpr/convert_element_type | solution.py:138
  692.2 19.6 dynamic_update_slice.24
  711.8 17.5 fusion.106
  730.5 24.7 %multiply_reduce_fusion.5 = (f32[8,512]{1,0:T(8,128)S(1)}, f32[8,512,2048]{2,1,0:T(8,128)}) fusion(f32[8,512,2048]{2,1,0:T(8,128)} %fusion.106, f32[8,512]{1,0:T(8,128)S(1)} %dynamic-slice_bitcast_fusion.2, bf16[2048,8,64]{0,2,1:T(8,128)(2,1)S(1)} %copy-done, bf16[2,512,8,64]{1,3,2,0:T(8,128)(2,1)} %get-tuple-element.525, s32[]{:T(128)S(6)} %copy.98, ...), kind=kOutput, calls=%fused_computation.20.clone.1 | convolution fusion | flops 1115680768 | bytes 70811648 | tf_op jit(solution)/shard_map/while/body/eval_jaxpr/qhe,khe->hqk/dot_general | solution.py:128
  755.3 27.4 %multiply_convert_fusion.3 = bf16[8,512,2048]{2,1,0:T(8,128)(2,1)} fusion(f32[8,512,2048]{2,1,0:T(8,128)} %get-tuple-element.461, f32[8,512,2048]{2,1,0:T(8,128)} %fusion.106, f32[8,512]{1,0:T(8,128)S(1)} %get-tuple-element.462), kind=kLoop, calls=%fused_computation.19.clone.1 | loop fusion | flops 25165824 | bytes 83902464 | tf_op jit(solution)/shard_map/while/body/eval_jaxpr/convert_element_type | solution.py:138
  821.6 19.6 dynamic_update_slice.24
  880.6 22.0 convolution_bitcast_fusion
  908.7 18.4 fusion.41
  927.9 26.0 %fusion.48 = f32[2048,7,512]{2,0,1:T(8,128)} fusion(f32[2048]{0:T(1024)S(1)} %bitcast.174, f32[2048]{0:T(1024)S(1)} %bitcast.167, bf16[1024,4,512]{0,2,1:T(8,128)(2,1)} %get-tuple-element.291, bf16[1024,1,512]{0,2,1:T(8,128)(2,1)S(1)} %convert_bitcast_fusion, bf16[1024,1,512]{0,2,1:T(8,128)(2,1)S(1)} %bitcast.153, bf16[1024,1,512]{0,2,1:T(8,128)(2,1)S(1)} %bitcast.156, ...), kind=kOutput, calls=%fused_computation.114 | convolution fusion | flops 15074328576 | bytes 40919040 | tf_op jit(solution)/shard_map/td,tgc->dgc/dot_general | solution.py:270
  953.9 17.6 convolution_bitcast_fusion.1
  978.4 97.2 %all-reduce.5.cloned.1.call-done = f32[1024,2048]{1,0:T(8,128)} async-done(((f32[1024,2048]{1,0:T(8,128)}), f32[1024,2048]{1,0:T(8,128)}) %all-reduce.5.cloned.1.call-update) | async-done | bytes 8388624 | tf_op jit(solution)/shard_map/psum | solution.py:275
  1087.2 338.8 %reduce-scatter.14.cloned.1.call-done = f32[5,512,512]{2,1,0:T(8,128)} async-done(((f32[5,512,2048]{2,1,0:T(8,128)}), f32[5,512,512]{2,1,0:T(8,128)}) %reduce-scatter.14.cloned.1.call-update) | async-done | bytes 5242896 | tf_op jit(solution)/shard_map/reduce_scatter | solution.py:303
  1426.1 485.5 %reduce-scatter.12.cloned.1.call-done = f32[512,7,512]{2,0,1:T(8,128)} async-done(((f32[2048,7,512]{2,0,1:T(8,128)}), f32[512,7,512]{2,0,1:T(8,128)}) %reduce-scatter.12.cloned.1.call-update) | async-done | bytes 7340048 | tf_op jit(solution)/shard_map/reduce_scatter | solution.py:302
  1924.2 79.1 %reduce-scatter.6.cloned.1.call-done = f32[1024,512]{1,0:T(8,128)} async-done(((f32[1024,2048]{1,0:T(8,128)}), f32[1024,512]{1,0:T(8,128)}) %reduce-scatter.6.cloned.1.call-update) | async-done | bytes 2097168 | tf_op jit(solution)/shard_map/reduce_scatter | solution.py:231
  2007.0 124.8 %all-reduce.7.cloned.1.call-done = f32[10,2048]{1,0:T(8,128)} async-done(((f32[10,2048]{1,0:T(8,128)}), f32[10,2048]{1,0:T(8,128)}) %all-reduce.7.cloned.1.call-update) | async-done | bytes 81936 | tf_op jit(solution)/shard_map/psum | solution.py:294
  2133.5 49.3 %all-reduce.9.cloned.1.call-done = (f32[512,7,512]{2,0,1:T(8,128)}, f32[5,512,512]{2,1,0:T(8,128)}) async-done(((f32[512,7,512]{2,0,1:T(8,128)}, f32[5,512,512]{2,1,0:T(8,128)}), (f32[512,7,512]{2,0,1:T(8,128)}, f32[5,512,512]{2,1,0:T(8,128)})) %all-reduce.9.cloned.1.call-update) | async-done | bytes 12582928 | tf_op jit(solution)/shard_map/psum | solution.py:300
  2182.8 17.7 multiply_subtract_fusion
  (168 shorter events, 320.2 us)
Async XLA Ops:
  7.2 262.4 %all-gather.6.cloned.1.call-start = ((), (), s32[]{:S(2)}) async-start(), calls=%async_computation.5 | async-start | bytes 18350080 | tf_op jit(solution)/shard_map/all_gather | solution.py:202
  14.2 439.6 %all-gather.10.cloned.1.call-start = ((), (), s32[]{:S(2)}) async-start(), calls=%async_computation.7 | async-start | bytes 13107200 | tf_op jit(solution)/shard_map/all_gather | solution.py:203
  18.6 460.1 %all-gather.8.cloned.1.call-start = ((), (), s32[]{:S(2)}) async-start(), calls=%async_computation.6 | async-start | bytes 3145728 | tf_op jit(solution)/shard_map/all_gather | solution.py:223
  21.9 267.7 %copy-start.14 = (f32[1024]{0:T(1024)}, f32[1024]{0:T(1024)S(1)}, u32[]{:S(2)}) copy-start(f32[1024]{0:T(1024)S(1)} %broadcast_multiply_fusion.7) | copy-start | bytes 12292
  25.8 263.9 %copy-start.12 = (f32[1024]{0:T(1024)}, f32[1024]{0:T(1024)S(1)}, u32[]{:S(2)}) copy-start(f32[1024]{0:T(1024)S(1)} %add_rsqrt_fusion) | copy-start | bytes 12292
  27.6 262.1 %copy-start.16 = (f32[1,2048]{1,0:T(1,128)}, f32[1,2048]{1,0:T(1,128)S(1)}, u32[]{:S(2)}) copy-start(f32[1,2048]{1,0:T(1,128)S(1)} %get-tuple-element.308) | copy-start | bytes 24580
  27.6 262.1 %copy-start.18 = (f32[1,2048]{1,0:T(1,128)}, f32[1,2048]{1,0:T(1,128)S(1)}, u32[]{:S(2)}) copy-start(f32[1,2048]{1,0:T(1,128)S(1)} %get-tuple-element.307) | copy-start | bytes 24580
  295.5 183.3 %all-gather.12.cloned.1.call-start = ((), (), s32[]{:S(2)}) async-start(), calls=%async_computation.13 | async-start | bytes 3145728 | tf_op jit(solution)/shard_map/all_gather | solution.py:224
  298.3 576.4 %reduce-scatter.8.cloned.1.call-start = ((), (), s32[]{:S(2)}) async-start(), calls=%async_computation.9 | async-start | bytes 6291456 | tf_op jit(solution)/shard_map/reduce_scatter | solution.py:255
  495.3 15.1 copy-start.1
  584.8 18.7 copy-start
  711.8 18.7 copy-start
  841.6 37.3 %reduce-scatter.10.cloned.1.call-start = ((), (), s32[]{:S(2)}) async-start(), calls=%async_computation.10 | async-start | bytes 6291456 | tf_op jit(solution)/shard_map/reduce_scatter | solution.py:256
  842.1 233.5 %all-reduce.5.cloned.1.call-start = ((), (), s32[]{:S(2)}) async-start(), calls=%async_computation.11 | async-start | bytes 16777216 | tf_op jit(solution)/shard_map/psum | solution.py:275
  859.3 16.7 copy-start.8
  859.3 16.7 copy-start.9
  902.6 523.4 %reduce-scatter.14.cloned.1.call-start = ((), (), s32[]{:S(2)}) async-start(), calls=%async_computation.15 | async-start | bytes 26214400 | tf_op jit(solution)/shard_map/reduce_scatter | solution.py:303
  927.2 984.4 %reduce-scatter.12.cloned.1.call-start = ((), (), s32[]{:S(2)}) async-start(), calls=%async_computation.14 | async-start | bytes 36700160 | tf_op jit(solution)/shard_map/reduce_scatter | solution.py:302
  953.8 1049.4 %reduce-scatter.6.cloned.1.call-start = ((), (), s32[]{:S(2)}) async-start(), calls=%async_computation.8 | async-start | bytes 10485760 | tf_op jit(solution)/shard_map/reduce_scatter | solution.py:231
  971.5 1160.3 %all-reduce.7.cloned.1.call-start = ((), (), s32[]{:S(2)}) async-start(), calls=%async_computation.12 | async-start | bytes 262144 | tf_op jit(solution)/shard_map/psum | solution.py:294
  1087.2 1095.6 %all-reduce.9.cloned.1.call-start = ((), (), s32[]{:S(2)}) async-start(), calls=%async_computation.16 | async-start | bytes 25165824 | tf_op jit(solution)/shard_map/psum | solution.py:300
  1919.3 212.5 %copy-start.7 = (f32[10,2048]{1,0:T(8,128)S(1)}, f32[10,2048]{1,0:T(8,128)}, u32[]{:S(2)}) copy-start(f32[10,2048]{1,0:T(8,128)} %param.21) | copy-start | bytes 245764
  1919.3 212.5 %copy-start.10 = (f32[10,2048]{1,0:T(8,128)S(1)}, f32[10,2048]{1,0:T(8,128)}, u32[]{:S(2)}) copy-start(f32[10,2048]{1,0:T(8,128)} %param.26) | copy-start | bytes 245764
  1919.3 212.5 %copy-start.11 = (f32[10,2048]{1,0:T(8,128)S(1)}, f32[10,2048]{1,0:T(8,128)}, u32[]{:S(2)}) copy-start(f32[10,2048]{1,0:T(8,128)} %param.27) | copy-start | bytes 245764
  (13 other events, 75.3 us)
Sparse Core Ops, SparseCore 0:
  14.3 255.1 all-gather.5
  271.7 182.0 all-gather.9
  455.9 8.7 all-gather.7
  466.7 11.7 all-gather.11
  841.7 12.9 reduce-scatter.7
  857.5 13.3 reduce-scatter.9
  902.7 172.8 all-reduce.4
  1078.1 347.8 reduce-scatter.13
  1428.4 483.0 reduce-scatter.11
  1914.8 88.4 reduce-scatter.5
  2009.4 122.3 all-reduce.6
  2134.2 48.5 all-reduce.8
where the time goes:
time: 2230 us; the launch traced here: 2220 us
  waiting for transfers between devices  1570 us (70%)
  matrix products  338 us (15%)
  other arithmetic  186 us (8%)
  local copies, waits for them, and re-layouts  94.5 us (4%)
    reduce_scatter x1, waiting for transfers between devices, body(): lax.psum_scatter(in_context, 'dp', scatter_dimension=0, tiled=True)  485 us
    reduce_scatter x1, waiting for transfers between devices, body(): lax.psum_scatter(out_context, 'dp', scatter_dimension=2, tiled=True)  339 us
    all_gather x1, waiting for transfers between devices, body(): lax.all_gather(in_weight.astype(jnp.bfloat16), 'dp', axis=0, tiled=True)  242 us
    all_gather x1, waiting for transfers between devices, body(): lax.all_gather(out_weight.astype(jnp.bfloat16), 'dp', axis=2, tiled=True)  155 us
    psum x1, waiting for transfers between devices, body(): lax.psum(jnp.concatenate([bias_rows, shared_rows], 0), ('dp', 'context',...  125 us
    psum x1, waiting for transfers between devices, body(): grad_normed = lax.psum(norm_partial, 'tensor')  97.2 us
    dot_general x4, matrix products, one_block(): jnp.einsum('qhe,khe->hqk', query_block, key_heads, preferred_element_type...  79.6 us
    reduce_scatter x1, waiting for transfers between devices, body(): lax.psum_scatter(partial_out, 'tensor', scatter_dimension=1, tiled=True)  79.1 us
  transfers between devices with their start and end apart: 12, of which 8 were waited for; matrix products, arithmetic and copies ran while one was open for 9% of the time, Pallas kernels for 0%

commit v1 on v0

v1 whole, which is shorter than its diff:
```python
import functools

import jax
import jax.numpy as jnp
from jax import lax
from jax.experimental import pallas as pl
from jax.experimental.pallas import tpu as pltpu
from jax.sharding import PartitionSpec as P

HD = 64
ROT = 32
STEP = 10
NIN = 7
MESH = pl.DeviceIdType.MESH
VMEM_LIMIT = 60 * 2**20

norm_eps = 1e-05
beta_one = 0.9
beta_two = 0.95
adam_eps = 1e-08
weight_decay = 0.1
rate_matrix = 0.02
rate_vector = 0.4


def adamw(master, gradient, moment_one, moment_two, step_rate, decay_rate):
    first_new = beta_one * moment_one + (1.0 - beta_one) * gradient
    second_new = beta_two * moment_two + (1.0 - beta_two) * gradient * gradient
    first_hat = first_new / (1.0 - beta_one**STEP)
    second_hat = second_new / (1.0 - beta_two**STEP)
    updated = master - step_rate * (
        first_hat / (jnp.sqrt(second_hat) + adam_eps) + decay_rate * master
    )
    return (updated, first_new, second_new)


def gelu_tanh(hidden_in):
    return jax.nn.gelu(hidden_in, approximate=True)


LANES = 2 * HD
WIDE = 4 * LANES
HID = WIDE // 2
ATT = 3 * LANES
LAG = 2

NT = (((1,), (1,)), ((), ()))
NN = (((1,), (0,)), ((), ()))
TN = (((0,), (0,)), ((), ()))


def dot(x, y, dims=NN):
    return lax.dot_general(x, y, dims, preferred_element_type=jnp.float32)


def line_barrier(n):
    z = lax.axis_index("dp")
    k = lax.axis_index("context")
    barrier = pltpu.get_barrier_semaphore()
    pl.semaphore_signal(barrier, inc=1, device_id={"context": 1 - k}, device_id_type=MESH)

    @pl.when(z < n - 1)
    def _():
        pl.semaphore_signal(barrier, inc=1, device_id={"dp": z + 1}, device_id_type=MESH)

    @pl.when(z > 0)
    def _():
        pl.semaphore_signal(barrier, inc=1, device_id={"dp": z - 1}, device_id_type=MESH)

    inner = jnp.where(z > 0, 1, 0) + jnp.where(z < n - 1, 1, 0)
    pl.semaphore_wait(barrier, 1 + inner)


def gelu_both(v):
    rate = 0.7978845608028654
    t = jnp.tanh(rate * (v + 0.044715 * (v * v * v)))
    value = 0.5 * v * (1.0 + t)
    slope = 0.5 * (1.0 + t) + 0.5 * v * (1.0 - t * t) * (rate * (1.0 + 3.0 * 0.044715 * (v * v)))
    return value, slope


def block_kernel(
    n, steps,
    own, tokens, cot_hbm, bias_ref, gain_ref, cos_ref, sin_ref, begin_ref,
    full, saved, total, swap, dkv_other,
    normed, cot, stage, wbuf, x, q_s, g_s, kv, dkv, dkv_tmp, mask, held, outgoing, swap_in, line, outbox,
    own_sem, send_sem, recv_sem, psend_sem, precv_sem,
    xsend_sem, xrecv_sem, lsend_sem, lrecv_sem, keep_sem, fsend_sem, frecv_sem,
    kvsend_sem, kvrecv_sem, dsend_sem, drecv_sem, load_sem, save_sem,
):
    units = 3 * steps
    size = own.shape[1]
    half = size // 2
    rows_all, width = normed.shape
    last = n - 1
    z = lax.axis_index("dp")
    k = lax.axis_index("context")
    mine = pl.ds(pl.multiple_of(k * half, half), half)
    theirs = pl.ds(pl.multiple_of((1 - k) * half, half), half)
    other_core = {"context": 1 - k}
    line_barrier(n)


    def hop(way, g, h, shard):
        source = own.at[g, mine] if isinstance(h, int) and h == 0 else full.at[g, shard, mine]
        return pltpu.make_async_remote_copy(
            src_ref=source,
            dst_ref=full.at[g, shard, mine],
            send_sem=send_sem.at[way, g, h],
            recv_sem=recv_sem.at[way, g, h],
            device_id={"dp": z + 1 - 2 * way},
            device_id_type=MESH,
        )

    def across(way, g, h, shard, rows):
        return pltpu.make_async_remote_copy(
            src_ref=full.at[g, shard, rows],
            dst_ref=full.at[g, shard, rows],
            send_sem=psend_sem.at[way, g, h],
            recv_sem=precv_sem.at[way, g, h],
            device_id=other_core,
            device_id_type=MESH,
        )

    def own_copy(g):
        return pltpu.make_async_copy(own.at[g], full.at[g, z], own_sem.at[g])

    def send_own(g):
        own_copy(g).start()

        @pl.when(z < last)
        def _():
            hop(0, g, 0, z).start()

        @pl.when(z > 0)
        def _():
            hop(1, g, 0, z).start()

    def gather_tick(m):
        @pl.when(m < units * last)
        def _():
            g, s = m // last, m % last + 1

            @pl.when((s == 1) & (g < units - 1))
            def _():
                send_own(g + 1)

            @pl.when(z >= s)
            def _():
                hop(0, g, s - 1, z - s).wait_recv()

                @pl.when(z < last)
                def _():
                    hop(0, g, s, z - s).start()

                across(0, g, s - 1, z - s, mine).start()

            @pl.when(z + s <= last)
            def _():
                hop(1, g, s - 1, z + s).wait_recv()

                @pl.when(z > 0)
                def _():
                    hop(1, g, s, z + s).start()

                across(1, g, s - 1, z + s, mine).start()

    def need(u):
        own_copy(u).wait()

        def one(i, carry):
            s = i + 1

            @pl.when(z >= s)
            def _():
                across(0, u, s - 1, z - s, theirs).wait_recv()

            @pl.when(z + s <= last)
            def _():
                across(1, u, s - 1, z + s, theirs).wait_recv()

            return carry

        lax.fori_loop(0, last, one, 0)
        pltpu.make_async_copy(full.at[u], wbuf, load_sem).start()
        pltpu.make_async_copy(full.at[u], wbuf, load_sem).wait()


    def exchange(g):
        return pltpu.make_async_remote_copy(
            src_ref=outgoing.at[g % 2],
            dst_ref=swap.at[g],
            send_sem=xsend_sem.at[g],
            recv_sem=xrecv_sem.at[g],
            device_id=other_core,
            device_id_type=MESH,
        )

    def slot_of(way, i):
        return i if way == 0 else n - i

    def pass_on(way, g, i):
        slot = slot_of(way, i)
        return pltpu.make_async_remote_copy(
            src_ref=line.at[g, slot],
            dst_ref=line.at[g, slot],
            send_sem=lsend_sem.at[way, g, i],
            recv_sem=lrecv_sem.at[way, g, i],
            device_id={"dp": z + 1 - 2 * way},
            device_id_type=MESH,
        )

    def keep(g):
        return pltpu.make_async_copy(outbox.at[g % (LAG + 3)], total.at[g, mine], keep_sem.at[g])

    def share(g, rows):
        return pltpu.make_async_remote_copy(
            src_ref=outbox.at[g % (LAG + 3)],
            dst_ref=total.at[g, rows],
            send_sem=fsend_sem.at[g],
            recv_sem=frecv_sem.at[g],
            device_id=other_core,
            device_id_type=MESH,
        )

    def prepare(g):
        exchange(g).wait_recv()
        pltpu.make_async_copy(swap.at[g], swap_in, load_sem).start()
        pltpu.make_async_copy(swap.at[g], swap_in, load_sem).wait()
        box = g % (LAG + 3)

        @pl.when(g >= LAG + 3)
        def _():
            keep(g - (LAG + 3)).wait()
            share(g - (LAG + 3), mine).wait_send()

        def one(j, carry):
            held[g % 3, j] += swap_in[j].astype(jnp.float32)
            return carry

        lax.fori_loop(0, n, one, 0)
        outbox[box] = held[g % 3, z]

    def scatter_step(way, m, distance):
        @pl.when((m >= 0) & (m < units * last))
        def _():
            g, i = m // last, m % last
            shard = n - 1 - i if way == 0 else i
            slot = slot_of(way, i)

            @pl.when(distance == 0)
            def _():
                line[g, slot] = held[g % 3, shard].astype(jnp.bfloat16)
                pass_on(way, g, i).start()

            @pl.when((distance > 0) & (distance <= last - i))
            def _():
                pass_on(way, g, i).wait_recv()

                @pl.when(distance < last - i)
                def _():
                    line[g, slot] = (line[g, slot].astype(jnp.float32) + held[g % 3, shard]).astype(
                        jnp.bfloat16
                    )
                    pass_on(way, g, i).start()

    def finish(g):
        box = g % (LAG + 3)

        @pl.when(z > 0)
        def _():
            outbox[box] += line[g, slot_of(0, n - 1 - z)].astype(jnp.float32)

        @pl.when(z < last)
        def _():
            outbox[box] += line[g, slot_of(1, z)].astype(jnp.float32)

        keep(g).start()
        share(g, mine).start()

    def scatter_tick(t):
        @pl.when((t >= 0) & (t % last == 0) & (t < units * last))
        def _():
            prepare(t // last)

        scatter_step(0, t - LAG * z, z)
        scatter_step(1, t - LAG * (last - z), last - z)
        done = t - last * (LAG + 1)

        @pl.when((done >= 0) & (done % last == 0))
        def _():
            finish(done // last)

    def ticks(gather_from, gather_count, scatter_from, scatter_count):
        def one_gather(i, carry):
            gather_tick(gather_from + i)
            return carry

        def one_scatter(i, carry):
            scatter_tick(scatter_from + i)
            return carry

        lax.fori_loop(0, gather_count, one_gather, 0)
        lax.fori_loop(0, scatter_count, one_scatter, 0)


    def normalize(i, carry):
        part = stage.shape[0]
        rows = pl.ds(pl.multiple_of(i * part, part), part)
        copy = pltpu.make_async_copy(tokens.at[rows], stage, load_sem)
        copy.start()
        copy.wait()

        def few(r, c):
            sub = pl.ds(pl.multiple_of(r * 64, 64), 64)
            there = pl.ds(pl.multiple_of(i * part + r * 64, 64), 64)
            inputs = stage[sub, :].astype(jnp.float32)
            centered = inputs - jnp.mean(inputs, 1, keepdims=True)
            inv_dev = lax.rsqrt(jnp.mean(centered * centered, 1, keepdims=True) + norm_eps)
            normed[there, :] = (centered * inv_dev * gain_ref[0:1, :] + gain_ref[1:2, :]).astype(
                jnp.bfloat16
            )
            return c

        lax.fori_loop(0, part // 64, few, 0)
        return carry

    def save(u):
        return pltpu.make_async_copy(x, saved.at[u], save_sem)

    def wait_saved(u):
        @pl.when(u > 0)
        def _():
            save(u - 1).wait()

    def gradients(u, split):
        @pl.when(u >= 2)
        def _():
            exchange(u - 2).wait_send()

        def one(j, carry):
            for core, place in ((k, None), (1 - k, outgoing)):
                cols = pl.ds(pl.multiple_of(j * size + core * half, half), half)
                into = dot(normed[:, cols], x[:, :split], TN)
                outof = dot(cot[:, cols], x[:, split:], TN)
                if place is None:
                    held[u % 3, j, :, :split] = into
                    held[u % 3, j, :, split:] = outof
                else:
                    place[u % 2, j, :, :split] = into.astype(jnp.bfloat16)
                    place[u % 2, j, :, split:] = outof.astype(jnp.bfloat16)
            return carry

        lax.fori_loop(0, n, one, 0)
        exchange(u).start()

    block = min(512, rows_all)

    def hidden_unit(u, gather_from, gather_count):
        need(u)
        wait_saved(u)

        def one(i, carry):
            rows = pl.ds(pl.multiple_of(i * block, block), block)
            pre = dot(normed[rows, :], wbuf[:, :, :HID].reshape(width, HID)) + bias_ref[u][:, :HID]
            value, slope = gelu_both(pre)
            x[rows, HID:] = value.astype(jnp.bfloat16)
            grad = dot(cot[rows, :], wbuf[:, :, HID:].reshape(width, HID))
            x[rows, :HID] = (grad * slope).astype(jnp.bfloat16)
            return carry

        lax.fori_loop(0, rows_all // block, one, 0)
        save(u).start()
        early = gather_count // 2
        scatter_from = (u - 1) * last
        ticks(gather_from, early, scatter_from, last // 2)
        gradients(u, HID)
        ticks(gather_from + early, gather_count - early, scatter_from + last // 2, last - last // 2)

    qblock = mask.shape[1]
    window = mask.shape[0]
    qblocks = rows_all // qblock

    def rope(v, rows, sign):
        half_rot = ROT // 2
        lane = lax.broadcasted_iota(jnp.int32, v.shape, 1) % HD
        ahead = pltpu.roll(v, LANES - half_rot, 1)
        behind = pltpu.roll(v, half_rot, 1)
        other = jnp.where(lane < half_rot, -ahead, behind)
        return v * cos_ref[rows, :] + other * (sign * sin_ref[rows, :])

    def send_kv(s):
        rows = pl.ds(pl.multiple_of(k * rows_all, rows_all), rows_all)
        return pltpu.make_async_remote_copy(
            src_ref=kv.at[s, :, rows],
            dst_ref=kv.at[s, :, rows],
            send_sem=kvsend_sem.at[s],
            recv_sem=kvrecv_sem.at[s],
            device_id=other_core,
            device_id_type=MESH,
        )

    def recv_kv(s):
        rows = pl.ds(pl.multiple_of((1 - k) * rows_all, rows_all), rows_all)
        return pltpu.make_async_remote_copy(
            src_ref=kv.at[s, :, rows],
            dst_ref=kv.at[s, :, rows],
            send_sem=kvsend_sem.at[s],
            recv_sem=kvrecv_sem.at[s],
            device_id=other_core,
            device_id_type=MESH,
        )

    def send_dkv(s):
        return pltpu.make_async_remote_copy(
            src_ref=dkv.at[:, pl.ds(0, rows_all)],
            dst_ref=dkv_other.at[s],
            send_sem=dsend_sem.at[s],
            recv_sem=drecv_sem.at[s],
            device_id=other_core,
            device_id_type=MESH,
        )

    def attention_unit(u, s, gather_from, gather_count):
        need(u)
        wait_saved(u)

        @pl.when((s > 0) & (k == 1))
        def _():
            send_dkv(s - 1).wait_send()

        def project(i, carry):
            rows = pl.ds(pl.multiple_of(i * block, block), block)
            there = pl.ds(pl.multiple_of(k * rows_all + i * block, block), block)
            pre = dot(normed[rows, :], wbuf[:, :, :ATT].reshape(width, ATT)) + bias_ref[u][:, :ATT]
            grad = dot(cot[rows, :], wbuf[:, :, ATT:].reshape(width, LANES))
            g_s[rows, :] = grad.astype(jnp.bfloat16)
            query = rope(pre[:, :LANES], rows, 1.0).astype(jnp.bfloat16)
            q_s[rows, :] = query * jnp.bfloat16(HD**-0.5)
            kv[s, 0, there, :] = rope(pre[:, LANES : 2 * LANES], rows, 1.0).astype(jnp.bfloat16)
            kv[s, 1, there, :] = pre[:, 2 * LANES :].astype(jnp.bfloat16)
            return carry

        lax.fori_loop(0, rows_all // block, project, 0)
        send_kv(s).start()
        dkv[...] = jnp.zeros_like(dkv)
        scatter_from = (u - 1) * last
        per_block = gather_count // qblocks
        early = gather_count - per_block * qblocks
        ticks(gather_from, early, scatter_from, 0)
        recv_kv(s).wait_recv()

        def queries(b, carry):
            first_query = k * rows_all + b * qblock
            first_key = pl.multiple_of(jnp.maximum(first_query + qblock - window, 0), qblock)
            rows = pl.ds(pl.multiple_of(b * qblock, qblock), qblock)
            keys = pl.ds(first_key, window)
            key_at = first_key + lax.broadcasted_iota(jnp.int32, (window, qblock), 0)
            query_at = first_query + lax.broadcasted_iota(jnp.int32, (window, qblock), 1)
            begin = begin_ref[0:1, rows]
            mask[...] = jnp.where((key_at >= begin) & (key_at <= query_at), 0.0, -1e30)
            lane = lax.broadcasted_iota(jnp.int32, (qblock, LANES), 1)
            att = jnp.zeros((qblock, LANES), jnp.float32)
            dq = jnp.zeros((qblock, LANES), jnp.float32)
            for head in range(2):
                inside = (lane >= head * HD) & (lane < (head + 1) * HD)
                q_own = jnp.where(inside, q_s[rows, :], jnp.zeros((qblock, LANES), jnp.bfloat16))
                g_own = jnp.where(inside, g_s[rows, :], jnp.zeros((qblock, LANES), jnp.bfloat16))
                scores = dot(kv[s, 0, keys, :], q_own, NT) + mask[...]
                weights = jnp.exp(scores - jnp.max(scores, 0, keepdims=True))
                probs = weights * (1.0 / jnp.sum(weights, 0, keepdims=True))
                probs_low = probs.astype(jnp.bfloat16)
                grad_probs = dot(kv[s, 1, keys, :], g_own, NT)
                inner = jnp.sum(probs * grad_probs, 0, keepdims=True)
                grad_scores = (probs * (grad_probs - inner)).astype(jnp.bfloat16)
                att = jnp.where(inside, dot(probs_low, kv[s, 1, keys, :], TN), att)
                dq = jnp.where(inside, dot(grad_scores, kv[s, 0, keys, :], TN), dq)
                dkv[1, keys, :] += dot(probs_low, g_own)
                dkv[0, keys, :] += dot(grad_scores, q_own)
            x[rows, ATT:] = att.astype(jnp.bfloat16)
            x[rows, :LANES] = rope(dq * HD**-0.5, rows, -1.0).astype(jnp.bfloat16)
            low, high = b * last // qblocks, (b + 1) * last // qblocks
            ticks(gather_from + early + b * per_block, per_block, scatter_from + low, high - low)
            return carry

        lax.fori_loop(0, qblocks, queries, 0)

        @pl.when(k == 1)
        def _():
            send_dkv(s).start()

        @pl.when(k == 0)
        def _():
            send_dkv(s).wait_recv()
            copy = pltpu.make_async_copy(dkv_other.at[s], dkv_tmp, load_sem)
            copy.start()
            copy.wait()

        @pl.when(k == 1)
        def _():
            dkv_tmp[...] = jnp.zeros_like(dkv_tmp)

        def turn(i, carry):
            rows = pl.ds(pl.multiple_of(i * qblock, qblock), qblock)
            there = pl.ds(pl.multiple_of(k * rows_all + i * qblock, qblock), qblock)
            x[rows, LANES : 2 * LANES] = rope(
                dkv[0, there, :] + dkv_tmp[0, rows, :], rows, -1.0
            ).astype(jnp.bfloat16)
            x[rows, 2 * LANES : ATT] = (dkv[1, there, :] + dkv_tmp[1, rows, :]).astype(jnp.bfloat16)
            return carry

        lax.fori_loop(0, qblocks, turn, 0)
        save(u).start()
        gradients(u, ATT)


    cot_copy = pltpu.make_async_copy(cot_hbm, cot, save_sem)
    cot_copy.start()
    send_own(0)
    lax.fori_loop(0, rows_all // stage.shape[0], normalize, 0)
    cot_copy.wait()
    per_step = 3 * last
    in_hidden = 2 * per_step // 9
    in_attention = per_step - 2 * in_hidden
    lead = max(last, 2 * last - in_hidden)
    ticks(0, lead, 0, 0)

    def super_step(s, carry):
        base = s * per_step + lead
        hidden_unit(3 * s, base, in_hidden)
        attention_unit(3 * s + 1, s, base + in_hidden, in_attention)
        hidden_unit(3 * s + 2, base + in_hidden + in_attention, in_hidden)
        return carry

    lax.fori_loop(0, steps, super_step, 0)
    ticks(0, 0, (units - 1) * last, last * (LAG + 1) + 1)


    save(units - 1).wait()
    exchange(units - 2).wait_send()
    exchange(units - 1).wait_send()

    @pl.when(k == 1)
    def _():
        send_dkv(steps - 1).wait_send()

    def drain_kv(s, carry):
        send_kv(s).wait_send()
        return carry

    lax.fori_loop(0, steps, drain_kv, 0)

    def drain(m, carry):
        g, s = m // last, m % last + 1

        @pl.when(s == 1)
        def _():
            @pl.when(z < last)
            def _():
                hop(0, g, 0, z).wait_send()

            @pl.when(z > 0)
            def _():
                hop(1, g, 0, z).wait_send()

            @pl.when(g >= units - (LAG + 3))
            def _():
                keep(g).wait()
                share(g, mine).wait_send()

            share(g, theirs).wait_recv()

        @pl.when(z >= s)
        def _():
            @pl.when(z < last)
            def _():
                hop(0, g, s, z - s).wait_send()

            across(0, g, s - 1, z - s, mine).wait_send()

        @pl.when(z + s <= last)
        def _():
            @pl.when(z > 0)
            def _():
                hop(1, g, s, z + s).wait_send()

            across(1, g, s - 1, z + s, mine).wait_send()

        for way in range(2):
            distance = z if way == 0 else last - z

            @pl.when(distance < last - (s - 1))
            def _():
                pass_on(way, g, s - 1).wait_send()

        return carry

    lax.fori_loop(0, units * last, drain, 0)


def run_block(own, tokens, cotangent, bias, gain, cosine, sine, begin):
    n = lax.axis_size("dp")
    units, size = own.shape[0], own.shape[1]
    steps = units // 3
    half = size // 2
    rows, width = tokens.shape
    qblock = min(256, rows)
    span = 2 * rows
    window = min(span, rows + qblock)
    low, full_type = jnp.bfloat16, jnp.float32
    anywhere = pl.BlockSpec(memory_space=pl.ANY)
    vm = pl.BlockSpec(memory_space=pltpu.VMEM)
    dma = pltpu.SemaphoreType.DMA
    return pl.pallas_call(
        functools.partial(block_kernel, n, steps),
        out_shape=(
            jax.ShapeDtypeStruct((units, n, size, WIDE), low),
            jax.ShapeDtypeStruct((units, rows, WIDE), low),
            jax.ShapeDtypeStruct((units, size, WIDE), full_type),
            jax.ShapeDtypeStruct((units, n, half, WIDE), low),
            jax.ShapeDtypeStruct((steps, 2, rows, LANES), full_type),
        ),
        in_specs=[anywhere] * 3 + [vm] * 5,
        out_specs=[anywhere] * 5,
        scratch_shapes=[
            pltpu.VMEM((rows, width), low),
            pltpu.VMEM((rows, width), low),
            pltpu.VMEM((256, width), low),
            pltpu.VMEM((n, size, WIDE), low),
            pltpu.VMEM((rows, WIDE), low),
            pltpu.VMEM((rows, LANES), low),
            pltpu.VMEM((rows, LANES), low),
            pltpu.VMEM((steps, 2, span, LANES), low),
            pltpu.VMEM((2, span, LANES), full_type),
            pltpu.VMEM((2, rows, LANES), full_type),
            pltpu.VMEM((window, qblock), full_type),
            pltpu.VMEM((3, n, half, WIDE), full_type),
            pltpu.VMEM((2, n, half, WIDE), low),
            pltpu.VMEM((n, half, WIDE), low),
            pltpu.VMEM((units, n + 1, half, WIDE), low),
            pltpu.VMEM((LAG + 3, half, WIDE), full_type),
            dma((units,)),
            dma((2, units, n)),
            dma((2, units, n)),
            dma((2, units, n)),
            dma((2, units, n)),
            dma((units,)),
            dma((units,)),
            dma((2, units, n - 1)),
            dma((2, units, n - 1)),
            dma((units,)),
            dma((units,)),
            dma((units,)),
            dma((steps,)),
            dma((steps,)),
            dma((steps,)),
            dma((steps,)),
            dma,
            dma,
        ],
        compiler_params=pltpu.CompilerParams(
            collective_id=1, has_side_effects=True, vmem_limit_bytes=VMEM_LIMIT
        ),
        name="parallel_block",
    )(own, tokens, cotangent, bias, gain, cosine, sine, begin)


def pack_weights(in_weight, out_weight):
    size, _, cols = in_weight.shape
    steps = cols // LANES
    into = jnp.transpose(in_weight, (1, 0, 2)).astype(jnp.bfloat16)
    outof = jnp.transpose(out_weight.astype(jnp.bfloat16), (0, 2, 1))
    per = cols // HID
    hid_in = into[3:].reshape(4, size, per, HID).transpose(0, 2, 1, 3).reshape(steps, 2, size, HID)
    hid_out = outof[1:].reshape(4, size, per, HID).transpose(0, 2, 1, 3).reshape(steps, 2, size, HID)
    hid = jnp.concatenate([hid_in, hid_out], 3)
    att_in = into[:3].reshape(3, size, steps, LANES).transpose(2, 1, 0, 3).reshape(steps, size, ATT)
    att_out = outof[0].reshape(size, steps, LANES).transpose(1, 0, 2)
    att = jnp.concatenate([att_in, att_out], 2)
    return jnp.stack([hid[:, 0], att, hid[:, 1]], 1).reshape(3 * steps, size, WIDE)


def unpack_columns(packed, lead):
    steps = packed.shape[0] // 3
    per = steps * LANES // HID
    by_step = packed.reshape((steps, 3) + lead + (WIDE,))
    hid = jnp.stack([by_step[:, 0], by_step[:, 2]], 1).reshape((4, per) + lead + (WIDE,))
    att = by_step[:, 1]
    axes = len(lead)

    def widen(v):
        order = (0,) + tuple(range(2, 2 + axes)) + (1, 2 + axes)
        return v.transpose(order).reshape((v.shape[0],) + lead + (v.shape[1] * v.shape[-1],))

    att_parts = jnp.stack([att[..., i * LANES : (i + 1) * LANES] for i in range(4)], 0)
    att_wide = widen(att_parts)
    into = jnp.concatenate([att_wide[:3], widen(hid[..., :HID])], 0)
    outof = jnp.concatenate([att_wide[3:], widen(hid[..., HID:])], 0)
    return into, outof


def layout(lengths_row, row_span):
    seg_ends = jnp.cumsum(lengths_row)
    seg_starts = seg_ends - lengths_row
    places = jnp.arange(row_span, dtype=jnp.int32)
    segment = jnp.sum((places[:, None] >= seg_ends[None, :]).astype(jnp.int32), 1)
    numbers = jnp.arange(lengths_row.shape[0], dtype=jnp.int32)
    return jnp.sum(jnp.where(segment[:, None] == numbers[None, :], seg_starts[None, :], 0), 1)


def rope_tables(places):
    half_rot = ROT // 2
    lane = jnp.arange(2 * HD, dtype=jnp.int32) % HD
    exponent = (lane % half_rot).astype(jnp.float32)
    frequency = 10000.0 ** (-2.0 * exponent / ROT)
    angles = places.astype(jnp.float32)[:, None] * frequency[None, :]
    turned = (lane < ROT)[None, :]
    cosine = jnp.where(turned, jnp.cos(angles), 1.0)
    sine = jnp.where(turned, jnp.sin(angles), 0.0)
    return cosine, sine


def body(
    tokens,
    cotangent,
    lengths,
    in_weight,
    out_weight,
    vectors,
    in_first,
    in_second,
    out_first,
    out_second,
    vec_first,
    vec_second,
):
    local_rows, model_width = tokens.shape
    slice_width = in_weight.shape[2]
    context_count = lax.axis_size("context")
    context_index = lax.axis_index("context")
    tensor_count = lax.axis_size("tensor")
    tensor_index = lax.axis_index("tensor")
    row_span = local_rows * context_count
    first_row = context_index * local_rows
    begin_all = layout(lengths[0], row_span)
    begin = lax.dynamic_slice_in_dim(begin_all, first_row, local_rows, 0)
    places = first_row + jnp.arange(local_rows, dtype=jnp.int32) - begin
    tables = rope_tables(places)

    inputs = tokens.astype(jnp.float32)
    centered = inputs - jnp.mean(inputs, 1, keepdims=True)
    inv_dev = lax.rsqrt(jnp.mean(centered * centered, 1, keepdims=True) + norm_eps)
    unit_rows = centered * inv_dev
    norm_gain = vectors[NIN + 1]
    column = tensor_index * slice_width
    in_bias = lax.dynamic_slice_in_dim(vectors[:NIN], column, slice_width, 1)
    steps = slice_width // LANES
    hid_bias = in_bias[3:].reshape(steps, 2, HID)
    att_bias = in_bias[:3].reshape(3, steps, LANES).transpose(1, 0, 2).reshape(steps, ATT)
    bias = jnp.stack(
        [
            jnp.pad(hid_bias[:, 0], ((0, 0), (0, WIDE - HID))),
            jnp.pad(att_bias, ((0, 0), (0, WIDE - ATT))),
            jnp.pad(hid_bias[:, 1], ((0, 0), (0, WIDE - HID))),
        ],
        1,
    ).reshape(3 * steps, 1, WIDE)
    own = pack_weights(in_weight, out_weight)
    full, saved, total_packed, _, _ = run_block(
        own, tokens, cotangent, bias, vectors[NIN + 1 : NIN + 3], tables[0], tables[1], begin[None]
    )
    total_in, total_out = unpack_columns(total_packed, (own.shape[1],))
    grad_projected, mixed = unpack_columns(saved, (local_rows,))

    units = full.shape[0]
    splits = [ATT if u % 3 == 1 else HID for u in range(units)]
    partial_out = sum(
        lax.dot_general(
            saved[u][:, splits[u] :], full[u].reshape(model_width, WIDE)[:, splits[u] :], NT,
            preferred_element_type=jnp.float32,
        )
        for u in range(units)
    )
    norm_partial = sum(
        lax.dot_general(
            saved[u][:, : splits[u]], full[u].reshape(model_width, WIDE)[:, : splits[u]], NT,
            preferred_element_type=jnp.float32,
        )
        for u in range(units)
    )
    branch = lax.psum_scatter(
        partial_out.astype(jnp.bfloat16), "tensor", scatter_dimension=1, tiled=True
    ).astype(jnp.float32)
    out_width = branch.shape[1]
    out_column = tensor_index * out_width
    residual = lax.dynamic_slice_in_dim(inputs, out_column, out_width, 1)
    out_bias = lax.dynamic_slice_in_dim(vectors[NIN], out_column, out_width, 0)
    result = (residual + (branch + out_bias[None])).astype(jnp.bfloat16)

    unit_partial = norm_partial * norm_gain
    row_sums = lax.psum(
        jnp.stack([jnp.sum(unit_partial, 1), jnp.sum(unit_partial * unit_rows, 1)], 0), "tensor"
    ) / model_width
    grad_normed = lax.psum_scatter(
        norm_partial.astype(jnp.bfloat16), "tensor", scatter_dimension=1, tiled=True
    ).astype(jnp.float32)
    unit_slice = lax.dynamic_slice_in_dim(unit_rows, out_column, out_width, 1)
    gain_slice = lax.dynamic_slice_in_dim(norm_gain, out_column, out_width, 0)
    cot_slice = lax.dynamic_slice_in_dim(cotangent, out_column, out_width, 1).astype(jnp.float32)
    token_grad = (
        inv_dev * (grad_normed * gain_slice - row_sums[0][:, None] - unit_slice * row_sums[1][:, None])
        + cot_slice
    )

    vector_slice = jnp.stack(
        [jnp.sum(grad_projected[g].astype(jnp.float32), 0) for g in range(NIN)]
        + [
            jnp.sum(cot_slice, 0),
            jnp.sum(grad_normed * unit_slice, 0),
            jnp.sum(grad_normed, 0),
        ],
        0,
    )
    vector_rows = lax.dynamic_update_slice_in_dim(
        jnp.zeros((NIN + 3, model_width), jnp.float32), vector_slice, column, 1
    )
    vector_grad = lax.psum(vector_rows, ("dp", "context", "tensor"))
    new_vectors, new_vec_first, new_vec_second = adamw(
        vectors, vector_grad, vec_first, vec_second, rate_vector, 0.0
    )
    new_in, new_in_first, new_in_second = adamw(
        in_weight, jnp.transpose(total_in, (1, 0, 2)), in_first, in_second, rate_matrix, weight_decay
    )
    new_out, new_out_first, new_out_second = adamw(
        out_weight, jnp.transpose(total_out, (0, 2, 1)), out_first, out_second, rate_matrix, weight_decay
    )
    return (
        result,
        token_grad,
        new_in,
        new_in_first,
        new_in_second,
        new_out,
        new_out_first,
        new_out_second,
        new_vectors,
        new_vec_first,
        new_vec_second,
    )


def solution(mesh):
    return jax.shard_map(
        body,
        mesh=mesh,
        in_specs=(
            P(("dp", "context"), None),
            P(("dp", "context"), None),
            P("dp", None),
            P("dp", None, "tensor"),
            P(None, "tensor", "dp"),
            P(),
            P("dp", None, "tensor"),
            P("dp", None, "tensor"),
            P(None, "tensor", "dp"),
            P(None, "tensor", "dp"),
            P(),
            P(),
        ),
        out_specs=(
            P(("dp", "context"), "tensor"),
            P(("dp", "context"), "tensor"),
            P("dp", None, "tensor"),
            P("dp", None, "tensor"),
            P("dp", None, "tensor"),
            P(None, "tensor", "dp"),
            P(None, "tensor", "dp"),
            P(None, "tensor", "dp"),
            P(),
            P(),
            P(),
        ),
        check_vma=False,
    )
```

time: 2230 us -> 866 us (0.39)
  waiting for transfers between devices: 1570 us -> 116 us
  Pallas kernels: 0 us -> 381 us
  matrix products: 338 us -> 177 us
  other arithmetic: 186 us -> 68.2 us
    reduce_scatter x5 -> x2, waiting for transfers between devices: 903 us -> 0.02 us  [the longest x1 0.02 us: body(): lax.psum_scatter(partial_out.astype(jnp.bfloat16), 'tensor', scatter_dime...]
    all_gather x4 -> x0, waiting for transfers between devices: 397 us -> none  [the longest x1 242 us: body(): lax.all_gather(in_weight.astype(jnp.bfloat16), 'dp', axis=0, tiled=True)]
    pallas_call x0 -> x1, Pallas kernels: none -> 381 us  [run_block(): pl.pallas_call(functools.partial(block_kernel, n, steps), out_shape=(jax....]
    dot_general x20 -> x24, matrix products: 338 us -> 177 us  [the longest x12 90.5 us: body(): lax.dot_general(saved[u][:, :splits[u]], full[u].reshape(model_width, WID...]
    psum x3 -> x1, waiting for transfers between devices: 271 us -> 116 us  [body(): vector_grad = lax.psum(vector_rows, ('dp', 'context', 'tensor'))]
    convert_element_type x4 -> x1, other arithmetic: 60.2 us -> 0.6 us  [rope_tables(): angles = places.astype(jnp.float32)[:, None] * frequency[None, :]]
    reduce_sum x5 -> x3, other arithmetic: 47.9 us -> 4.8 us  [the longest x1 3.81 us: body(): jnp.sum(grad_normed, 0)]
    dynamic_update_slice x5 -> x1, local copies, waits for them, and re-layouts: 41.4 us -> 0.01 us  [body(): lax.dynamic_update_slice_in_dim(jnp.zeros((NIN + 3, model_width), jnp.flo...]
  transfers between devices with their start and end apart: 12 -> 3, of which waited for: 8 -> 1; matrix products, arithmetic and copies ran while one was open for 9% -> 19% of each run, Pallas kernels for 0% -> 0%
where the time goes in v1:
time: 866 us; the launch traced here: 859 us
  Pallas kernels  381 us (44%)
  matrix products  177 us (20%)
  waiting for transfers between devices  116 us (13%)
  local copies, waits for them, and re-layouts  90.9 us (10%)
  other arithmetic  68.2 us (8%)
  between operations  14.7 us (2%)
  blocking collectives  11.5 us (1%)
    pallas_call x1, Pallas kernels, run_block(): pl.pallas_call(functools.partial(block_kernel, n, steps), out_shape=(jax....  381 us
    psum x1, waiting for transfers between devices, body(): vector_grad = lax.psum(vector_rows, ('dp', 'context', 'tensor'))  116 us
    dot_general x12, matrix products, body(): lax.dot_general(saved[u][:, :splits[u]], full[u].reshape(model_width, WID...  90.5 us
    dot_general x12, matrix products, body(): lax.dot_general(saved[u][:, splits[u]:], full[u].reshape(model_width, WID...  86.1 us
    sub x3, other arithmetic, adamw(): master - step_rate * (first_hat / (jnp.sqrt(second_hat) + adam_eps) + dec...  27.2 us
  transfers between devices with their start and end apart: 3, of which 1 were waited for; matrix products, arithmetic and copies ran while one was open for 19% of the time, Pallas kernels for 0%

profile of v1, /device:TPU:0, one launch (start us, length us, event | category | flops | bytes accessed | tf_op | source)
XLA Modules:
  0.0 859.2 jit_solution(9304517837320201784)
XLA Ops:
  7.3 6.9 copy.51
  27.4 6.6 fusion.4
  34.0 8.6 %copy.53 = bf16[4,3,512,512]{3,2,1,0:T(8,128)(2,1)} copy(bf16[4,3,512,512]{2,3,1,0:T(8,128)(2,1)} %fusion.4) | data formatting | bytes 12582912 | tf_op jit(solution)/shard_map/stack | solution.py:680
  49.1 381.4 %parallel_block.1 = (bf16[12,4,512,512]{3,2,1,0:T(8,128)(2,1)}, bf16[12,1024,512]{2,1,0:T(8,128)(2,1)}, f32[12,512,512]{2,1,0:T(8,128)}, bf16[12,4,256,512]{3,2,1,0:T(8,128)(2,1)}, f32[4,2,1024,128]{3,2,1,0:T(8,128)}) custom-call(bf16[12,512,512]{2,1,0:T(8,128)(2,1)} %bitcast.158, bf16[1024,2048]{1,0:T(8,128)(2,1)} %tokens.1, bf16[1024,2048]{1,0:T(8,128)(2,1)} %cot_hbm.1, ...), custom_call_target="tpu_custom_call" | custom-call | tf_op jit(solution)/shard_map/parallel_block/pallas_call | solution.py:614
  430.5 9.2 %slice_bitcast_fusion.11 = (bf16[1024,512]{1,0:T(8,128)(2,1)}, bf16[1024,512]{1,0:T(8,128)(2,1)S(1)}, bf16[1024,512]{1,0:T(8,128)(2,1)}, bf16[1024,512]{1,0:T(8,...) fusion(bf16[12,1024,512]{2,1,0:T(8,128)(2,1)} %get-tuple-element.14), kind=kLoop, calls=%fused_computation.105 | loop fusion | bytes 25165824 | tf_op jit(solution)/shard_map/squeeze | solution.py:779
  439.7 16.5 %fusion.96 = (bf16[1,4,512,512]{3,2,1,0:T(8,128)(2,1)S(1)}, bf16[1,4,512,512]{3,2,1,0:T(8,128)(2,1)}, bf16[1,4,512,512]{3,2,1,0:T(8,128)(2,1)}, bf16[1,4,512,512...) fusion(bf16[12,4,512,512]{3,2,1,0:T(8,128)(2,1)} %get-tuple-ele, ...), kind=kLoop, calls=%fused_computation.184 | loop fusion | bytes 50331648 | tf_op jit(solution)/shard_map/slice | solution.py:779
  459.9 5.7 fusion.15
  465.6 5.6 fusion.17
  471.2 5.6 fusion.19
  476.8 5.7 fusion.21
  514.6 35.9 %multiply_reduce_fusion.2 = (f32[1024]{0:T(1024)S(1)}, f32[1024]{0:T(1024)S(1)}, bf16[1024,2048]{1,0:T(8,128)(2,1)}, f32[1024,2048]{1,0:T(8,128)}) fusion(f32[2048]{0:T(1024)S(1)} %bitcast.198, f32[1024]{0:T(1024)S(1)} %add_rsqrt_fusion, f32[1024]{0:T(1024)S(1)} %broadcast_multiply_fusion.1, bf16[1024,2048]{1,0:T(8,128)(2,1)} %tokens.1, ...), kind=kOutput, calls=%fused_computation.10 | convolution fusion | flops 1113585664 | bytes 110649344 | tf_op jit(solution)/shard_map/dot_general | solution.py:785
  550.6 5.9 fusion.80
  556.4 5.6 fusion.76
  562.0 5.7 fusion.72
  567.7 5.7 fusion.68
  605.6 31.2 %add_convert_fusion = bf16[1024,2048]{1,0:T(8,128)(2,1)} fusion(f32[1024,2048]{1,0:T(8,128)} %fusion.68, f32[1024,2048]{1,0:T(8,128)} %fusion.39, f32[1024,2048]{1,0:T(8,128)} %fusion.41, f32[1024,2048]{1,0:T(8,128)} %fusion.72, f32[1024,2048]{1,0:T(8,128)} %fusion.43, f32[1024,2048]{1,0:T(8,128)} %fusion.45, f32[1024,2048]{1,0:T(8,128)} %fusion.76, ...), kind=kOutput, calls=%fused_computation.9 | convolution fusion | flops 1098907648 | bytes 98041856 | tf_op jit(solution)/shard_map/dot_general | solution.py:778
  636.9 6.7 convert_element_type.76
  643.6 6.8 fusion.97
  651.3 9.9 %slice_bitcast_fusion.1 = (f32[4,512,512]{2,1,0:T(8,128)S(1)}, f32[4,1,512,512]{3,2,1,0:T(8,128)}, f32[4,1,512,512]{3,2,1,0:T(8,128)}) fusion(f32[4,3,512,512]{3,2,1,0:T(8,128)} %bitcast.169), kind=kLoop, calls=%fused_computation.31 | loop fusion | bytes 25165824 | tf_op jit(solution)/shard_map/squeeze | solution.py:688
  665.4 5.9 fusion.9
  681.4 11.5 %psum.14 = f32[2,1024]{1,0:T(2,128)S(1)} all-reduce(f32[2,1024]{1,0:T(2,128)S(1)} %pad_maximum_fusion.3), channel_id=1, replica_groups=mesh['dp'=4,'context'=2,'tensor'=4] {'tensor'}, use_global_device_ids=true, to_apply=%region_9.10 | all-reduce | flops 2048 | bytes 16384 | tf_op jit(solution)/shard_map/psum | solution.py:801
  701.5 10.1 %multiply_subtract_fusion.1 = (f32[5,512,512]{2,1,0:T(8,128)}, f32[5,512,512]{2,1,0:T(8,128)}, f32[5,512,512]{2,1,0:T(8,128)}) fusion(f32[5,512,512]{2,1,0:T(8,128)S(1)} %bitcast.160, f32[4,512,512]{1,2,0:T(8,128)S(1)} %bitcast.166, f32[1,512,512]{1,2,0:T(8,128)S(1)} %bitcast.197, f32[5,512,512]{2,1,0:T(8,128)} %param.20, f32[5,512,512]{2,1,0:T(8,128)} %param.21), kind=kLoop, calls=%fused_computation.22 | loop fusion | flops 20971520 | bytes 36700160 | tf_op jit(solution)/shard_map/sub | solution.py:31
  711.6 15.4 %multiply_subtract_fusion = (f32[512,7,512]{2,0,1:T(8,128)}, f32[512,7,512]{2,0,1:T(8,128)}, f32[512,7,512]{2,0,1:T(8,128)}) fusion(f32[512,7,512]{2,0,1:T(8,128)} %param.15, f32[4,512,512]{2,1,0:T(8,128)} %bitcast.165, f32[3,512,512]{2,1,0:T(8,128)S(1)} %copy_bitcast_fusion, f32[512,7,512]{2,0,1:T(8,128)} %param.18, f32[512,7,512]{2,0,1:T(8,128)} %param.19), kind=kLoop, calls=%fused_computation.15 | loop fusion | flops 29360128 | bytes 51380224 | tf_op jit(solution)/shard_map/sub | solution.py:31
  734.8 115.7 %all-reduce.5.cloned.1.call-done = f32[10,2048]{1,0:T(8,128)} async-done(((f32[10,2048]{1,0:T(8,128)}), f32[10,2048]{1,0:T(8,128)}) %all-reduce.5.cloned.1.call-update) | async-done | bytes 81936 | tf_op jit(solution)/shard_map/psum | solution.py:827
  (188 shorter events, 120.8 us)
Async XLA Ops:
  7.2 719.8 %reduce-scatter.5.cloned.1.call-start = ((), (), s32[]{:S(2)}) async-start(), calls=%async_computation.3 | async-start | bytes 5242880 | tf_op jit(solution)/shard_map/reduce_scatter | solution.py:804
  14.2 4.8 copy-start
  21.6 5.4 slice-start.2
  459.8 5.7 copy-start.21
  459.9 5.7 copy-start.24
  465.6 5.6 copy-start.22
  465.6 5.6 copy-start.25
  471.2 5.6 copy-start.23
  471.2 5.6 copy-start.26
  476.8 5.7 copy-start.6
  476.8 5.7 copy-start.27
  496.2 4.7 copy-start.14
  496.2 4.7 copy-start.35
  550.5 181.1 %reduce-scatter.3.cloned.1.call-start = ((), (), s32[]{:S(2)}) async-start(), calls=%async_computation.2 | async-start | bytes 5242880 | tf_op jit(solution)/shard_map/reduce_scatter | solution.py:791
  567.7 5.7 copy-start.19
  567.7 5.7 copy-start.40
  582.4 4.7 copy-start.34
  596.3 4.9 copy-start.7
  596.3 4.9 copy-start.28
  636.8 213.7 %all-reduce.5.cloned.1.call-start = ((), (), s32[]{:S(2)}) async-start(), calls=%async_computation.4 | async-start | bytes 262144 | tf_op jit(solution)/shard_map/psum | solution.py:827
  696.8 4.7 copy-start.42
  726.9 123.6 %copy-start.45 = (f32[10,2048]{1,0:T(8,128)S(1)}, f32[10,2048]{1,0:T(8,128)}, u32[]{:S(2)}) copy-start(f32[10,2048]{1,0:T(8,128)} %param.17) | copy-start | bytes 245764
  727.0 123.6 %copy-start.46 = (f32[10,2048]{1,0:T(8,128)S(1)}, f32[10,2048]{1,0:T(8,128)}, u32[]{:S(2)}) copy-start(f32[10,2048]{1,0:T(8,128)} %param.22) | copy-start | bytes 245764
  727.0 123.5 %copy-start.47 = (f32[10,2048]{1,0:T(8,128)S(1)}, f32[10,2048]{1,0:T(8,128)}, u32[]{:S(2)}) copy-start(f32[10,2048]{1,0:T(8,128)} %param.23) | copy-start | bytes 245764
  (31 other events, 121.9 us)
Sparse Core Ops, SparseCore 0:
  550.6 51.0 reduce-scatter.4
  636.9 51.0 reduce-scatter.2
  731.7 118.7 all-reduce.4

commit v2 on v1

v2 whole, which is shorter than its diff:
```python
import functools

import jax
import jax.numpy as jnp
from jax import lax
from jax.experimental import pallas as pl
from jax.experimental.pallas import tpu as pltpu
from jax.sharding import PartitionSpec as P

HD = 64
ROT = 32
STEP = 10
NIN = 7
MESH = pl.DeviceIdType.MESH
VMEM_LIMIT = 60 * 2**20

norm_eps = 1e-05
beta_one = 0.9
beta_two = 0.95
adam_eps = 1e-08
weight_decay = 0.1
rate_matrix = 0.02
rate_vector = 0.4


def adamw(master, gradient, moment_one, moment_two, step_rate, decay_rate):
    first_new = beta_one * moment_one + (1.0 - beta_one) * gradient
    second_new = beta_two * moment_two + (1.0 - beta_two) * gradient * gradient
    first_hat = first_new / (1.0 - beta_one**STEP)
    second_hat = second_new / (1.0 - beta_two**STEP)
    updated = master - step_rate * (
        first_hat / (jnp.sqrt(second_hat) + adam_eps) + decay_rate * master
    )
    return (updated, first_new, second_new)


LANES = 2 * HD
WIDE = 4 * LANES
HID = WIDE // 2
ATT = 3 * LANES
LAG = 2

NT = (((1,), (1,)), ((), ()))
NN = (((1,), (0,)), ((), ()))
TN = (((0,), (0,)), ((), ()))


def dot(x, y, dims=NN):
    return lax.dot_general(x, y, dims, preferred_element_type=jnp.float32)


def greet(n, peers):
    z = lax.axis_index("dp")
    k = lax.axis_index("context")
    t = lax.axis_index("tensor")
    barrier = pltpu.get_barrier_semaphore()
    pl.semaphore_signal(barrier, inc=1, device_id={"context": 1 - k}, device_id_type=MESH)
    for i in range(1, n):
        pl.semaphore_signal(barrier, inc=1, device_id={"dp": lax.rem(z + i, n)}, device_id_type=MESH)
    for i in range(1, peers):
        pl.semaphore_signal(
            barrier, inc=1, device_id={"tensor": lax.rem(t + i, peers)}, device_id_type=MESH
        )
    pl.semaphore_wait(barrier, n + peers - 1)


def gelu_both(v):
    rate = 0.7978845608028654
    t = jnp.tanh(rate * (v + 0.044715 * (v * v * v)))
    value = 0.5 * v * (1.0 + t)
    slope = 0.5 * (1.0 + t) + 0.5 * v * (1.0 - t * t) * (rate * (1.0 + 3.0 * 0.044715 * (v * v)))
    return value, slope


def block_kernel(
    n, steps, peers,
    in_w, out_w, tokens, cot_hbm, bias_ref, vec_ref, cos_ref, sin_ref, begin_ref,
    full, saved, total, swap, dkv_other, arrived, result, token_grad, vec_grad,
    kv, held, line, outbox, stats, vec, vec_core, vec_line, vec_all, sums, sums_in,
    send_sem, recv_sem, psend_sem, precv_sem,
    xsend_sem, xrecv_sem, lsend_sem, lrecv_sem, keep_sem, fsend_sem, frecv_sem,
    kvsend_sem, kvrecv_sem, dsend_sem, drecv_sem, load_sem, save_sem, weight_sem, pack_sem,
    tsend_sem, trecv_sem, ssend_sem, srecv_sem, vsend_sem, vrecv_sem, tile_sem, out_sem,
):
    units = 3 * steps
    size, cols_all = in_w.shape[1], in_w.shape[2]
    half = size // 2
    rows_all, width = tokens.shape
    tensor = lax.axis_index("tensor")
    columns = pl.ds(pl.multiple_of(tensor * size, size), size)
    last = n - 1
    z = lax.axis_index("dp")
    k = lax.axis_index("context")
    mine = pl.ds(pl.multiple_of(k * half, half), half)
    theirs = pl.ds(pl.multiple_of((1 - k) * half, half), half)
    other_core = {"context": 1 - k}
    greet(n, peers)


    def hop(way, g, h, shard):
        return pltpu.make_async_remote_copy(
            src_ref=full.at[g, shard, mine],
            dst_ref=full.at[g, shard, mine],
            send_sem=send_sem.at[way, g, h],
            recv_sem=recv_sem.at[way, g, h],
            device_id={"dp": z + 1 - 2 * way},
            device_id_type=MESH,
        )

    def across(way, g, h, shard, rows):
        return pltpu.make_async_remote_copy(
            src_ref=full.at[g, shard, rows],
            dst_ref=full.at[g, shard, rows],
            send_sem=psend_sem.at[way, g, h],
            recv_sem=precv_sem.at[way, g, h],
            device_id=other_core,
            device_id_type=MESH,
        )

    def send_own(g):
        @pl.when(z < last)
        def _():
            hop(0, g, 0, z).start()

        @pl.when(z > 0)
        def _():
            hop(1, g, 0, z).start()

    def gather_tick(m):
        @pl.when(m < units * last)
        def _():
            g, s = m // last, m % last + 1

            @pl.when((s == 1) & (g < units - 1))
            def _():
                send_own(g + 1)

            @pl.when(z >= s)
            def _():
                hop(0, g, s - 1, z - s).wait_recv()

                @pl.when(z < last)
                def _():
                    hop(0, g, s, z - s).start()

                across(0, g, s - 1, z - s, mine).start()

            @pl.when(z + s <= last)
            def _():
                hop(1, g, s - 1, z + s).wait_recv()

                @pl.when(z > 0)
                def _():
                    hop(1, g, s, z + s).start()

                across(1, g, s - 1, z + s, mine).start()

    def need(u):
        def one(i, carry):
            s = i + 1

            @pl.when(z >= s)
            def _():
                across(0, u, s - 1, z - s, theirs).wait_recv()

            @pl.when(z + s <= last)
            def _():
                across(1, u, s - 1, z + s, theirs).wait_recv()

            return carry

        lax.fori_loop(0, last, one, 0)

    def send_kv(s):
        rows = pl.ds(pl.multiple_of(k * rows_all, rows_all), rows_all)
        return pltpu.make_async_remote_copy(
            src_ref=kv.at[s, :, rows],
            dst_ref=kv.at[s, :, rows],
            send_sem=kvsend_sem.at[s],
            recv_sem=kvrecv_sem.at[s],
            device_id=other_core,
            device_id_type=MESH,
        )


    def exchange_from(outgoing, g):
        return pltpu.make_async_remote_copy(
            src_ref=outgoing,
            dst_ref=swap.at[g],
            send_sem=xsend_sem.at[g],
            recv_sem=xrecv_sem.at[g],
            device_id=other_core,
            device_id_type=MESH,
        )

    def slot_of(way, i):
        return i if way == 0 else n - i

    def pass_on(way, g, i):
        slot = slot_of(way, i)
        return pltpu.make_async_remote_copy(
            src_ref=line.at[g, slot],
            dst_ref=line.at[g, slot],
            send_sem=lsend_sem.at[way, g, i],
            recv_sem=lrecv_sem.at[way, g, i],
            device_id={"dp": z + 1 - 2 * way},
            device_id_type=MESH,
        )

    def keep(g):
        return pltpu.make_async_copy(outbox.at[g % (LAG + 3)], total.at[g, mine], keep_sem.at[g])

    def share(g, rows):
        return pltpu.make_async_remote_copy(
            src_ref=outbox.at[g % (LAG + 3)],
            dst_ref=total.at[g, rows],
            send_sem=fsend_sem.at[g],
            recv_sem=frecv_sem.at[g],
            device_id=other_core,
            device_id_type=MESH,
        )

    def prepare(g, swap_in):
        exchange_from(swap_in, g).wait_recv()
        pltpu.make_async_copy(swap.at[g], swap_in, load_sem).start()
        pltpu.make_async_copy(swap.at[g], swap_in, load_sem).wait()
        box = g % (LAG + 3)

        @pl.when(g >= LAG + 3)
        def _():
            keep(g - (LAG + 3)).wait()
            share(g - (LAG + 3), mine).wait_send()

        def one(j, carry):
            held[g % 3, j] += swap_in[j].astype(jnp.float32)
            return carry

        lax.fori_loop(0, n, one, 0)
        outbox[box] = held[g % 3, z]

    def scatter_step(way, m, distance):
        @pl.when((m >= 0) & (m < units * last))
        def _():
            g, i = m // last, m % last
            shard = n - 1 - i if way == 0 else i
            slot = slot_of(way, i)

            @pl.when(distance == 0)
            def _():
                line[g, slot] = held[g % 3, shard].astype(jnp.bfloat16)
                pass_on(way, g, i).start()

            @pl.when((distance > 0) & (distance <= last - i))
            def _():
                pass_on(way, g, i).wait_recv()

                @pl.when(distance < last - i)
                def _():
                    line[g, slot] = (line[g, slot].astype(jnp.float32) + held[g % 3, shard]).astype(
                        jnp.bfloat16
                    )
                    pass_on(way, g, i).start()

    def finish(g):
        box = g % (LAG + 3)

        @pl.when(z > 0)
        def _():
            outbox[box] += line[g, slot_of(0, n - 1 - z)].astype(jnp.float32)

        @pl.when(z < last)
        def _():
            outbox[box] += line[g, slot_of(1, z)].astype(jnp.float32)

        keep(g).start()
        share(g, mine).start()

    def scatter_tick(t, swap_in):
        @pl.when((t >= 0) & (t % last == 0) & (t < units * last))
        def _():
            prepare(t // last, swap_in)

        scatter_step(0, t - LAG * z, z)
        scatter_step(1, t - LAG * (last - z), last - z)
        done = t - last * (LAG + 1)

        @pl.when((done >= 0) & (done % last == 0))
        def _():
            finish(done // last)

    def run_ticks(swap_in, gather_from, gather_count, scatter_from, scatter_count):
        def one_gather(i, carry):
            gather_tick(gather_from + i)
            return carry

        def one_scatter(i, carry):
            scatter_tick(scatter_from + i, swap_in)
            return carry

        lax.fori_loop(0, gather_count, one_gather, 0)
        lax.fori_loop(0, scatter_count, one_scatter, 0)

    def forward_backward(
        normed, cot, stage, raw_in, raw_out, packed, wbuf, x, q_s, g_s, dkv, dkv_tmp, mask, outgoing, swap_in
    ):

        def exchange(g):
            return exchange_from(outgoing.at[g % 2], g)

        def ticks(gather_from, gather_count, scatter_from, scatter_count):
            run_ticks(swap_in, gather_from, gather_count, scatter_from, scatter_count)

        def normalize(i):
            part = stage.shape[0]
            rows = pl.ds(pl.multiple_of(i * part, part), part)
            copy = pltpu.make_async_copy(tokens.at[rows], stage, load_sem)
            copy.start()
            copy.wait()

            def few(r, c):
                sub = pl.ds(pl.multiple_of(r * 64, 64), 64)
                there = pl.ds(pl.multiple_of(i * part + r * 64, 64), 64)
                inputs = stage[sub, :].astype(jnp.float32)
                centered = inputs - jnp.mean(inputs, 1, keepdims=True)
                inv_dev = lax.rsqrt(jnp.mean(centered * centered, 1, keepdims=True) + norm_eps)
                normed[there, :] = (
                    centered * inv_dev * vec_ref[NIN + 1 : NIN + 2, :] + vec_ref[NIN + 2 : NIN + 3, :]
                ).astype(jnp.bfloat16)
                lane = lax.broadcasted_iota(jnp.int32, (64, LANES), 1)
                stats[there, :] = jnp.where(lane == 0, jnp.mean(inputs, 1, keepdims=True), inv_dev)
                return c

            lax.fori_loop(0, part // 64, few, 0)

        def hidden_place(i):
            return i * HID // cols_all, pl.multiple_of(i * HID % cols_all, HID)

        def pack(u):
            s = u // 3

            def fetch(copies):
                for copy in copies:
                    copy.start()
                for copy in copies:
                    copy.wait()

            @pl.when(u % 3 == 1)
            def _():
                cols = pl.ds(pl.multiple_of(s * LANES, LANES), LANES)
                fetch(
                    [
                        pltpu.make_async_copy(
                            in_w.at[g, :, cols], raw_in.at[:, pl.ds(g * LANES, LANES)], pack_sem.at[g]
                        )
                        for g in range(3)
                    ]
                    + [pltpu.make_async_copy(out_w.at[0, cols], raw_out.at[pl.ds(0, LANES)], pack_sem.at[3])]
                )
                packed[:, :ATT] = raw_in[...].astype(jnp.bfloat16)
                packed[:, ATT:] = raw_out[:LANES, :].astype(jnp.bfloat16).T

            @pl.when(u % 3 != 1)
            def _():
                group, first = hidden_place(2 * s + (u % 3) // 2)
                cols = pl.ds(first, HID)
                fetch(
                    [
                        pltpu.make_async_copy(
                            in_w.at[3 + group, :, cols], raw_in.at[:, pl.ds(0, HID)], pack_sem.at[0]
                        ),
                        pltpu.make_async_copy(out_w.at[1 + group, cols], raw_out, pack_sem.at[1]),
                    ]
                )
                packed[:, :HID] = raw_in[:, :HID].astype(jnp.bfloat16)
                packed[:, HID:] = raw_out[...].astype(jnp.bfloat16).T

            copy = pltpu.make_async_copy(packed, full.at[u, z], load_sem)
            copy.start()
            copy.wait()

        def fetch_weights(u):
            return pltpu.make_async_copy(full.at[u], wbuf, weight_sem)

        def next_weights(u):
            @pl.when(u < units)
            def _():
                need(u)
                fetch_weights(u).start()

        def column_sums(split):
            ones = jnp.ones((8, rows_all), jnp.bfloat16)
            return dot(ones, x[:, :split])[0:1, :]

        def save(u):
            return pltpu.make_async_copy(x, saved.at[u], save_sem)

        def wait_saved(u):
            @pl.when(u > 0)
            def _():
                save(u - 1).wait()

        def gradients(u, split):
            @pl.when(u >= 2)
            def _():
                exchange(u - 2).wait_send()

            def one(j, carry):
                for core, place in ((k, None), (1 - k, outgoing)):
                    cols = pl.ds(pl.multiple_of(j * size + core * half, half), half)
                    into = dot(normed[:, cols], x[:, :split], TN)
                    outof = dot(cot[:, cols], x[:, split:], TN)
                    if place is None:
                        held[u % 3, j, :, :split] = into
                        held[u % 3, j, :, split:] = outof
                    else:
                        place[u % 2, j, :, :split] = into.astype(jnp.bfloat16)
                        place[u % 2, j, :, split:] = outof.astype(jnp.bfloat16)
                return carry

            lax.fori_loop(0, n, one, 0)
            exchange(u).start()

        block = min(512, rows_all)

        def hidden_unit(u, i_hidden, gather_from, gather_count):
            fetch_weights(u).wait()
            wait_saved(u)

            def one(i, carry):
                rows = pl.ds(pl.multiple_of(i * block, block), block)
                pre = dot(normed[rows, :], wbuf[:, :, :HID].reshape(width, HID)) + bias_ref[u][:, :HID]
                value, slope = gelu_both(pre)
                x[rows, HID:] = value.astype(jnp.bfloat16)
                grad = dot(cot[rows, :], wbuf[:, :, HID:].reshape(width, HID))
                x[rows, :HID] = (grad * slope).astype(jnp.bfloat16)
                return carry

            lax.fori_loop(0, rows_all // block, one, 0)
            save(u).start()
            scatter_from = (u - 1) * last
            ticks(gather_from, gather_count, scatter_from, last // 2)
            next_weights(u + 1)
            group, first = hidden_place(i_hidden)
            vec[pl.ds(3 + group, 1), pl.ds(first, HID)] = column_sums(HID)
            gradients(u, HID)
            ticks(0, 0, scatter_from + last // 2, last - last // 2)

        qblock = mask.shape[1]
        window = mask.shape[0]
        qblocks = rows_all // qblock

        def rope(v, rows, sign):
            half_rot = ROT // 2
            lane = lax.broadcasted_iota(jnp.int32, v.shape, 1) % HD
            ahead = pltpu.roll(v, LANES - half_rot, 1)
            behind = pltpu.roll(v, half_rot, 1)
            other = jnp.where(lane < half_rot, -ahead, behind)
            return v * cos_ref[rows, :] + other * (sign * sin_ref[rows, :])

        def recv_kv(s):
            rows = pl.ds(pl.multiple_of((1 - k) * rows_all, rows_all), rows_all)
            return pltpu.make_async_remote_copy(
                src_ref=kv.at[s, :, rows],
                dst_ref=kv.at[s, :, rows],
                send_sem=kvsend_sem.at[s],
                recv_sem=kvrecv_sem.at[s],
                device_id=other_core,
                device_id_type=MESH,
            )

        def send_dkv(s):
            return pltpu.make_async_remote_copy(
                src_ref=dkv.at[:, pl.ds(0, rows_all)],
                dst_ref=dkv_other.at[s],
                send_sem=dsend_sem.at[s],
                recv_sem=drecv_sem.at[s],
                device_id=other_core,
                device_id_type=MESH,
            )

        def attention_unit(u, s, gather_from, gather_count):
            fetch_weights(u).wait()
            wait_saved(u)

            @pl.when((s > 0) & (k == 1))
            def _():
                send_dkv(s - 1).wait_send()

            def project(i, carry):
                rows = pl.ds(pl.multiple_of(i * block, block), block)
                there = pl.ds(pl.multiple_of(k * rows_all + i * block, block), block)
                pre = dot(normed[rows, :], wbuf[:, :, :ATT].reshape(width, ATT)) + bias_ref[u][:, :ATT]
                grad = dot(cot[rows, :], wbuf[:, :, ATT:].reshape(width, LANES))
                g_s[rows, :] = grad.astype(jnp.bfloat16)
                query = rope(pre[:, :LANES], rows, 1.0).astype(jnp.bfloat16)
                q_s[rows, :] = query * jnp.bfloat16(HD**-0.5)
                kv[s, 0, there, :] = rope(pre[:, LANES : 2 * LANES], rows, 1.0).astype(jnp.bfloat16)
                kv[s, 1, there, :] = pre[:, 2 * LANES :].astype(jnp.bfloat16)
                return carry

            lax.fori_loop(0, rows_all // block, project, 0)
            send_kv(s).start()
            dkv[...] = jnp.zeros_like(dkv)
            scatter_from = (u - 1) * last
            per_block = gather_count // qblocks
            early = gather_count - per_block * qblocks
            ticks(gather_from, early, scatter_from, 0)
            recv_kv(s).wait_recv()

            def queries(b, carry):
                first_query = k * rows_all + b * qblock
                first_key = pl.multiple_of(jnp.maximum(first_query + qblock - window, 0), qblock)
                rows = pl.ds(pl.multiple_of(b * qblock, qblock), qblock)
                keys = pl.ds(first_key, window)
                key_at = first_key + lax.broadcasted_iota(jnp.int32, (window, qblock), 0)
                query_at = first_query + lax.broadcasted_iota(jnp.int32, (window, qblock), 1)
                begin = begin_ref[0:1, rows]
                mask[...] = jnp.where((key_at >= begin) & (key_at <= query_at), 0.0, -1e30)
                lane = lax.broadcasted_iota(jnp.int32, (qblock, LANES), 1)
                att = jnp.zeros((qblock, LANES), jnp.float32)
                dq = jnp.zeros((qblock, LANES), jnp.float32)
                for head in range(2):
                    inside = (lane >= head * HD) & (lane < (head + 1) * HD)
                    q_own = jnp.where(inside, q_s[rows, :], jnp.zeros((qblock, LANES), jnp.bfloat16))
                    g_own = jnp.where(inside, g_s[rows, :], jnp.zeros((qblock, LANES), jnp.bfloat16))
                    scores = dot(kv[s, 0, keys, :], q_own, NT) + mask[...]
                    weights = jnp.exp(scores - jnp.max(scores, 0, keepdims=True))
                    probs = weights * (1.0 / jnp.sum(weights, 0, keepdims=True))
                    probs_low = probs.astype(jnp.bfloat16)
                    grad_probs = dot(kv[s, 1, keys, :], g_own, NT)
                    inner = jnp.sum(probs * grad_probs, 0, keepdims=True)
                    grad_scores = (probs * (grad_probs - inner)).astype(jnp.bfloat16)
                    att = jnp.where(inside, dot(probs_low, kv[s, 1, keys, :], TN), att)
                    dq = jnp.where(inside, dot(grad_scores, kv[s, 0, keys, :], TN), dq)
                    dkv[1, keys, :] += dot(probs_low, g_own)
                    dkv[0, keys, :] += dot(grad_scores, q_own)
                x[rows, ATT:] = att.astype(jnp.bfloat16)
                x[rows, :LANES] = rope(dq * HD**-0.5, rows, -1.0).astype(jnp.bfloat16)
                low, high = b * last // qblocks, (b + 1) * last // qblocks
                ticks(gather_from + early + b * per_block, per_block, scatter_from + low, high - low)
                return carry

            lax.fori_loop(0, qblocks, queries, 0)

            @pl.when(k == 1)
            def _():
                send_dkv(s).start()

            @pl.when(k == 0)
            def _():
                send_dkv(s).wait_recv()
                copy = pltpu.make_async_copy(dkv_other.at[s], dkv_tmp, load_sem)
                copy.start()
                copy.wait()

            @pl.when(k == 1)
            def _():
                dkv_tmp[...] = jnp.zeros_like(dkv_tmp)

            def turn(i, carry):
                rows = pl.ds(pl.multiple_of(i * qblock, qblock), qblock)
                there = pl.ds(pl.multiple_of(k * rows_all + i * qblock, qblock), qblock)
                x[rows, LANES : 2 * LANES] = rope(
                    dkv[0, there, :] + dkv_tmp[0, rows, :], rows, -1.0
                ).astype(jnp.bfloat16)
                x[rows, 2 * LANES : ATT] = (dkv[1, there, :] + dkv_tmp[1, rows, :]).astype(jnp.bfloat16)
                return carry

            lax.fori_loop(0, qblocks, turn, 0)
            save(u).start()
            next_weights(u + 1)
            bias_grad = column_sums(ATT)
            for g in range(3):
                vec[g : g + 1, pl.ds(pl.multiple_of(s * LANES, LANES), LANES)] = bias_grad[
                    :, g * LANES : (g + 1) * LANES
                ]
            gradients(u, ATT)


        cot_copy = pltpu.make_async_copy(cot_hbm, cot, save_sem)
        cot_copy.start()
        per_step = 3 * last
        in_hidden = 2 * per_step // 9
        in_attention = per_step - 2 * in_hidden
        lead = max(last, 2 * last - in_hidden)
        norm_blocks = rows_all // stage.shape[0]
        pack(0)
        send_own(0)
        pack(1)

        def begin_step(i, carry):
            @pl.when(i + 2 < units)
            def _():
                pack(i + 2)

            @pl.when(i < norm_blocks)
            def _():
                normalize(i)

            @pl.when(i < lead)
            def _():
                gather_tick(i)

            return carry

        lax.fori_loop(0, max(units - 2, norm_blocks, lead), begin_step, 0)
        cot_copy.wait()
        next_weights(0)
        vec[...] = jnp.zeros_like(vec)
        vec[NIN : NIN + 1, :] = dot(jnp.ones((8, rows_all), jnp.bfloat16), cot[:, columns])[0:1, :]

        def super_step(s, carry):
            base = s * per_step + lead
            hidden_unit(3 * s, 2 * s, base, in_hidden)
            attention_unit(3 * s + 1, s, base + in_hidden, in_attention)
            hidden_unit(3 * s + 2, 2 * s + 1, base + in_hidden + in_attention, in_hidden)
            return carry

        lax.fori_loop(0, steps, super_step, 0)

        save(units - 1).wait()
        exchange(units - 2).wait_send()
        exchange(units - 1).wait_send()

        @pl.when(k == 1)
        def _():
            send_dkv(steps - 1).wait_send()


    def tensor_copy(what, i, source):
        return pltpu.make_async_remote_copy(
            src_ref=source,
            dst_ref=arrived.at[what, i],
            send_sem=tsend_sem.at[what, i],
            recv_sem=trecv_sem.at[what, i],
            device_id={"tensor": lax.rem(tensor + 1 + i, peers)},
            device_id_type=MESH,
        )

    def sums_copy(i):
        return pltpu.make_async_remote_copy(
            src_ref=sums,
            dst_ref=sums_in.at[i],
            send_sem=ssend_sem.at[i],
            recv_sem=srecv_sem.at[i],
            device_id={"tensor": lax.rem(tensor + 1 + i, peers)},
            device_id_type=MESH,
        )

    def finals(xs, tile, blocks, swap_in):
        part = size // 2
        tiles = 2 * peers

        def fetch_tile(q):
            shard = lax.rem(tensor + 1 + q // 2, peers)
            rows = pl.ds(pl.multiple_of(q % 2 * part, part), part)
            return pltpu.make_async_copy(full.at[:, shard, rows], tile.at[q % 2], tile_sem.at[q % 2])

        fetch_xs = pltpu.make_async_copy(saved, xs.at[pl.ds(0, units)], load_sem)
        fetch_xs.start()
        fetch_tile(0).start()
        fetch_xs.wait()
        block = min(512, rows_all)

        def products(q, store):
            @pl.when(q + 1 < tiles)
            def _():
                fetch_tile(q + 1).start()

            fetch_tile(q).wait()

            def one(r, carry):
                rows = pl.ds(pl.multiple_of(r * block, block), block)
                grads, branch = None, None
                for u in range(units):
                    split = ATT if u % 3 == 1 else HID
                    left = dot(xs[u, rows, :split], tile[q % 2, u, :, :split], NT)
                    right = dot(xs[u, rows, split:], tile[q % 2, u, :, split:], NT)
                    grads = left if grads is None else grads + left
                    branch = right if branch is None else branch + right
                store(r, 0, grads)
                store(r, 1, branch)
                return carry

            lax.fori_loop(0, rows_all // block, one, 0)

        scatter_from = (units - 1) * last
        scatter_count = last * (LAG + 1) + 1
        remote = 2 * (peers - 1)

        def remote_tile(q, carry):
            i, h = q // 2, q % 2

            def store(r, what, value):
                rows = pl.ds(pl.multiple_of(r * block, block), block)
                cols = pl.ds(pl.multiple_of(h * part, part), part)
                blocks[what, i, rows, cols] = value.astype(jnp.bfloat16)

            products(q, store)

            @pl.when(h == 1)
            def _():
                tensor_copy(0, i, blocks.at[0, i]).start()

            low, high = q * scatter_count // remote, (q + 1) * scatter_count // remote
            run_ticks(swap_in, 0, 0, scatter_from + low, high - low)
            return carry

        lax.fori_loop(0, remote, remote_tile, 0)

        def start_branch(i, carry):
            tensor_copy(1, i, blocks.at[1, i]).start()
            return carry

        lax.fori_loop(0, peers - 1, start_branch, 0)

        for h in range(2):

            def store(r, what, value):
                for a in range(block // half):
                    held[what, r * (block // half) + a, :, h * part : (h + 1) * part] = value[
                        a * half : (a + 1) * half
                    ]

            products(remote + h, store)

        tok_at, cot_at, out_at = 2 * (peers - 1), 2 * (peers - 1) + 1, 2 * (peers - 1) + 2
        bring = [
            pltpu.make_async_copy(tokens.at[:, columns], xs.at[tok_at, :, pl.ds(0, size)], tile_sem.at[0]),
            pltpu.make_async_copy(cot_hbm.at[:, columns], xs.at[cot_at, :, pl.ds(0, size)], tile_sem.at[1]),
        ]
        for copy in bring:
            copy.start()
        for copy in bring:
            copy.wait()

        def collect(what):
            def one(i, carry):
                tensor_copy(what, i, blocks.at[what, i]).wait_recv()
                copy = pltpu.make_async_copy(
                    arrived.at[what, i], xs.at[what * (peers - 1) + i, :, pl.ds(0, size)], load_sem
                )
                copy.start()
                copy.wait()
                return carry

            lax.fori_loop(0, peers - 1, one, 0)

        def summed(what, r, rows):
            value = held[what, r, :, :size]
            for i in range(peers - 1):
                value += xs[what * (peers - 1) + i, rows, :size].astype(jnp.float32)
            return value

        gain = vec_ref[NIN + 1 : NIN + 2, columns]
        ones = jnp.ones((8, size), jnp.float32)

        def unit_of(rows):
            token = xs[tok_at, rows, :size].astype(jnp.float32)
            return (token - stats[rows, 0:1]) * stats[rows, 1:2]

        collect(0)

        def first_pass(r, carry):
            rows = pl.ds(pl.multiple_of(r * half, half), half)
            grad = summed(0, r, rows)
            held[0, r, :, :size] = grad
            unit = unit_of(rows)
            scaled = grad * gain
            sums[0:8, rows] = lax.dot_general(
                ones, scaled, NT, precision=lax.Precision.HIGHEST, preferred_element_type=jnp.float32
            )
            sums[8:16, rows] = lax.dot_general(
                ones, scaled * unit, NT, precision=lax.Precision.HIGHEST, preferred_element_type=jnp.float32
            )
            vec[NIN + 1 : NIN + 2, :] += jnp.sum(grad * unit, 0, keepdims=True)
            vec[NIN + 2 : NIN + 3, :] += jnp.sum(grad, 0, keepdims=True)
            return carry

        lax.fori_loop(0, rows_all // half, first_pass, 0)
        for i in range(peers - 1):
            sums_copy(i).start()
        to_core = pltpu.make_async_remote_copy(
            src_ref=vec, dst_ref=vec_core, send_sem=vsend_sem.at[0], recv_sem=vrecv_sem.at[0],
            device_id=other_core, device_id_type=MESH,
        )
        to_core.start()
        for i in range(peers - 1):
            sums_copy(i).wait_recv()
        inv_width = 1.0 / width

        def second_pass(r, carry):
            rows = pl.ds(pl.multiple_of(r * half, half), half)
            means = sums[:, rows]
            for i in range(peers - 1):
                means += sums_in[i, :, rows]
            means = (means * inv_width).T
            unit = unit_of(rows)
            held[0, r, :, :size] = stats[rows, 1:2] * (
                held[0, r, :, :size] * gain - means[:, 0:1] - unit * means[:, 8:9]
            ) + xs[cot_at, rows, :size].astype(jnp.float32)
            return carry

        lax.fori_loop(0, rows_all // half, second_pass, 0)
        put_grad = pltpu.make_async_copy(held.at[0, :, :, pl.ds(0, size)], token_grad, out_sem.at[0])
        put_grad.start()

        to_core.wait_recv()
        vec_line[z] = vec[...] + vec_core[...]

        def along_dp(i):
            return pltpu.make_async_remote_copy(
                src_ref=vec_line.at[z], dst_ref=vec_line.at[z],
                send_sem=vsend_sem.at[1 + i], recv_sem=vrecv_sem.at[1 + i],
                device_id={"dp": lax.rem(z + 1 + i, n)}, device_id_type=MESH,
            )

        def from_dp(i):
            there = lax.rem(z + n - 1 - i, n)
            return pltpu.make_async_remote_copy(
                src_ref=vec_line.at[there], dst_ref=vec_line.at[there],
                send_sem=vsend_sem.at[1 + i], recv_sem=vrecv_sem.at[1 + i],
                device_id={"dp": lax.rem(z + 1 + i, n)}, device_id_type=MESH,
            )

        for i in range(n - 1):
            along_dp(i).start()
        for i in range(n - 1):
            from_dp(i).wait_recv()
        vec_sum = vec_line[0]
        for i in range(1, n):
            vec_sum += vec_line[i]
        vec_all[tensor] = vec_sum

        def along_tensor(i):
            return pltpu.make_async_remote_copy(
                src_ref=vec_all.at[tensor], dst_ref=vec_all.at[tensor],
                send_sem=vsend_sem.at[n + i], recv_sem=vrecv_sem.at[n + i],
                device_id={"tensor": lax.rem(tensor + 1 + i, peers)}, device_id_type=MESH,
            )

        def from_tensor(i):
            there = lax.rem(tensor + peers - 1 - i, peers)
            return pltpu.make_async_remote_copy(
                src_ref=vec_all.at[there], dst_ref=vec_all.at[there],
                send_sem=vsend_sem.at[n + i], recv_sem=vrecv_sem.at[n + i],
                device_id={"tensor": lax.rem(tensor + 1 + i, peers)}, device_id_type=MESH,
            )

        for i in range(peers - 1):
            along_tensor(i).start()

        collect(1)
        out_bias = vec_ref[NIN : NIN + 1, columns]

        def third_pass(r, carry):
            rows = pl.ds(pl.multiple_of(r * half, half), half)
            value = xs[tok_at, rows, :size].astype(jnp.float32) + (summed(1, r, rows) + out_bias)
            xs[out_at, rows, :size] = value.astype(jnp.bfloat16)
            return carry

        lax.fori_loop(0, rows_all // half, third_pass, 0)
        put_result = pltpu.make_async_copy(xs.at[out_at, :, pl.ds(0, size)], result, out_sem.at[1])
        put_result.start()

        for i in range(peers - 1):
            from_tensor(i).wait_recv()
        vec_grad[...] = vec_all[...]
        put_grad.wait()
        put_result.wait()
        to_core.wait_send()
        for i in range(n - 1):
            along_dp(i).wait_send()
        for i in range(peers - 1):
            along_tensor(i).wait_send()
            sums_copy(i).wait_send()
            tensor_copy(0, i, blocks.at[0, i]).wait_send()
            tensor_copy(1, i, blocks.at[1, i]).wait_send()

    low, wide = jnp.bfloat16, jnp.float32
    window, qblock = rows_all + min(256, rows_all), min(256, rows_all)
    pl.run_scoped(
        forward_backward,
        pltpu.VMEM((rows_all, width), low),
        pltpu.VMEM((rows_all, width), low),
        pltpu.VMEM((rows_all // 4, width), low),
        pltpu.VMEM((size, ATT), wide),
        pltpu.VMEM((HID, size), wide),
        pltpu.VMEM((size, WIDE), low),
        pltpu.VMEM((n, size, WIDE), low),
        pltpu.VMEM((rows_all, WIDE), low),
        pltpu.VMEM((rows_all, LANES), low),
        pltpu.VMEM((rows_all, LANES), low),
        pltpu.VMEM((2, 2 * rows_all, LANES), wide),
        pltpu.VMEM((2, rows_all, LANES), wide),
        pltpu.VMEM((window, qblock), wide),
        pltpu.VMEM((2, n, half, WIDE), low),
        pltpu.VMEM((n, half, WIDE), low),
    )
    pl.run_scoped(
        finals,
        pltpu.VMEM((max(units, 2 * peers + 1), rows_all, WIDE), low),
        pltpu.VMEM((2, units, size // 2, WIDE), low),
        pltpu.VMEM((2, peers - 1, rows_all, size), low),
        pltpu.VMEM((n, half, WIDE), low),
    )


    def drain_kv(s, carry):
        send_kv(s).wait_send()
        return carry

    lax.fori_loop(0, steps, drain_kv, 0)

    def drain(m, carry):
        g, s = m // last, m % last + 1

        @pl.when(s == 1)
        def _():
            @pl.when(z < last)
            def _():
                hop(0, g, 0, z).wait_send()

            @pl.when(z > 0)
            def _():
                hop(1, g, 0, z).wait_send()

            @pl.when(g >= units - (LAG + 3))
            def _():
                keep(g).wait()
                share(g, mine).wait_send()

            share(g, theirs).wait_recv()

        @pl.when(z >= s)
        def _():
            @pl.when(z < last)
            def _():
                hop(0, g, s, z - s).wait_send()

            across(0, g, s - 1, z - s, mine).wait_send()

        @pl.when(z + s <= last)
        def _():
            @pl.when(z > 0)
            def _():
                hop(1, g, s, z + s).wait_send()

            across(1, g, s - 1, z + s, mine).wait_send()

        for way in range(2):
            distance = z if way == 0 else last - z

            @pl.when(distance < last - (s - 1))
            def _():
                pass_on(way, g, s - 1).wait_send()

        return carry

    lax.fori_loop(0, units * last, drain, 0)


def run_block(in_weight, out_weight, tokens, cotangent, bias, vectors, cosine, sine, begin):
    n, peers = lax.axis_size("dp"), lax.axis_size("tensor")
    size, cols_all = in_weight.shape[1:]
    steps = cols_all // LANES
    units = 3 * steps
    half = size // 2
    rows, width = tokens.shape
    assert width == n * size == peers * cols_all and size == cols_all and rows == n * half
    low, wide = jnp.bfloat16, jnp.float32
    anywhere = pl.BlockSpec(memory_space=pl.ANY)
    vm = pl.BlockSpec(memory_space=pltpu.VMEM)
    dma = pltpu.SemaphoreType.DMA
    return pl.pallas_call(
        functools.partial(block_kernel, n, steps, peers),
        out_shape=(
            jax.ShapeDtypeStruct((units, n, size, WIDE), low),
            jax.ShapeDtypeStruct((units, rows, WIDE), low),
            jax.ShapeDtypeStruct((units, size, WIDE), wide),
            jax.ShapeDtypeStruct((units, n, half, WIDE), low),
            jax.ShapeDtypeStruct((steps, 2, rows, LANES), wide),
            jax.ShapeDtypeStruct((2, peers - 1, rows, size), low),
            jax.ShapeDtypeStruct((rows, size), low),
            jax.ShapeDtypeStruct((n, half, size), wide),
            jax.ShapeDtypeStruct((peers, 16, size), wide),
        ),
        in_specs=[anywhere] * 4 + [vm] * 5,
        out_specs=[anywhere] * 8 + [vm],
        scratch_shapes=[
            pltpu.VMEM((steps, 2, 2 * rows, LANES), low),
            pltpu.VMEM((3, n, half, WIDE), wide),
            pltpu.VMEM((units, n + 1, half, WIDE), low),
            pltpu.VMEM((LAG + 3, half, WIDE), wide),
            pltpu.VMEM((rows, LANES), wide),
            pltpu.VMEM((16, size), wide),
            pltpu.VMEM((16, size), wide),
            pltpu.VMEM((n, 16, size), wide),
            pltpu.VMEM((peers, 16, size), wide),
            pltpu.VMEM((16, rows), wide),
            pltpu.VMEM((peers - 1, 16, rows), wide),
            dma((2, units, n)),
            dma((2, units, n)),
            dma((2, units, n)),
            dma((2, units, n)),
            dma((units,)),
            dma((units,)),
            dma((2, units, n - 1)),
            dma((2, units, n - 1)),
            dma((units,)),
            dma((units,)),
            dma((units,)),
            dma((steps,)),
            dma((steps,)),
            dma((steps,)),
            dma((steps,)),
            dma,
            dma,
            dma,
            dma((4,)),
            dma((2, peers - 1)),
            dma((2, peers - 1)),
            dma((peers - 1,)),
            dma((peers - 1,)),
            dma((n + peers - 1,)),
            dma((n + peers - 1,)),
            dma((2,)),
            dma((2,)),
        ],
        compiler_params=pltpu.CompilerParams(
            collective_id=1, has_side_effects=True, vmem_limit_bytes=VMEM_LIMIT
        ),
        name="parallel_block",
    )(in_weight, out_weight, tokens, cotangent, bias, vectors, cosine, sine, begin)


def adam_kernel(turned, total, w, m, v, new_w, new_m, new_v):
    gradient = total[0].T if turned else total[0]
    new_w[0], new_m[0], new_v[0] = adamw(w[0], gradient, m[0], v[0], rate_matrix, weight_decay)


def adam_weights(turned, total, weight, first, second):
    groups, cols_all = weight.shape[0], weight.shape[1 if turned else 2]
    size = total.shape[1]
    lead = 1 if turned else 3

    def place(g, c):
        i = ((g - lead) * cols_all + c * LANES) // HID
        unit = jnp.where(g < lead, 3 * c + 1, 3 * (i // 2) + 2 * (i % 2))
        lane = jnp.where(g < lead, 3 if turned else g, c % 2 + (2 if turned else 0))
        return unit, 0, lane

    if turned:
        spec = pl.BlockSpec((1, LANES, size), lambda g, c: (g, c, 0))
    else:
        spec = pl.BlockSpec((1, size, LANES), lambda g, c: (g, 0, c))
    return pl.pallas_call(
        functools.partial(adam_kernel, turned),
        grid=(groups, cols_all // LANES),
        out_shape=tuple(jax.ShapeDtypeStruct(weight.shape, jnp.float32) for _ in range(3)),
        in_specs=[pl.BlockSpec((1, size, LANES), place)] + [spec] * 3,
        out_specs=[spec] * 3,
        compiler_params=pltpu.CompilerParams(vmem_limit_bytes=VMEM_LIMIT),
        name="adam_out" if turned else "adam_in",
    )(total, weight, first, second)


def layout(lengths_row, row_span):
    seg_ends = jnp.cumsum(lengths_row)
    seg_starts = seg_ends - lengths_row
    places = jnp.arange(row_span, dtype=jnp.int32)
    segment = jnp.sum((places[:, None] >= seg_ends[None, :]).astype(jnp.int32), 1)
    numbers = jnp.arange(lengths_row.shape[0], dtype=jnp.int32)
    return jnp.sum(jnp.where(segment[:, None] == numbers[None, :], seg_starts[None, :], 0), 1)


def rope_tables(places):
    half_rot = ROT // 2
    lane = jnp.arange(2 * HD, dtype=jnp.int32) % HD
    exponent = (lane % half_rot).astype(jnp.float32)
    frequency = 10000.0 ** (-2.0 * exponent / ROT)
    angles = places.astype(jnp.float32)[:, None] * frequency[None, :]
    turned = (lane < ROT)[None, :]
    cosine = jnp.where(turned, jnp.cos(angles), 1.0)
    sine = jnp.where(turned, jnp.sin(angles), 0.0)
    return cosine, sine


def body(
    tokens,
    cotangent,
    lengths,
    in_weight,
    out_weight,
    vectors,
    in_first,
    in_second,
    out_first,
    out_second,
    vec_first,
    vec_second,
):
    local_rows, model_width = tokens.shape
    slice_width = in_weight.shape[2]
    context_count = lax.axis_size("context")
    context_index = lax.axis_index("context")
    tensor_index = lax.axis_index("tensor")
    row_span = local_rows * context_count
    first_row = context_index * local_rows
    begin_all = layout(lengths[0], row_span)
    begin = lax.dynamic_slice_in_dim(begin_all, first_row, local_rows, 0)
    places = first_row + jnp.arange(local_rows, dtype=jnp.int32) - begin
    tables = rope_tables(places)

    column = tensor_index * slice_width
    in_bias = lax.dynamic_slice_in_dim(vectors[:NIN], column, slice_width, 1)
    steps = slice_width // LANES
    hid_bias = in_bias[3:].reshape(steps, 2, HID)
    att_bias = in_bias[:3].reshape(3, steps, LANES).transpose(1, 0, 2).reshape(steps, ATT)
    bias = jnp.stack(
        [
            jnp.pad(hid_bias[:, 0], ((0, 0), (0, WIDE - HID))),
            jnp.pad(att_bias, ((0, 0), (0, WIDE - ATT))),
            jnp.pad(hid_bias[:, 1], ((0, 0), (0, WIDE - HID))),
        ],
        1,
    ).reshape(3 * steps, 1, WIDE)
    by_group = jnp.transpose(in_weight, (1, 0, 2))
    _, _, total, _, _, _, result, token_grad, vec_grad = run_block(
        by_group, out_weight, tokens, cotangent, bias, vectors, tables[0], tables[1], begin[None]
    )
    token_grad = token_grad.reshape(local_rows, slice_width)
    vector_grad = jnp.transpose(vec_grad, (1, 0, 2)).reshape(-1, model_width)[: NIN + 3]
    new_vectors, new_vec_first, new_vec_second = adamw(
        vectors, vector_grad, vec_first, vec_second, rate_vector, 0.0
    )
    new_in, new_in_first, new_in_second = (
        jnp.transpose(v, (1, 0, 2))
        for v in adam_weights(
            False, total, by_group, jnp.transpose(in_first, (1, 0, 2)), jnp.transpose(in_second, (1, 0, 2))
        )
    )
    new_out, new_out_first, new_out_second = adam_weights(
        True, total, out_weight, out_first, out_second
    )
    return (
        result,
        token_grad,
        new_in,
        new_in_first,
        new_in_second,
        new_out,
        new_out_first,
        new_out_second,
        new_vectors,
        new_vec_first,
        new_vec_second,
    )


def solution(mesh):
    return jax.shard_map(
        body,
        mesh=mesh,
        in_specs=(
            P(("dp", "context"), None),
            P(("dp", "context"), None),
            P("dp", None),
            P("dp", None, "tensor"),
            P(None, "tensor", "dp"),
            P(),
            P("dp", None, "tensor"),
            P("dp", None, "tensor"),
            P(None, "tensor", "dp"),
            P(None, "tensor", "dp"),
            P(),
            P(),
        ),
        out_specs=(
            P(("dp", "context"), "tensor"),
            P(("dp", "context"), "tensor"),
            P("dp", None, "tensor"),
            P("dp", None, "tensor"),
            P("dp", None, "tensor"),
            P(None, "tensor", "dp"),
            P(None, "tensor", "dp"),
            P(None, "tensor", "dp"),
            P(),
            P(),
            P(),
        ),
        check_vma=False,
    )
```

time: 866 us -> 559 us (0.65)
  matrix products: 177 us -> 0 us
  Pallas kernels: 381 us -> 544 us
  waiting for transfers between devices: 116 us -> 0 us
  local copies, waits for them, and re-layouts: 90.9 us -> 4.96 us
  other arithmetic: 68.2 us -> 6.16 us
  between operations: 14.7 us -> 0.79 us
  blocking collectives: 11.5 us -> 0 us
    dot_general x24 -> x0, matrix products: 177 us -> none  [the longest x12 90.5 us: body(): lax.dot_general(saved[u][:, :splits[u]], full[u].reshape(model_width, WID...]
    pallas_call x1 -> x3, Pallas kernels: 381 us -> 544 us  [the longest x1 495 us: run_block(): pl.pallas_call(functools.partial(block_kernel, n, steps, peers), out_shap...]
    psum x1 -> x0, waiting for transfers between devices: 116 us -> none  [body(): vector_grad = lax.psum(vector_rows, ('dp', 'context', 'tensor'))]
    slice x13 -> x1, local copies, waits for them, and re-layouts: 32.8 us -> 0.96 us  [body(): jnp.transpose(vec_grad, (1, 0, 2)).reshape(-1, model_width)[:NIN + 3]]
    sub x3 -> x1, other arithmetic: 27.2 us -> 0.8 us  [adamw(): master - step_rate * (first_hat / (jnp.sqrt(second_hat) + adam_eps) + dec...]
    squeeze x2 -> x0, local copies, waits for them, and re-layouts: 19 us -> none  [the longest x1 9.87 us: unpack_columns(): att = by_step[:, 1]]
    unnamed x107 -> x14, local copies, waits for them, and re-layouts: 14.4 us -> 2.38 us
    another operation x5 -> x0, local copies, waits for them, and re-layouts: 11.7 us -> none  [the longest x1 8.61 us: pack_weights(): jnp.stack([hid[:, 0], att, hid[:, 1]], 1).reshape(3 * steps, size, WIDE)]
  transfers between devices with their start and end apart: 3 -> 0, of which waited for: 1 -> 0; matrix products, arithmetic and copies ran while one was open for 19% -> 0% of each run, Pallas kernels for 0% -> 0%
where the time goes in v2:
time: 559 us; the launch traced here: 556 us
  Pallas kernels  544 us (97%)
  other arithmetic  6.16 us (1%)
    pallas_call x1, Pallas kernels, run_block(): pl.pallas_call(functools.partial(block_kernel, n, steps, peers), out_shap...  495 us
    pallas_call x2, Pallas kernels, adam_weights(): pl.pallas_call(functools.partial(adam_kernel, turned), grid=(groups, cols...  49.7 us

profile of v2, /device:TPU:0, one launch (start us, length us, event | category | flops | bytes accessed | tf_op | source)
XLA Modules:
  0.0 556.4 jit_solution(15288217520429553983)
XLA Ops:
  0.6 0.8 reduce-window.4
  1.5 0.7 fusion.7
  2.2 0.1 convert_reduce_fusion
  2.3 0.1 select_reduce_fusion
  2.3 0.6 subtract_convert_fusion
  2.9 0.8 slice.21
  3.8 0.1 dynamic-slice
  4.0 0.6 reshape.84.bias_ref
  4.7 3.0 fusion.1
  7.7 0.0 copy-start.2
  7.7 0.0 copy-start.3
  7.7 494.7 %parallel_block.1 = (bf16[12,4,512,512]{3,2,1,0:T(8,128)(2,1)}, bf16[12,1024,512]{2,1,0:T(8,128)(2,1)}, f32[12,512,512]{2,1,0:T(8,128)}, bf16[12,4,256,512]{3,2,...) custom-call(f32[7,512,512]{2,1,0:T(8,128)} %bitcast.29, ...), custom_call_target="tpu_custom_call" | custom-call | tf_op jit(solution)/shard_map/parallel_block/pallas_call | solution.py:975
  502.5 1.0 copy.32
  503.5 0.0 copy-done.2
  503.5 0.0 copy-done.3
  503.5 0.0 copy-done.4
  503.5 0.8 multiply_subtract_fusion
  504.3 21.1 %adam_out.1 = (f32[5,512,512]{2,1,0:T(8,128)}, f32[5,512,512]{2,1,0:T(8,128)}, f32[5,512,512]{2,1,0:T(8,128)}) custom-call(f32[12,512,512]{2,1,0:T(8,128)} %get-tuple-element.23.total, f32[5,512,512]{2,1,0:T(8,128)} %w.1, f32[5,512,512]{2,1,0:T(8,128)} %m.1, f32[5,512,512]{2,1,0:T(8,128)} %v.1), custom_call_target="tpu_custom_call" | custom-call | tf_op jit(solution)/shard_map/adam_out/pallas_call | solution.py:1057
  525.4 0.0 copy-start
  525.4 28.7 %adam_in.1 = (f32[7,512,512]{2,1,0:T(8,128)}, f32[7,512,512]{2,1,0:T(8,128)}, f32[7,512,512]{2,1,0:T(8,128)}) custom-call(f32[12,512,512]{2,1,0:T(8,128)} %get-tuple-element.23.total, f32[7,512,512]{2,1,0:T(8,128)} %bitcast.30, f32[7,512,512]{2,1,0:T(8,128)} %bitcast.31, f32[7,512,512]{2,1,0:T(8,128)} %bitcast.32), custom_call_target="tpu_custom_call" | custom-call | tf_op jit(solution)/shard_map/adam_in/pallas_call | solution.py:1057
  554.1 0.0 copy-done.1
  554.1 1.0 copy.36
  555.0 0.0 copy-done
  555.0 1.3 copy.37
  (16 shorter events, 0.2 us)
Async XLA Ops:
  7.7 495.8 %copy-start.2 = (f32[10,2048]{1,0:T(8,128)S(1)}, f32[10,2048]{1,0:T(8,128)}, u32[]{:S(2)}) copy-start(f32[10,2048]{1,0:T(8,128)} %vec_ref.1) | copy-start | bytes 245764
  7.7 495.8 %copy-start.3 = (f32[10,2048]{1,0:T(8,128)S(1)}, f32[10,2048]{1,0:T(8,128)}, u32[]{:S(2)}) copy-start(f32[10,2048]{1,0:T(8,128)} %param.22) | copy-start | bytes 245764
  7.7 495.8 %copy-start.4 = (f32[10,2048]{1,0:T(8,128)S(1)}, f32[10,2048]{1,0:T(8,128)}, u32[]{:S(2)}) copy-start(f32[10,2048]{1,0:T(8,128)} %param.23) | copy-start | bytes 245764
  525.4 28.7 %copy-start.1 = (bf16[1024,512]{1,0:T(8,128)(2,1)S(1)}, bf16[1024,512]{1,0:T(8,128)(2,1)}, u32[]{:S(2)}) copy-start(bf16[1024,512]{1,0:T(8,128)(2,1)} %get-tuple-element.51) | copy-start | bytes 3145732
  525.4 29.6 %copy-start = (f32[4,256,512]{2,1,0:T(8,128)S(1)}, f32[4,256,512]{2,1,0:T(8,128)}, u32[]{:S(2)}) copy-start(f32[4,256,512]{2,1,0:T(8,128)} %get-tuple-element.22) | copy-start | bytes 6291460

commit v3 on v2

--- a/solution.py
+++ b/solution.py
@@ -38,7 +38,7 @@
 WIDE = 4 * LANES
 HID = WIDE // 2
 ATT = 3 * LANES
-LAG = 2
+LAG = 3
 
 NT = (((1,), (1,)), ((), ()))
 NN = (((1,), (0,)), ((), ()))
@@ -72,6 +72,20 @@
     return value, slope
 
 
+def schedule(n):
+    last = n - 1
+    per_step = 3 * last
+    in_hidden = 2 * per_step // 9
+    in_attention = per_step - 2 * in_hidden
+    done = (in_hidden, in_hidden + in_attention, per_step)
+    lead = max([last * (n + i) - done[i] for i in range(3)] + [last * (n - 1)])
+    behind = max(done[i] - last * i for i in range(3))
+    depth = 3
+    while any(done[i] - behind < last * (i - depth) + LAG * (n - 2) + 1 for i in range(3)):
+        depth += 1
+    return per_step, in_hidden, in_attention, lead, behind, depth
+
+
 def block_kernel(
     n, steps, peers,
     in_w, out_w, tokens, cot_hbm, bias_ref, vec_ref, cos_ref, sin_ref, begin_ref,
@@ -79,16 +93,17 @@
     kv, held, line, outbox, stats, vec, vec_core, vec_line, vec_all, sums, sums_in,
     send_sem, recv_sem, psend_sem, precv_sem,
     xsend_sem, xrecv_sem, lsend_sem, lrecv_sem, keep_sem, fsend_sem, frecv_sem,
-    kvsend_sem, kvrecv_sem, dsend_sem, drecv_sem, load_sem, save_sem, weight_sem, pack_sem,
+    kvsend_sem, kvrecv_sem, dsend_sem, drecv_sem, load_sem, save_sem, weight_sem, pack_sem, put_sem, rows_sem, swap_sem,
     tsend_sem, trecv_sem, ssend_sem, srecv_sem, vsend_sem, vrecv_sem, tile_sem, out_sem,
 ):
     units = 3 * steps
+    last = n - 1
+    per_step, in_hidden, in_attention, lead, behind, depth = schedule(n)
     size, cols_all = in_w.shape[1], in_w.shape[2]
     half = size // 2
     rows_all, width = tokens.shape
     tensor = lax.axis_index("tensor")
     columns = pl.ds(pl.multiple_of(tensor * size, size), size)
-    last = n - 1
     z = lax.axis_index("dp")
     k = lax.axis_index("context")
     mine = pl.ds(pl.multiple_of(k * half, half), half)
@@ -127,14 +142,15 @@
             hop(1, g, 0, z).start()
 
     def gather_tick(m):
-        @pl.when(m < units * last)
-        def _():
-            g, s = m // last, m % last + 1
-
-            @pl.when((s == 1) & (g < units - 1))
-            def _():
-                send_own(g + 1)
-
+        s = m % last + 1
+        g = m // last - (s - 1)
+
+        @pl.when((s == 1) & (g < units - 1))
+        def _():
+            send_own(g + 1)
+
+        @pl.when((g >= 0) & (g < units))
+        def _():
             @pl.when(z >= s)
             def _():
                 hop(0, g, s - 1, z - s).wait_recv()
@@ -208,11 +224,11 @@
         )
 
     def keep(g):
-        return pltpu.make_async_copy(outbox.at[g % (LAG + 3)], total.at[g, mine], keep_sem.at[g])
+        return pltpu.make_async_copy(outbox.at[g % (LAG + 2)], total.at[g, mine], keep_sem.at[g])
 
     def share(g, rows):
         return pltpu.make_async_remote_copy(
-            src_ref=outbox.at[g % (LAG + 3)],
+            src_ref=outbox.at[g % (LAG + 2)],
             dst_ref=total.at[g, rows],
             send_sem=fsend_sem.at[g],
             recv_sem=frecv_sem.at[g],
@@ -220,23 +236,27 @@
             device_id_type=MESH,
         )
 
+    def fetch_swapped(g, swap_in):
+        @pl.when(g >= 0)
+        def _():
+            exchange_from(swap_in, g).wait_recv()
+            pltpu.make_async_copy(swap.at[g], swap_in, swap_sem).start()
+
     def prepare(g, swap_in):
-        exchange_from(swap_in, g).wait_recv()
-        pltpu.make_async_copy(swap.at[g], swap_in, load_sem).start()
-        pltpu.make_async_copy(swap.at[g], swap_in, load_sem).wait()
-        box = g % (LAG + 3)
-
-        @pl.when(g >= LAG + 3)
-        def _():
-            keep(g - (LAG + 3)).wait()
-            share(g - (LAG + 3), mine).wait_send()
+        pltpu.make_async_copy(swap.at[g], swap_in, swap_sem).wait()
+        box = g % (LAG + 2)
+
+        @pl.when(g >= LAG + 2)
+        def _():
+            keep(g - (LAG + 2)).wait()
+            share(g - (LAG + 2), mine).wait_send()
 
         def one(j, carry):
-            held[g % 3, j] += swap_in[j].astype(jnp.float32)
+            held[g % depth, j] += swap_in[j].astype(jnp.float32)
             return carry
 
         lax.fori_loop(0, n, one, 0)
-        outbox[box] = held[g % 3, z]
+        outbox[box] = held[g % depth, z]
 
     def scatter_step(way, m, distance):
         @pl.when((m >= 0) & (m < units * last))
@@ -247,7 +267,7 @@
 
             @pl.when(distance == 0)
             def _():
-                line[g, slot] = held[g % 3, shard].astype(jnp.bfloat16)
+                line[g, slot] = held[g % depth, shard].astype(jnp.bfloat16)
                 pass_on(way, g, i).start()
 
             @pl.when((distance > 0) & (distance <= last - i))
@@ -256,13 +276,13 @@
 
                 @pl.when(distance < last - i)
                 def _():
-                    line[g, slot] = (line[g, slot].astype(jnp.float32) + held[g % 3, shard]).astype(
+                    line[g, slot] = (line[g, slot].astype(jnp.float32) + held[g % depth, shard]).astype(
                         jnp.bfloat16
                     )
                     pass_on(way, g, i).start()
 
     def finish(g):
-        box = g % (LAG + 3)
+        box = g % (LAG + 2)
 
         @pl.when(z > 0)
         def _():
@@ -282,7 +302,7 @@
 
         scatter_step(0, t - LAG * z, z)
         scatter_step(1, t - LAG * (last - z), last - z)
-        done = t - last * (LAG + 1)
+        done = t - last * LAG
 
         @pl.when((done >= 0) & (done % last == 0))
         def _():
@@ -310,17 +330,24 @@
         def ticks(gather_from, gather_count, scatter_from, scatter_count):
             run_ticks(swap_in, gather_from, gather_count, scatter_from, scatter_count)
 
+        part = stage.shape[1]
+        norm_blocks = rows_all // part
+
+        def fetch_rows(i):
+            rows = pl.ds(pl.multiple_of(i * part, part), part)
+            return pltpu.make_async_copy(tokens.at[rows], stage.at[i % 2], rows_sem.at[i % 2])
+
         def normalize(i):
-            part = stage.shape[0]
-            rows = pl.ds(pl.multiple_of(i * part, part), part)
-            copy = pltpu.make_async_copy(tokens.at[rows], stage, load_sem)
-            copy.start()
-            copy.wait()
+            @pl.when(i + 1 < norm_blocks)
+            def _():
+                fetch_rows(i + 1).start()
+
+            fetch_rows(i).wait()
 
             def few(r, c):
                 sub = pl.ds(pl.multiple_of(r * 64, 64), 64)
                 there = pl.ds(pl.multiple_of(i * part + r * 64, 64), 64)
-                inputs = stage[sub, :].astype(jnp.float32)
+                inputs = stage[i % 2, sub, :].astype(jnp.float32)
                 centered = inputs - jnp.mean(inputs, 1, keepdims=True)
                 inv_dev = lax.rsqrt(jnp.mean(centered * centered, 1, keepdims=True) + norm_eps)
                 normed[there, :] = (
@@ -335,48 +362,65 @@
         def hidden_place(i):
             return i * HID // cols_all, pl.multiple_of(i * HID % cols_all, HID)
 
-        def pack(u):
-            s = u // 3
-
-            def fetch(copies):
+        def fetch_raw(u, start):
+            s, slot = u // 3, u % 2
+
+            def each(copies):
                 for copy in copies:
-                    copy.start()
-                for copy in copies:
-                    copy.wait()
+                    copy.start() if start else copy.wait()
 
             @pl.when(u % 3 == 1)
             def _():
                 cols = pl.ds(pl.multiple_of(s * LANES, LANES), LANES)
-                fetch(
+                each(
                     [
                         pltpu.make_async_copy(
-                            in_w.at[g, :, cols], raw_in.at[:, pl.ds(g * LANES, LANES)], pack_sem.at[g]
+                            in_w.at[g, :, cols],
+                            raw_in.at[slot, :, pl.ds(g * LANES, LANES)],
+                            pack_sem.at[slot, g],
                         )
                         for g in range(3)
                     ]
-                    + [pltpu.make_async_copy(out_w.at[0, cols], raw_out.at[pl.ds(0, LANES)], pack_sem.at[3])]
+                    + [
+                        pltpu.make_async_copy(
+                            out_w.at[0, cols], raw_out.at[slot, pl.ds(0, LANES)], pack_sem.at[slot, 3]
+                        )
+                    ]
                 )
-                packed[:, :ATT] = raw_in[...].astype(jnp.bfloat16)
-                packed[:, ATT:] = raw_out[:LANES, :].astype(jnp.bfloat16).T
 
             @pl.when(u % 3 != 1)
             def _():
                 group, first = hidden_place(2 * s + (u % 3) // 2)
                 cols = pl.ds(first, HID)
-                fetch(
+                each(
                     [
                         pltpu.make_async_copy(
-                            in_w.at[3 + group, :, cols], raw_in.at[:, pl.ds(0, HID)], pack_sem.at[0]
+                            in_w.at[3 + group, :, cols],
+                            raw_in.at[slot, :, pl.ds(0, HID)],
+                            pack_sem.at[slot, 0],
                         ),
-                        pltpu.make_async_copy(out_w.at[1 + group, cols], raw_out, pack_sem.at[1]),
+                        pltpu.make_async_copy(out_w.at[1 + group, cols], raw_out.at[slot], pack_sem.at[slot, 1]),
                     ]
                 )
-                packed[:, :HID] = raw_in[:, :HID].astype(jnp.bfloat16)
-                packed[:, HID:] = raw_out[...].astype(jnp.bfloat16).T
-
-            copy = pltpu.make_async_copy(packed, full.at[u, z], load_sem)
-            copy.start()
-            copy.wait()
+
+        def put_packed(u):
+            return pltpu.make_async_copy(packed.at[u % 2], full.at[u, z], put_sem.at[u % 2])
+
+        def pack(u):
+            slot = u % 2
+            fetch_raw(u, False)
+
+            @pl.when(u % 3 == 1)
+            def _():
+                packed[slot, :, :ATT] = raw_in[slot].astype(jnp.bfloat16)
+                packed[slot, :, ATT:] = raw_out[slot, :LANES, :].astype(jnp.bfloat16).T
+
+            @pl.when(u % 3 != 1)
+            def _():
+                packed[slot, :, :HID] = raw_in[slot, :, :HID].astype(jnp.bfloat16)
+                packed[slot, :, HID:] = raw_out[slot].astype(jnp.bfloat16).T
+
+            put_packed(u).start()
 
         def fetch_weights(u):
             return pltpu.make_async_copy(full.at[u], wbuf, weight_sem)
@@ -410,8 +454,8 @@
                     into = dot(normed[:, cols], x[:, :split], TN)
                     outof = dot(cot[:, cols], x[:, split:], TN)
                     if place is None:
-                        held[u % 3, j, :, :split] = into
-                        held[u % 3, j, :, split:] = outof
+                        held[u % depth, j, :, :split] = into
+                        held[u % depth, j, :, split:] = outof
                     else:
                         place[u % 2, j, :, :split] = into.astype(jnp.bfloat16)
                         place[u % 2, j, :, split:] = outof.astype(jnp.bfloat16)
@@ -422,7 +466,7 @@
 
         block = min(512, rows_all)
 
-        def hidden_unit(u, i_hidden, gather_from, gather_count):
+        def hidden_unit(u, i_hidden, at):
             fetch_weights(u).wait()
             wait_saved(u)
 
@@ -437,13 +481,12 @@
 
             lax.fori_loop(0, rows_all // block, one, 0)
             save(u).start()
-            scatter_from = (u - 1) * last
-            ticks(gather_from, gather_count, scatter_from, last // 2)
+            fetch_swapped(u - 1, swap_in)
+            ticks(at + lead, in_hidden, at - behind, in_hidden)
             next_weights(u + 1)
             group, first = hidden_place(i_hidden)
             vec[pl.ds(3 + group, 1), pl.ds(first, HID)] = column_sums(HID)
             gradients(u, HID)
-            ticks(0, 0, scatter_from + last // 2, last - last // 2)
 
         qblock = mask.shape[1]
         window = mask.shape[0]
@@ -478,7 +521,7 @@
                 device_id_type=MESH,
             )
 
-        def attention_unit(u, s, gather_from, gather_count):
+        def attention_unit(u, s, at):
             fetch_weights(u).wait()
             wait_saved(u)
 
@@ -501,10 +544,10 @@
             lax.fori_loop(0, rows_all // block, project, 0)
             send_kv(s).start()
             dkv[...] = jnp.zeros_like(dkv)
-            scatter_from = (u - 1) * last
-            per_block = gather_count // qblocks
-            early = gather_count - per_block * qblocks
-            ticks(gather_from, early, scatter_from, 0)
+            per_block = in_attention // qblocks
+            early = in_attention - per_block * qblocks
+            fetch_swapped(u - 1, swap_in)
+            ticks(at + lead, early, at - behind, early)
             recv_kv(s).wait_recv()
 
             def queries(b, carry):
@@ -536,8 +579,8 @@
                     dkv[0, keys, :] += dot(grad_scores, q_own)
                 x[rows, ATT:] = att.astype(jnp.bfloat16)
                 x[rows, :LANES] = rope(dq * HD**-0.5, rows, -1.0).astype(jnp.bfloat16)
-                low, high = b * last // qblocks, (b + 1) * last // qblocks
-                ticks(gather_from + early + b * per_block, per_block, scatter_from + low, high - low)
+                there = at + early + b * per_block
+                ticks(there + lead, per_block, there - behind, per_block)
                 return carry
 
             lax.fori_loop(0, qblocks, queries, 0)
@@ -579,14 +622,15 @@
 
         cot_copy = pltpu.make_async_copy(cot_hbm, cot, save_sem)
         cot_copy.start()
-        per_step = 3 * last
-        in_hidden = 2 * per_step // 9
-        in_attention = per_step - 2 * in_hidden
-        lead = max(last, 2 * last - in_hidden)
-        norm_blocks = rows_all // stage.shape[0]
-        pack(0)
-        send_own(0)
-        pack(1)
+        fetch_rows(0).start()
+        fetch_raw(0, True)
+        fetch_raw(1, True)
+        for u in range(2):
+            pack(u)
+            put_packed(u).wait()
+            if u == 0:
+                send_own(0)
+            fetch_raw(u + 2, True)
 
         def begin_step(i, carry):
             @pl.when(i + 2 < units)
@@ -596,6 +640,14 @@
             @pl.when(i < norm_blocks)
             def _():
                 normalize(i)
+
+            @pl.when(i + 2 < units)
+            def _():
+                put_packed(i + 2).wait()
+
+            @pl.when(i + 4 < units)
+            def _():
+                fetch_raw(i + 4, True)
 
             @pl.when(i < lead)
             def _():
@@ -610,10 +662,10 @@
         vec[NIN : NIN + 1, :] = dot(jnp.ones((8, rows_all), jnp.bfloat16), cot[:, columns])[0:1, :]
 
         def super_step(s, carry):
-            base = s * per_step + lead
-            hidden_unit(3 * s, 2 * s, base, in_hidden)
-            attention_unit(3 * s + 1, s, base + in_hidden, in_attention)
-            hidden_unit(3 * s + 2, 2 * s + 1, base + in_hidden + in_attention, in_hidden)
+            at = s * per_step
+            hidden_unit(3 * s, 2 * s, at)
+            attention_unit(3 * s + 1, s, at + in_hidden)
+            hidden_unit(3 * s + 2, 2 * s + 1, at + in_hidden + in_attention)
             return carry
 
         lax.fori_loop(0, steps, super_step, 0)
@@ -627,13 +679,35 @@
             send_dkv(steps - 1).wait_send()
 
 
-    def tensor_copy(what, i, source):
+    square = peers == 4
+    upper, lower = pl.ds(0, rows_all // 2), pl.ds(rows_all // 2, rows_all // 2)
+
+    def beside(axis):
+        return tensor + 1 - 2 * (tensor % 2) if axis == 0 else tensor + 2 - 4 * (tensor // 2)
+
+    def block_at(i):
+        if not square:
+            return lax.rem(tensor + 1 + i, peers)
+        return jnp.where(
+            i == 0, 3 - tensor, jnp.where(i == 1, beside(0), jnp.where(i == 2, beside(1), tensor))
+        )
+
+    def tensor_copy(blocks, what, message):
+        if square:
+            slot, rows, axis = ((0, upper, 0), (0, lower, 1), (1, upper, 0), (2, lower, 1), (1, lower, 0), (2, upper, 1))[
+                message
+            ]
+            source, there = blocks.at[what, slot, rows], arrived.at[what, slot, rows]
+            target = beside(axis)
+        else:
+            source, there = blocks.at[what, message], arrived.at[what, message]
+            target = block_at(message)
         return pltpu.make_async_remote_copy(
             src_ref=source,
-            dst_ref=arrived.at[what, i],
-            send_sem=tsend_sem.at[what, i],
-            recv_sem=trecv_sem.at[what, i],
-            device_id={"tensor": lax.rem(tensor + 1 + i, peers)},
+            dst_ref=there,
+            send_sem=tsend_sem.at[what, message],
+            recv_sem=trecv_sem.at[what, message],
+            device_id={"tensor": target},
             device_id_type=MESH,
         )
 
@@ -647,18 +721,19 @@
             device_id_type=MESH,
         )
 
-    def finals(xs, tile, blocks, swap_in):
+    def finals(xs, tile, blocks, swap_in, passing):
         part = size // 2
         tiles = 2 * peers
 
         def fetch_tile(q):
-            shard = lax.rem(tensor + 1 + q // 2, peers)
+            shard = block_at(q // 2)
             rows = pl.ds(pl.multiple_of(q % 2 * part, part), part)
             return pltpu.make_async_copy(full.at[:, shard, rows], tile.at[q % 2], tile_sem.at[q % 2])
 
         fetch_xs = pltpu.make_async_copy(saved, xs.at[pl.ds(0, units)], load_sem)
         fetch_xs.start()
         fetch_tile(0).start()
+        fetch_swapped(units - 1, swap_in)
         fetch_xs.wait()
         block = min(512, rows_all)
 
@@ -684,35 +759,64 @@
 
             lax.fori_loop(0, rows_all // block, one, 0)
 
-        scatter_from = (units - 1) * last
-        scatter_count = last * (LAG + 1) + 1
+        scatter_from = units * last - behind
+        scatter_count = last * (LAG - 1) + 1 + behind
         remote = 2 * (peers - 1)
 
-        def remote_tile(q, carry):
-            i, h = q // 2, q % 2
-
-            def store(r, what, value):
-                rows = pl.ds(pl.multiple_of(r * block, block), block)
-                cols = pl.ds(pl.multiple_of(h * part, part), part)
-                blocks[what, i, rows, cols] = value.astype(jnp.bfloat16)
-
-            products(q, store)
-
-            @pl.when(h == 1)
-            def _():
-                tensor_copy(0, i, blocks.at[0, i]).start()
-
-            low, high = q * scatter_count // remote, (q + 1) * scatter_count // remote
-            run_ticks(swap_in, 0, 0, scatter_from + low, high - low)
-            return carry
-
-        lax.fori_loop(0, remote, remote_tile, 0)
-
-        def start_branch(i, carry):
-            tensor_copy(1, i, blocks.at[1, i]).start()
-            return carry
-
-        lax.fori_loop(0, peers - 1, start_branch, 0)
+        def remote_tile(i):
+            def one(h, carry):
+                def store(r, what, value):
+                    rows = pl.ds(pl.multiple_of(r * block, block), block)
+                    cols = pl.ds(pl.multiple_of(h * part, part), part)
+                    blocks[what, i, rows, cols] = value.astype(jnp.bfloat16)
+
+                q = 2 * i + h
+                products(q, store)
+                low, high = q * scatter_count // remote, (q + 1) * scatter_count // remote
+                run_ticks(swap_in, 0, 0, scatter_from + low, high - low)
+                return carry
+
+            lax.fori_loop(0, 2, one, 0)
+
+        def send(what, *messages):
+            for message in messages:
+                tensor_copy(blocks, what, message).start()
+
+        def add_half(what, slot, rows, message, onward):
+            tensor_copy(blocks, what, message).wait_recv()
+            copy = pltpu.make_async_copy(
+                arrived.at[what, 0, rows], passing, load_sem
+            )
+            copy.start()
+            copy.wait()
+            blocks[what, slot, rows, :] = (
+                blocks[what, slot, rows, :].astype(jnp.float32) + passing[...].astype(jnp.float32)
+            ).astype(jnp.bfloat16)
+            send(what, onward)
+
+        if square:
+            remote_tile(0)
+            send(0, 0, 1)
+            remote_tile(1)
+            send(0, 2)
+            remote_tile(2)
+            send(0, 3)
+            add_half(0, 1, lower, 1, 4)
+            add_half(0, 2, upper, 0, 5)
+            send(1, 0, 1, 2, 3)
+        else:
+
+            def one_block(i, carry):
+                remote_tile(i)
+                send(0, i)
+                return carry
+
+            def one_branch(i, carry):
+                send(1, i)
+                return carry
+
+            lax.fori_loop(0, peers - 1, one_block, 0)
+            lax.fori_loop(0, peers - 1, one_branch, 0)
 
         for h in range(2):
 
@@ -723,6 +827,10 @@
                     ]
 
             products(remote + h, store)
+
+        if square:
+            add_half(1, 1, lower, 1, 4)
+            add_half(1, 2, upper, 0, 5)
 
         tok_at, cot_at, out_at = 2 * (peers - 1), 2 * (peers - 1) + 1, 2 * (peers - 1) + 2
         bring = [
@@ -734,22 +842,29 @@
         for copy in bring:
             copy.wait()
 
+        first = 1 if square else 0
+        count = peers - 1 - first
+
         def collect(what):
+            for message in range(2, 6) if square else ():
+                tensor_copy(blocks, what, message).wait_recv()
+
             def one(i, carry):
-                tensor_copy(what, i, blocks.at[what, i]).wait_recv()
+                if not square:
+                    tensor_copy(blocks, what, i).wait_recv()
                 copy = pltpu.make_async_copy(
-                    arrived.at[what, i], xs.at[what * (peers - 1) + i, :, pl.ds(0, size)], load_sem
+                    arrived.at[what, first + i], xs.at[what * count + i, :, pl.ds(0, size)], load_sem
                 )
                 copy.start()
                 copy.wait()
                 return carry
 
-            lax.fori_loop(0, peers - 1, one, 0)
+            lax.fori_loop(0, count, one, 0)
 
         def summed(what, r, rows):
             value = held[what, r, :, :size]
-            for i in range(peers - 1):
-                value += xs[what * (peers - 1) + i, rows, :size].astype(jnp.float32)
+            for i in range(count):
+                value += xs[what * count + i, rows, :size].astype(jnp.float32)
             return value
 
         gain = vec_ref[NIN + 1 : NIN + 2, columns]
@@ -874,8 +989,9 @@
         for i in range(peers - 1):
             along_tensor(i).wait_send()
             sums_copy(i).wait_send()
-            tensor_copy(0, i, blocks.at[0, i]).wait_send()
-            tensor_copy(1, i, blocks.at[1, i]).wait_send()
+        for i in range(6 if square else peers - 1):
+            tensor_copy(blocks, 0, i).wait_send()
+            tensor_copy(blocks, 1, i).wait_send()
 
     low, wide = jnp.bfloat16, jnp.float32
     window, qblock = rows_all + min(256, rows_all), min(256, rows_all)
@@ -883,10 +999,10 @@
         forward_backward,
         pltpu.VMEM((rows_all, width), low),
         pltpu.VMEM((rows_all, width), low),
-        pltpu.VMEM((rows_all // 4, width), low),
-        pltpu.VMEM((size, ATT), wide),
-        pltpu.VMEM((HID, size), wide),
-        pltpu.VMEM((size, WIDE), low),
+        pltpu.VMEM((2, rows_all // 8, width), low),
+        pltpu.VMEM((2, size, ATT), wide),
+        pltpu.VMEM((2, HID, size), wide),
+        pltpu.VMEM((2, size, WIDE), low),
         pltpu.VMEM((n, size, WIDE), low),
         pltpu.VMEM((rows_all, WIDE), low),
         pltpu.VMEM((rows_all, LANES), low),
@@ -903,6 +1019,7 @@
         pltpu.VMEM((2, units, size // 2, WIDE), low),
         pltpu.VMEM((2, peers - 1, rows_all, size), low),
         pltpu.VMEM((n, half, WIDE), low),
+        pltpu.VMEM((rows_all // 2, size), low),
     )
 
 
@@ -925,7 +1042,7 @@
             def _():
                 hop(1, g, 0, z).wait_send()
 
-            @pl.when(g >= units - (LAG + 3))
+            @pl.when(g >= units - (LAG + 2))
             def _():
                 keep(g).wait()
                 share(g, mine).wait_send()
@@ -989,9 +1106,9 @@
         out_specs=[anywhere] * 8 + [vm],
         scratch_shapes=[
             pltpu.VMEM((steps, 2, 2 * rows, LANES), low),
-            pltpu.VMEM((3, n, half, WIDE), wide),
+            pltpu.VMEM((schedule(n)[-1], n, half, WIDE), wide),
             pltpu.VMEM((units, n + 1, half, WIDE), low),
-            pltpu.VMEM((LAG + 3, half, WIDE), wide),
+            pltpu.VMEM((LAG + 2, half, WIDE), wide),
             pltpu.VMEM((rows, LANES), wide),
             pltpu.VMEM((16, size), wide),
             pltpu.VMEM((16, size), wide),
@@ -1017,9 +1134,12 @@
             dma,
             dma,
             dma,
-            dma((4,)),
-            dma((2, peers - 1)),
-            dma((2, peers - 1)),
+            dma((2, 4)),
+            dma((2,)),
+            dma((2,)),
+            dma,
+            dma((2, 6 if peers == 4 else peers - 1)),
+            dma((2, 6 if peers == 4 else peers - 1)),
             dma((peers - 1,)),
             dma((peers - 1,)),
             dma((n + peers - 1,)),
@@ -1034,35 +1154,59 @@
     )(in_weight, out_weight, tokens, cotangent, bias, vectors, cosine, sine, begin)
 
 
-def adam_kernel(turned, total, w, m, v, new_w, new_m, new_v):
-    gradient = total[0].T if turned else total[0]
-    new_w[0], new_m[0], new_v[0] = adamw(w[0], gradient, m[0], v[0], rate_matrix, weight_decay)
-
-
-def adam_weights(turned, total, weight, first, second):
-    groups, cols_all = weight.shape[0], weight.shape[1 if turned else 2]
-    size = total.shape[1]
-    lead = 1 if turned else 3
-
-    def place(g, c):
-        i = ((g - lead) * cols_all + c * LANES) // HID
-        unit = jnp.where(g < lead, 3 * c + 1, 3 * (i // 2) + 2 * (i % 2))
-        lane = jnp.where(g < lead, 3 if turned else g, c % 2 + (2 if turned else 0))
+def adam_kernel(into, chunks, *refs):
+    pieces, refs = refs[:chunks], refs[chunks:]
+    g = pl.program_id(0)
+
+    def update(weights, turned):
+        w, m, v, new_w, new_m, new_v = weights
+        for c, piece in enumerate(pieces):
+            part = slice(c * LANES, (c + 1) * LANES)
+            at = (0, part) if turned else (0, slice(None), part)
+            gradient = piece[0].T if turned else piece[0]
+            new_w[at], new_m[at], new_v[at] = adamw(
+                w[at], gradient, m[at], v[at], rate_matrix, weight_decay
+            )
+
+    @pl.when(g < into)
+    def _():
+        update(refs[:3] + refs[6:9], False)
+
+    @pl.when(g >= into)
+    def _():
+        update(refs[3:6] + refs[9:], True)
+
+
+def adam_weights(total, in_arrays, out_arrays):
+    into, size, cols_all = in_arrays[0].shape
+    outof = out_arrays[0].shape[0]
+    chunks = cols_all // LANES
+
+    def place(c, g):
+        is_in = g < into
+        group = jnp.where(is_in, g, g - into)
+        lead = jnp.where(is_in, 3, 1)
+        i = jnp.maximum((group - lead) * cols_all + c * LANES, 0) // HID
+        unit = jnp.where(group < lead, 3 * c + 1, 3 * (i // 2) + 2 * (i % 2))
+        lane = jnp.where(
+            group < lead, jnp.where(is_in, group, 3), c % 2 + jnp.where(is_in, 0, 2)
+        )
         return unit, 0, lane
 
-    if turned:
-        spec = pl.BlockSpec((1, LANES, size), lambda g, c: (g, c, 0))
-    else:
-        spec = pl.BlockSpec((1, size, LANES), lambda g, c: (g, 0, c))
-    return pl.pallas_call(
-        functools.partial(adam_kernel, turned),
-        grid=(groups, cols_all // LANES),
-        out_shape=tuple(jax.ShapeDtypeStruct(weight.shape, jnp.float32) for _ in range(3)),
-        in_specs=[pl.BlockSpec((1, size, LANES), place)] + [spec] * 3,
-        out_specs=[spec] * 3,
+    in_spec = pl.BlockSpec((1, size, cols_all), lambda g: (jnp.minimum(g, into - 1), 0, 0))
+    out_spec = pl.BlockSpec((1, cols_all, size), lambda g: (jnp.maximum(g - into, 0), 0, 0))
+    results = pl.pallas_call(
+        functools.partial(adam_kernel, into, chunks),
+        grid=(into + outof,),
+        out_shape=tuple(jax.ShapeDtypeStruct(v.shape, jnp.float32) for v in in_arrays + out_arrays),
+        in_specs=[pl.BlockSpec((1, size, LANES), functools.partial(place, c)) for c in range(chunks)]
+        + [in_spec] * 3
+        + [out_spec] * 3,
+        out_specs=[in_spec] * 3 + [out_spec] * 3,
         compiler_params=pltpu.CompilerParams(vmem_limit_bytes=VMEM_LIMIT),
-        name="adam_out" if turned else "adam_in",
-    )(total, weight, first, second)
+        name="adam_weights",
+    )(*[total] * chunks, *in_arrays, *out_arrays)
+    return results[:3], results[3:]
 
 
 def layout(lengths_row, row_span):
@@ -1134,15 +1278,11 @@
     new_vectors, new_vec_first, new_vec_second = adamw(
         vectors, vector_grad, vec_first, vec_second, rate_vector, 0.0
     )
-    new_in, new_in_first, new_in_second = (
-        jnp.transpose(v, (1, 0, 2))
-        for v in adam_weights(
-            False, total, by_group, jnp.transpose(in_first, (1, 0, 2)), jnp.transpose(in_second, (1, 0, 2))
-        )
+    by_group_moments = [jnp.transpose(v, (1, 0, 2)) for v in (in_first, in_second)]
+    new_by_group, (new_out, new_out_first, new_out_second) = adam_weights(
+        total, [by_group] + by_group_moments, [out_weight, out_first, out_second]
     )
-    new_out, new_out_first, new_out_second = adam_weights(
-        True, total, out_weight, out_first, out_second
-    )
+    new_in, new_in_first, new_in_second = (jnp.transpose(v, (1, 0, 2)) for v in new_by_group)
     return (
         result,
         token_grad,

time: 559 us -> 453 us (0.81)
  Pallas kernels: 544 us -> 440 us
    pallas_call x1, Pallas kernels: 495 us -> 407 us  [run_block(): pl.pallas_call(functools.partial(block_kernel, n, steps, peers), out_shap...]
    pallas_call x2 -> x1, Pallas kernels: 49.7 us -> 33.1 us  [adam_weights(): pl.pallas_call(functools.partial(adam_kernel, into, chunks), grid=(into +...]
where the time goes in v3:
time: 453 us; the launch traced here: 452 us
  Pallas kernels  440 us (97%)
  other arithmetic  6.16 us (1%)
  local copies, waits for them, and re-layouts  4.96 us (1%)
    pallas_call x1, Pallas kernels, run_block(): pl.pallas_call(functools.partial(block_kernel, n, steps, peers), out_shap...  407 us
    pallas_call x1, Pallas kernels, adam_weights(): pl.pallas_call(functools.partial(adam_kernel, into, chunks), grid=(into +...  33.1 us

profile of v3, /device:TPU:0, one launch (start us, length us, event | category | flops | bytes accessed | tf_op | source)
XLA Modules:
  0.0 452.2 jit_solution(11563508837734745155)
XLA Ops:
  0.6 0.8 reduce-window.4
  1.5 0.7 fusion.7
  2.2 0.1 convert_reduce_fusion
  2.3 0.1 select_reduce_fusion
  2.3 0.6 subtract_convert_fusion
  2.9 0.8 slice.21
  3.8 0.1 dynamic-slice
  4.0 0.6 reshape.84.bias_ref
  4.7 3.0 fusion.1
  7.7 0.0 copy-start.3
  7.7 0.0 copy-start.4
  7.7 407.2 %parallel_block.1 = (bf16[12,4,512,512]{3,2,1,0:T(8,128)(2,1)}, bf16[12,1024,512]{2,1,0:T(8,128)(2,1)}, f32[12,512,512]{2,1,0:T(8,128)}, bf16[12,4,256,512]{3,2,...) custom-call(f32[7,512,512]{2,1,0:T(8,128)} %bitcast.29, ...), custom_call_target="tpu_custom_call" | custom-call | tf_op jit(solution)/shard_map/parallel_block/pallas_call | solution.py:1092
  414.9 1.0 copy.32
  416.0 0.0 copy-done.2
  416.0 0.0 copy-done.3
  416.0 0.0 copy-done.4
  416.0 0.8 multiply_subtract_fusion
  416.8 0.0 copy-start.1
  416.8 0.0 copy-start
  416.8 33.1 %adam_weights.1 = (f32[7,512,512]{2,1,0:T(8,128)}, f32[7,512,512]{2,1,0:T(8,128)}, f32[7,512,512]{2,1,0:T(8,128)}, f32[5,512,512]{2,1,0:T(8,128)}, f32[5,512,512]{2,1,0:T(8,128)}, /*index=5*/f32[5,512,512]{2,1,0:T(8,128)}) custom-call(f32[12,512,512]{2,1,0:T(8,128)} %get-tuple-element.23.refs_0_.refs_1_.refs_2_.refs_3_, ...), custom_call_target="tpu_custom_call" | custom-call | tf_op jit(solution)/shard_map/adam_weights/pallas_call | solution.py:1198
  449.9 0.0 copy-done.1
  449.9 1.0 copy.36
  450.9 0.0 copy-done
  450.9 1.3 copy.37
  (15 shorter events, 0.2 us)
Async XLA Ops:
  7.7 408.3 %copy-start.2 = (f32[10,2048]{1,0:T(8,128)S(1)}, f32[10,2048]{1,0:T(8,128)}, u32[]{:S(2)}) copy-start(f32[10,2048]{1,0:T(8,128)} %vec_ref.1) | copy-start | bytes 245764
  7.7 408.3 %copy-start.3 = (f32[10,2048]{1,0:T(8,128)S(1)}, f32[10,2048]{1,0:T(8,128)}, u32[]{:S(2)}) copy-start(f32[10,2048]{1,0:T(8,128)} %param.22) | copy-start | bytes 245764
  7.7 408.3 %copy-start.4 = (f32[10,2048]{1,0:T(8,128)S(1)}, f32[10,2048]{1,0:T(8,128)}, u32[]{:S(2)}) copy-start(f32[10,2048]{1,0:T(8,128)} %param.23) | copy-start | bytes 245764
  416.8 33.1 %copy-start.1 = (bf16[1024,512]{1,0:T(8,128)(2,1)S(1)}, bf16[1024,512]{1,0:T(8,128)(2,1)}, u32[]{:S(2)}) copy-start(bf16[1024,512]{1,0:T(8,128)(2,1)} %get-tuple-element.51) | copy-start | bytes 3145732
  416.8 34.1 %copy-start = (f32[4,256,512]{2,1,0:T(8,128)S(1)}, f32[4,256,512]{2,1,0:T(8,128)}, u32[]{:S(2)}) copy-start(f32[4,256,512]{2,1,0:T(8,128)} %get-tuple-element.22) | copy-start | bytes 6291460

commit v4 on v3

--- a/solution.py
+++ b/solution.py
@@ -38,7 +38,7 @@
 WIDE = 4 * LANES
 HID = WIDE // 2
 ATT = 3 * LANES
-LAG = 3
+LAG = 8
 
 NT = (((1,), (1,)), ((), ()))
 NN = (((1,), (0,)), ((), ()))
@@ -79,26 +79,25 @@
     in_attention = per_step - 2 * in_hidden
     done = (in_hidden, in_hidden + in_attention, per_step)
     lead = max([last * (n + i) - done[i] for i in range(3)] + [last * (n - 1)])
-    behind = max(done[i] - last * i for i in range(3))
-    depth = 3
-    while any(done[i] - behind < last * (i - depth) + LAG * (n - 2) + 1 for i in range(3)):
-        depth += 1
-    return per_step, in_hidden, in_attention, lead, behind, depth
+    out_hidden, out_attention = in_hidden // 2, in_attention
+    behind = max(out_hidden + last, out_hidden + out_attention, 2 * out_hidden + out_attention - last)
+    return per_step, in_hidden, in_attention, lead, out_hidden, out_attention, behind
 
 
 def block_kernel(
     n, steps, peers,
     in_w, out_w, tokens, cot_hbm, bias_ref, vec_ref, cos_ref, sin_ref, begin_ref,
-    full, saved, total, swap, dkv_other, arrived, result, token_grad, vec_grad,
-    kv, held, line, outbox, stats, vec, vec_core, vec_line, vec_all, sums, sums_in,
+    full, saved, total, swap, kept, dkv_other, arrived, result, token_grad, vec_grad,
+    kv, moved, returned, extra, held, pieces, line, outbox, stats, vec, vec_core, vec_line, vec_all, sums, sums_in,
     send_sem, recv_sem, psend_sem, precv_sem,
     xsend_sem, xrecv_sem, lsend_sem, lrecv_sem, keep_sem, fsend_sem, frecv_sem,
-    kvsend_sem, kvrecv_sem, dsend_sem, drecv_sem, load_sem, save_sem, weight_sem, pack_sem, put_sem, rows_sem, swap_sem,
+    kvsend_sem, kvrecv_sem, dsend_sem, drecv_sem, msend_sem, mrecv_sem, bsend_sem, brecv_sem, esend_sem, erecv_sem, load_sem, save_sem, weight_sem, pack_sem, put_sem, rows_sem, swap_sem, held_sem, piece_sem, box_sem,
     tsend_sem, trecv_sem, ssend_sem, srecv_sem, vsend_sem, vrecv_sem, tile_sem, out_sem,
 ):
     units = 3 * steps
     last = n - 1
-    per_step, in_hidden, in_attention, lead, behind, depth = schedule(n)
+    per_step, in_hidden, in_attention, lead, out_hidden, out_attention, behind = schedule(n)
+    depth, boxes = 2, 3
     size, cols_all = in_w.shape[1], in_w.shape[2]
     half = size // 2
     rows_all, width = tokens.shape
@@ -223,12 +222,15 @@
             device_id_type=MESH,
         )
 
+    my_part = pl.ds(pl.multiple_of(k * HID, HID), HID)
+    their_part = pl.ds(pl.multiple_of((1 - k) * HID, HID), HID)
+
     def keep(g):
-        return pltpu.make_async_copy(outbox.at[g % (LAG + 2)], total.at[g, mine], keep_sem.at[g])
+        return pltpu.make_async_copy(outbox.at[g % boxes], total.at[g, my_part], keep_sem.at[g])
 
     def share(g, rows):
         return pltpu.make_async_remote_copy(
-            src_ref=outbox.at[g % (LAG + 2)],
+            src_ref=outbox.at[g % boxes],
             dst_ref=total.at[g, rows],
             send_sem=fsend_sem.at[g],
             recv_sem=frecv_sem.at[g],
@@ -242,47 +244,89 @@
             exchange_from(swap_in, g).wait_recv()
             pltpu.make_async_copy(swap.at[g], swap_in, swap_sem).start()
 
+    def put_held(g):
+        return pltpu.make_async_copy(held.at[g % depth], kept.at[g], held_sem.at[g % depth])
+
     def prepare(g, swap_in):
-        pltpu.make_async_copy(swap.at[g], swap_in, swap_sem).wait()
-        box = g % (LAG + 2)
-
-        @pl.when(g >= LAG + 2)
-        def _():
-            keep(g - (LAG + 2)).wait()
-            share(g - (LAG + 2), mine).wait_send()
-
-        def one(j, carry):
-            held[g % depth, j] += swap_in[j].astype(jnp.float32)
-            return carry
-
-        lax.fori_loop(0, n, one, 0)
-        outbox[box] = held[g % depth, z]
-
-    def scatter_step(way, m, distance):
-        @pl.when((m >= 0) & (m < units * last))
-        def _():
-            g, i = m // last, m % last
-            shard = n - 1 - i if way == 0 else i
-            slot = slot_of(way, i)
-
+        @pl.when(g >= 0)
+        def _():
+            pltpu.make_async_copy(swap.at[g], swap_in, swap_sem).wait()
+
+            def one(j, carry):
+                held[g % depth, j] += swap_in[j].astype(jnp.float32)
+                return carry
+
+            lax.fori_loop(0, n, one, 0)
+            put_held(g).start()
+
+    def wait_put(g):
+        @pl.when(g >= 0)
+        def _():
+            put_held(g).wait()
+
+    def piece_copy(way, g, i, slot):
+        shard = n - 1 - i if way == 0 else i
+        return pltpu.make_async_copy(kept.at[g, shard], pieces.at[way, slot], piece_sem.at[way, slot])
+
+    def box_copy(g):
+        return pltpu.make_async_copy(kept.at[g, z], outbox.at[g % boxes], box_sem.at[g % boxes])
+
+    def needs(way, t):
+        distance = z if way == 0 else last - z
+        m = t - LAG * distance
+        g, i = m // last, m % last
+        return g, i, (m >= 0) & (m < units * last) & (distance < last - i)
+
+    def fetch_pieces(t):
+        for way in range(2):
+            g, i, needed = needs(way, t)
+
+            @pl.when(needed)
+            def _():
+                piece_copy(way, g, i, t % 2).start()
+
+        done = t - last * LAG
+
+        @pl.when((done >= 0) & (done % last == 0))
+        def _():
+            g = done // last
+
+            @pl.when(g >= boxes)
+            def _():
+                keep(g - boxes).wait()
+                share(g - boxes, my_part).wait_send()
+
+            box_copy(g).start()
+
+    def scatter_step(way, t):
+        distance = z if way == 0 else last - z
+        m = t - LAG * distance
+        g, i, needed = needs(way, t)
+        slot = slot_of(way, i)
+
+        @pl.when(needed)
+        def _():
+            piece_copy(way, g, i, t % 2).wait()
+
+        @pl.when((m >= 0) & (m < units * last) & (distance > 0) & (distance <= last - i))
+        def _():
+            pass_on(way, g, i).wait_recv()
+
+        @pl.when(needed)
+        def _():
             @pl.when(distance == 0)
             def _():
-                line[g, slot] = held[g % depth, shard].astype(jnp.bfloat16)
-                pass_on(way, g, i).start()
-
-            @pl.when((distance > 0) & (distance <= last - i))
-            def _():
-                pass_on(way, g, i).wait_recv()
-
-                @pl.when(distance < last - i)
-                def _():
-                    line[g, slot] = (line[g, slot].astype(jnp.float32) + held[g % depth, shard]).astype(
-                        jnp.bfloat16
-                    )
-                    pass_on(way, g, i).start()
+                line[g, slot] = pieces[way, t % 2].astype(jnp.bfloat16)
+
+            @pl.when(distance > 0)
+            def _():
+                line[g, slot] = (line[g, slot].astype(jnp.float32) + pieces[way, t % 2]).astype(jnp.bfloat16)
+
+            pass_on(way, g, i).start()
 
     def finish(g):
-        box = g % (LAG + 2)
+        box = g % boxes
+        box_copy(g).wait()
 
         @pl.when(z > 0)
         def _():
@@ -293,42 +337,45 @@
             outbox[box] += line[g, slot_of(1, z)].astype(jnp.float32)
 
         keep(g).start()
-        share(g, mine).start()
-
-    def scatter_tick(t, swap_in):
-        @pl.when((t >= 0) & (t % last == 0) & (t < units * last))
-        def _():
-            prepare(t // last, swap_in)
-
-        scatter_step(0, t - LAG * z, z)
-        scatter_step(1, t - LAG * (last - z), last - z)
+        share(g, my_part).start()
+
+    def scatter_tick(t):
+        scatter_step(0, t)
+        scatter_step(1, t)
         done = t - last * LAG
 
         @pl.when((done >= 0) & (done % last == 0))
         def _():
             finish(done // last)
 
-    def run_ticks(swap_in, gather_from, gather_count, scatter_from, scatter_count):
+    def run_ticks(gather_from, gather_count, scatter_from, scatter_count):
         def one_gather(i, carry):
             gather_tick(gather_from + i)
             return carry
 
         def one_scatter(i, carry):
-            scatter_tick(scatter_from + i, swap_in)
+            @pl.when(i + 1 < scatter_count)
+            def _():
+                fetch_pieces(scatter_from + i + 1)
+
+            scatter_tick(scatter_from + i)
             return carry
 
+        if not isinstance(scatter_count, int):
+            pl.when(scatter_count > 0)(lambda: fetch_pieces(scatter_from))
+        elif scatter_count:
+            fetch_pieces(scatter_from)
         lax.fori_loop(0, gather_count, one_gather, 0)
         lax.fori_loop(0, scatter_count, one_scatter, 0)
 
     def forward_backward(
-        normed, cot, stage, raw_in, raw_out, packed, wbuf, x, q_s, g_s, dkv, dkv_tmp, mask, outgoing, swap_in
+        normed, cot, stage, raw_in, raw_out, packed, wbuf, x, qg, dkv, back, dkv_tmp, mask, outgoing, swap_in
     ):
 
         def exchange(g):
             return exchange_from(outgoing.at[g % 2], g)
 
-        def ticks(gather_from, gather_count, scatter_from, scatter_count):
-            run_ticks(swap_in, gather_from, gather_count, scatter_from, scatter_count)
+        ticks = run_ticks
 
         part = stage.shape[1]
         norm_blocks = rows_all // part
@@ -448,27 +495,47 @@
             def _():
                 exchange(u - 2).wait_send()
 
-            def one(j, carry):
-                for core, place in ((k, None), (1 - k, outgoing)):
-                    cols = pl.ds(pl.multiple_of(j * size + core * half, half), half)
-                    into = dot(normed[:, cols], x[:, :split], TN)
-                    outof = dot(cot[:, cols], x[:, split:], TN)
-                    if place is None:
-                        held[u % depth, j, :, :split] = into
-                        held[u % depth, j, :, split:] = outof
-                    else:
-                        place[u % 2, j, :, :split] = into.astype(jnp.bfloat16)
-                        place[u % 2, j, :, split:] = outof.astype(jnp.bfloat16)
+            def part(first, end, j):
+                turns = [(first, min(end, split), normed), (max(first, split), end, cot)]
+                return [
+                    (low, high, dot(x[:, low:high], rows[:, pl.ds(pl.multiple_of(j * size, size), size)], TN))
+                    for low, high, rows in turns
+                    if low < high
+                ]
+
+            for core in range(2):
+
+                @pl.when(k == core)
+                def _():
+                    def one(j, carry):
+                        for low, high, value in part(core * HID, (core + 1) * HID, j):
+                            held[u % depth, j, low - core * HID : high - core * HID] = value
+                        for low, high, value in part((1 - core) * HID, (2 - core) * HID, j):
+                            outgoing[u % 2, j, low - (1 - core) * HID : high - (1 - core) * HID] = value.astype(
+                                jnp.bfloat16
+                            )
+                        return carry
+
+                    lax.fori_loop(0, n, one, 0)
+
+            exchange(u).start()
+
+        block = min(512, rows_all)
+
+        def other_first_ticks():
+            def one(m, carry):
+                @pl.when((m // last != m % last) & (m != last))
+                def _():
+                    gather_tick(m)
+
                 return carry
 
-            lax.fori_loop(0, n, one, 0)
-            exchange(u).start()
-
-        block = min(512, rows_all)
-
-        def hidden_unit(u, i_hidden, at):
+            lax.fori_loop(0, lead, one, 0)
+
+        def hidden_unit(u, i_hidden, at, out_at, opens):
             fetch_weights(u).wait()
             wait_saved(u)
+            wait_put(u - 2)
 
             def one(i, carry):
                 rows = pl.ds(pl.multiple_of(i * block, block), block)
@@ -482,11 +549,27 @@
             lax.fori_loop(0, rows_all // block, one, 0)
             save(u).start()
             fetch_swapped(u - 1, swap_in)
-            ticks(at + lead, in_hidden, at - behind, in_hidden)
-            next_weights(u + 1)
+
+            def gather():
+                ticks(at + lead, in_hidden, 0, 0)
+                next_weights(u + 1)
+
+            if opens:
+                pl.when(u > 0)(gather)
+            else:
+                gather()
+            ticks(0, 0, out_at - behind, out_hidden)
+            prepare(u - 1, swap_in)
             group, first = hidden_place(i_hidden)
             vec[pl.ds(3 + group, 1), pl.ds(first, HID)] = column_sums(HID)
             gradients(u, HID)
+            if opens:
+
+                @pl.when(u == 0)
+                def _():
+                    other_first_ticks()
+                    gather()
+
 
         qblock = mask.shape[1]
         window = mask.shape[0]
@@ -521,73 +604,165 @@
                 device_id_type=MESH,
             )
 
-        def attention_unit(u, s, at):
+        def send_first(s):
+            return pltpu.make_async_remote_copy(
+                src_ref=qg.at[:, pl.ds(0, qblock)],
+                dst_ref=moved.at[s],
+                send_sem=msend_sem.at[s],
+                recv_sem=mrecv_sem.at[s],
+                device_id=other_core,
+                device_id_type=MESH,
+            )
+
+        def send_back(s):
+            return pltpu.make_async_remote_copy(
+                src_ref=back,
+                dst_ref=returned.at[s],
+                send_sem=bsend_sem.at[s],
+                recv_sem=brecv_sem.at[s],
+                device_id=other_core,
+                device_id_type=MESH,
+            )
+
+        def send_extra(s):
+            return pltpu.make_async_remote_copy(
+                src_ref=dkv.at[:, pl.ds(rows_all, qblock)],
+                dst_ref=extra.at[s],
+                send_sem=esend_sem.at[s],
+                recv_sem=erecv_sem.at[s],
+                device_id=other_core,
+                device_id_type=MESH,
+            )
+
+        def sent(s):
+            @pl.when(k == 1)
+            def _():
+                send_dkv(s).wait_send()
+                send_first(s).wait_send()
+
+            @pl.when(k == 0)
+            def _():
+                send_back(s).wait_send()
+                send_extra(s).wait_send()
+
+        def attend(s, q_low, g_low, first_query, first_key, span):
+            keys = pl.ds(first_key, span)
+            key_at = first_key + lax.broadcasted_iota(jnp.int32, (span, qblock), 0)
+            query_at = first_query + lax.broadcasted_iota(jnp.int32, (span, qblock), 1)
+            begin = begin_ref[0:1, pl.ds(pl.multiple_of(first_query, qblock), qblock)]
+            mask[:span] = jnp.where((key_at >= begin) & (key_at <= query_at), 0.0, -1e30)
+            lane = lax.broadcasted_iota(jnp.int32, (qblock, LANES), 1)
+            att = jnp.zeros((qblock, LANES), jnp.float32)
+            dq = jnp.zeros((qblock, LANES), jnp.float32)
+            for head in range(2):
+                inside = (lane >= head * HD) & (lane < (head + 1) * HD)
+                q_own = jnp.where(inside, q_low, jnp.zeros((qblock, LANES), jnp.bfloat16))
+                g_own = jnp.where(inside, g_low, jnp.zeros((qblock, LANES), jnp.bfloat16))
+                scores = dot(kv[s, 0, keys, :], q_own, NT) + mask[:span]
+                weights = jnp.exp(scores - jnp.max(scores, 0, keepdims=True))
+                probs = weights * (1.0 / jnp.sum(weights, 0, keepdims=True))
+                probs_low = probs.astype(jnp.bfloat16)
+                grad_probs = dot(kv[s, 1, keys, :], g_own, NT)
+                inner = jnp.sum(probs * grad_probs, 0, keepdims=True)
+                grad_scores = (probs * (grad_probs - inner)).astype(jnp.bfloat16)
+                att = jnp.where(inside, dot(probs_low, kv[s, 1, keys, :], TN), att)
+                dq = jnp.where(inside, dot(grad_scores, kv[s, 0, keys, :], TN), dq)
+                dkv[1, keys, :] += dot(probs_low, g_own)
+                dkv[0, keys, :] += dot(grad_scores, q_own)
+            return att, dq * HD**-0.5
+
+        def attend_own(s, b, first_key, span):
+            rows = pl.ds(pl.multiple_of(b * qblock, qblock), qblock)
+            att, dq = attend(s, qg[0, rows, :], qg[1, rows, :], k * rows_all + b * qblock, first_key, span)
+            x[rows, ATT:] = att.astype(jnp.bfloat16)
+            x[rows, :LANES] = rope(dq, rows, -1.0).astype(jnp.bfloat16)
+
+        def attention_unit(u, s, at, out_at):
             fetch_weights(u).wait()
             wait_saved(u)
-
-            @pl.when((s > 0) & (k == 1))
-            def _():
-                send_dkv(s - 1).wait_send()
+            wait_put(u - 2)
+
+            @pl.when(s > 0)
+            def _():
+                sent(s - 1)
 
             def project(i, carry):
                 rows = pl.ds(pl.multiple_of(i * block, block), block)
                 there = pl.ds(pl.multiple_of(k * rows_all + i * block, block), block)
                 pre = dot(normed[rows, :], wbuf[:, :, :ATT].reshape(width, ATT)) + bias_ref[u][:, :ATT]
-                grad = dot(cot[rows, :], wbuf[:, :, ATT:].reshape(width, LANES))
-                g_s[rows, :] = grad.astype(jnp.bfloat16)
                 query = rope(pre[:, :LANES], rows, 1.0).astype(jnp.bfloat16)
-                q_s[rows, :] = query * jnp.bfloat16(HD**-0.5)
+                qg[0, rows, :] = query * jnp.bfloat16(HD**-0.5)
                 kv[s, 0, there, :] = rope(pre[:, LANES : 2 * LANES], rows, 1.0).astype(jnp.bfloat16)
                 kv[s, 1, there, :] = pre[:, 2 * LANES :].astype(jnp.bfloat16)
                 return carry
 
             lax.fori_loop(0, rows_all // block, project, 0)
             send_kv(s).start()
+
+            def project_grad(i, carry):
+                rows = pl.ds(pl.multiple_of(i * block, block), block)
+                grad = dot(cot[rows, :], wbuf[:, :, ATT:].reshape(width, LANES))
+                qg[1, rows, :] = grad.astype(jnp.bfloat16)
+                return carry
+
+            lax.fori_loop(0, rows_all // block, project_grad, 0)
+
+            @pl.when(k == 1)
+            def _():
+                send_first(s).start()
+
             dkv[...] = jnp.zeros_like(dkv)
             per_block = in_attention // qblocks
             early = in_attention - per_block * qblocks
+            out_block = out_attention // qblocks
+            out_early = out_attention - out_block * qblocks
             fetch_swapped(u - 1, swap_in)
-            ticks(at + lead, early, at - behind, early)
+            ticks(at + lead, early, out_at - behind, out_early)
+            prepare(u - 1, swap_in)
             recv_kv(s).wait_recv()
 
-            def queries(b, carry):
-                first_query = k * rows_all + b * qblock
-                first_key = pl.multiple_of(jnp.maximum(first_query + qblock - window, 0), qblock)
-                rows = pl.ds(pl.multiple_of(b * qblock, qblock), qblock)
-                keys = pl.ds(first_key, window)
-                key_at = first_key + lax.broadcasted_iota(jnp.int32, (window, qblock), 0)
-                query_at = first_query + lax.broadcasted_iota(jnp.int32, (window, qblock), 1)
-                begin = begin_ref[0:1, rows]
-                mask[...] = jnp.where((key_at >= begin) & (key_at <= query_at), 0.0, -1e30)
-                lane = lax.broadcasted_iota(jnp.int32, (qblock, LANES), 1)
-                att = jnp.zeros((qblock, LANES), jnp.float32)
-                dq = jnp.zeros((qblock, LANES), jnp.float32)
-                for head in range(2):
-                    inside = (lane >= head * HD) & (lane < (head + 1) * HD)
-                    q_own = jnp.where(inside, q_s[rows, :], jnp.zeros((qblock, LANES), jnp.bfloat16))
-                    g_own = jnp.where(inside, g_s[rows, :], jnp.zeros((qblock, LANES), jnp.bfloat16))
-                    scores = dot(kv[s, 0, keys, :], q_own, NT) + mask[...]
-                    weights = jnp.exp(scores - jnp.max(scores, 0, keepdims=True))
-                    probs = weights * (1.0 / jnp.sum(weights, 0, keepdims=True))
-                    probs_low = probs.astype(jnp.bfloat16)
-                    grad_probs = dot(kv[s, 1, keys, :], g_own, NT)
-                    inner = jnp.sum(probs * grad_probs, 0, keepdims=True)
-                    grad_scores = (probs * (grad_probs - inner)).astype(jnp.bfloat16)
-                    att = jnp.where(inside, dot(probs_low, kv[s, 1, keys, :], TN), att)
-                    dq = jnp.where(inside, dot(grad_scores, kv[s, 0, keys, :], TN), dq)
-                    dkv[1, keys, :] += dot(probs_low, g_own)
-                    dkv[0, keys, :] += dot(grad_scores, q_own)
-                x[rows, ATT:] = att.astype(jnp.bfloat16)
-                x[rows, :LANES] = rope(dq * HD**-0.5, rows, -1.0).astype(jnp.bfloat16)
-                there = at + early + b * per_block
-                ticks(there + lead, per_block, there - behind, per_block)
+            def turn_of(b, carry):
+                @pl.when((k == 1) & (b < qblocks - 1))
+                def _():
+                    first_key = pl.multiple_of(rows_all + (b + 2) * qblock - window, qblock)
+                    attend_own(s, b + 1, first_key, window)
+
+                @pl.when((k == 1) & (b == qblocks - 2))
+                def _():
+                    send_dkv(s).start()
+
+                for own in range(qblocks):
+
+                    @pl.when((k == 0) & (b == (own if own > 1 else 0)))
+                    def _():
+                        attend_own(s, own, 0, (own + 1) * qblock)
+
+                @pl.when((k == 0) & (b == 1))
+                def _():
+                    send_first(s).wait_recv()
+                    att, dq = attend(s, moved[s, 0], moved[s, 1], rows_all, 0, window)
+                    back[0], back[1] = att, dq
+                    send_back(s).start()
+                    send_extra(s).start()
+
+                ticks(
+                    at + early + b * per_block + lead,
+                    per_block,
+                    out_at + out_early + b * out_block - behind,
+                    out_block,
+                )
                 return carry
 
-            lax.fori_loop(0, qblocks, queries, 0)
+            lax.fori_loop(0, qblocks, turn_of, 0)
+            first_rows, own_rows = pl.ds(0, qblock), pl.ds(0, rows_all)
 
             @pl.when(k == 1)
             def _():
-                send_dkv(s).start()
+                send_back(s).wait_recv()
+                send_extra(s).wait_recv()
+                x[first_rows, ATT:] = returned[s, 0].astype(jnp.bfloat16)
+                x[first_rows, :LANES] = rope(returned[s, 1], first_rows, -1.0).astype(jnp.bfloat16)
+                dkv[:, pl.ds(rows_all, qblock)] += extra[s]
 
             @pl.when(k == 0)
             def _():
@@ -595,18 +770,13 @@
                 copy = pltpu.make_async_copy(dkv_other.at[s], dkv_tmp, load_sem)
                 copy.start()
                 copy.wait()
-
-            @pl.when(k == 1)
-            def _():
-                dkv_tmp[...] = jnp.zeros_like(dkv_tmp)
+                dkv[:, own_rows] += dkv_tmp[...]
 
             def turn(i, carry):
                 rows = pl.ds(pl.multiple_of(i * qblock, qblock), qblock)
                 there = pl.ds(pl.multiple_of(k * rows_all + i * qblock, qblock), qblock)
-                x[rows, LANES : 2 * LANES] = rope(
-                    dkv[0, there, :] + dkv_tmp[0, rows, :], rows, -1.0
-                ).astype(jnp.bfloat16)
-                x[rows, 2 * LANES : ATT] = (dkv[1, there, :] + dkv_tmp[1, rows, :]).astype(jnp.bfloat16)
+                x[rows, LANES : 2 * LANES] = rope(dkv[0, there, :], rows, -1.0).astype(jnp.bfloat16)
+                x[rows, 2 * LANES : ATT] = dkv[1, there, :].astype(jnp.bfloat16)
                 return carry
 
             lax.fori_loop(0, qblocks, turn, 0)
@@ -649,13 +819,21 @@
             def _():
                 fetch_raw(i + 4, True)
 
-            @pl.when(i < lead)
-            def _():
-                gather_tick(i)
+            @pl.when(i == 0)
+            def _():
+                gather_tick(0)
+
+            @pl.when(i == 1)
+            def _():
+                gather_tick(last)
+
+            @pl.when((i >= 2) & (i <= last))
+            def _():
+                gather_tick((i - 1) * last + i - 1)
 
             return carry
 
-        lax.fori_loop(0, max(units - 2, norm_blocks, lead), begin_step, 0)
+        lax.fori_loop(0, max(units - 2, norm_blocks, n), begin_step, 0)
         cot_copy.wait()
         next_weights(0)
         vec[...] = jnp.zeros_like(vec)
@@ -663,9 +841,12 @@
 
         def super_step(s, carry):
             at = s * per_step
-            hidden_unit(3 * s, 2 * s, at)
-            attention_unit(3 * s + 1, s, at + in_hidden)
-            hidden_unit(3 * s + 2, 2 * s + 1, at + in_hidden + in_attention)
+            out_at = s * (2 * out_hidden + out_attention)
+            hidden_unit(3 * s, 2 * s, at, out_at, True)
+            attention_unit(3 * s + 1, s, at + in_hidden, out_at + out_hidden)
+            hidden_unit(
+                3 * s + 2, 2 * s + 1, at + in_hidden + in_attention, out_at + out_hidden + out_attention, False
+            )
             return carry
 
         lax.fori_loop(0, steps, super_step, 0)
@@ -674,9 +855,7 @@
         exchange(units - 2).wait_send()
         exchange(units - 1).wait_send()
 
-        @pl.when(k == 1)
-        def _():
-            send_dkv(steps - 1).wait_send()
+        sent(steps - 1)
 
 
     square = peers == 4
@@ -734,6 +913,9 @@
         fetch_xs.start()
         fetch_tile(0).start()
         fetch_swapped(units - 1, swap_in)
+        prepare(units - 1, swap_in)
+        wait_put(units - 2)
+        wait_put(units - 1)
         fetch_xs.wait()
         block = min(512, rows_all)
 
@@ -759,9 +941,15 @@
 
             lax.fori_loop(0, rows_all // block, one, 0)
 
-        scatter_from = units * last - behind
-        scatter_count = last * (LAG - 1) + 1 + behind
+        scatter_at = steps * (2 * out_hidden + out_attention) - behind
+        scatter_count = (units - 1) * last + last * LAG + 1 - scatter_at
         remote = 2 * (peers - 1)
+        tile_count = scatter_count * 2 // 5 // remote
+        rest_at, rest_count = scatter_at + tile_count * remote, scatter_count - tile_count * remote
+        cuts = [rest_at + rest_count * share_of // 16 for share_of in (0, 2, 5, 8, 11, 13, 16)]
+
+        def rest(i):
+            run_ticks(0, 0, cuts[i], cuts[i + 1] - cuts[i])
 
         def remote_tile(i):
             def one(h, carry):
@@ -772,8 +960,7 @@
 
                 q = 2 * i + h
                 products(q, store)
-                low, high = q * scatter_count // remote, (q + 1) * scatter_count // remote
-                run_ticks(swap_in, 0, 0, scatter_from + low, high - low)
+                run_ticks(0, 0, scatter_at + q * tile_count, tile_count)
                 return carry
 
             lax.fori_loop(0, 2, one, 0)
@@ -821,13 +1008,14 @@
         for h in range(2):
 
             def store(r, what, value):
-                for a in range(block // half):
-                    held[what, r * (block // half) + a, :, h * part : (h + 1) * part] = value[
-                        a * half : (a + 1) * half
+                for a in range(block // HID):
+                    held[what, r * (block // HID) + a, :, h * part : (h + 1) * part] = value[
+                        a * HID : (a + 1) * HID
                     ]
 
             products(remote + h, store)
 
+        rest(0)
         if square:
             add_half(1, 1, lower, 1, 4)
             add_half(1, 2, upper, 0, 5)
@@ -862,7 +1050,7 @@
             lax.fori_loop(0, count, one, 0)
 
         def summed(what, r, rows):
-            value = held[what, r, :, :size]
+            value = held[what, r]
             for i in range(count):
                 value += xs[what * count + i, rows, :size].astype(jnp.float32)
             return value
@@ -874,12 +1062,13 @@
             token = xs[tok_at, rows, :size].astype(jnp.float32)
             return (token - stats[rows, 0:1]) * stats[rows, 1:2]
 
+        rest(1)
         collect(0)
 
         def first_pass(r, carry):
-            rows = pl.ds(pl.multiple_of(r * half, half), half)
+            rows = pl.ds(pl.multiple_of(r * HID, HID), HID)
             grad = summed(0, r, rows)
-            held[0, r, :, :size] = grad
+            held[0, r] = grad
             unit = unit_of(rows)
             scaled = grad * gain
             sums[0:8, rows] = lax.dot_general(
@@ -892,7 +1081,7 @@
             vec[NIN + 2 : NIN + 3, :] += jnp.sum(grad, 0, keepdims=True)
             return carry
 
-        lax.fori_loop(0, rows_all // half, first_pass, 0)
+        lax.fori_loop(0, rows_all // HID, first_pass, 0)
         for i in range(peers - 1):
             sums_copy(i).start()
         to_core = pltpu.make_async_remote_copy(
@@ -900,26 +1089,28 @@
             device_id=other_core, device_id_type=MESH,
         )
         to_core.start()
+        rest(2)
         for i in range(peers - 1):
             sums_copy(i).wait_recv()
         inv_width = 1.0 / width
 
         def second_pass(r, carry):
-            rows = pl.ds(pl.multiple_of(r * half, half), half)
+            rows = pl.ds(pl.multiple_of(r * HID, HID), HID)
             means = sums[:, rows]
             for i in range(peers - 1):
                 means += sums_in[i, :, rows]
             means = (means * inv_width).T
             unit = unit_of(rows)
-            held[0, r, :, :size] = stats[rows, 1:2] * (
-                held[0, r, :, :size] * gain - means[:, 0:1] - unit * means[:, 8:9]
+            held[0, r] = stats[rows, 1:2] * (
+                held[0, r] * gain - means[:, 0:1] - unit * means[:, 8:9]
             ) + xs[cot_at, rows, :size].astype(jnp.float32)
             return carry
 
-        lax.fori_loop(0, rows_all // half, second_pass, 0)
-        put_grad = pltpu.make_async_copy(held.at[0, :, :, pl.ds(0, size)], token_grad, out_sem.at[0])
+        lax.fori_loop(0, rows_all // HID, second_pass, 0)
+        put_grad = pltpu.make_async_copy(held.at[0, pl.ds(0, rows_all // HID)], token_grad, out_sem.at[0])
         put_grad.start()
 
+        rest(3)
         to_core.wait_recv()
         vec_line[z] = vec[...] + vec_core[...]
 
@@ -965,18 +1156,20 @@
         for i in range(peers - 1):
             along_tensor(i).start()
 
+        rest(4)
         collect(1)
         out_bias = vec_ref[NIN : NIN + 1, columns]
 
         def third_pass(r, carry):
-            rows = pl.ds(pl.multiple_of(r * half, half), half)
+            rows = pl.ds(pl.multiple_of(r * HID, HID), HID)
             value = xs[tok_at, rows, :size].astype(jnp.float32) + (summed(1, r, rows) + out_bias)
             xs[out_at, rows, :size] = value.astype(jnp.bfloat16)
             return carry
 
-        lax.fori_loop(0, rows_all // half, third_pass, 0)
+        lax.fori_loop(0, rows_all // HID, third_pass, 0)
         put_result = pltpu.make_async_copy(xs.at[out_at, :, pl.ds(0, size)], result, out_sem.at[1])
         put_result.start()
+        rest(5)
 
         for i in range(peers - 1):
             from_tensor(i).wait_recv()
@@ -994,7 +1187,7 @@
             tensor_copy(blocks, 1, i).wait_send()
 
     low, wide = jnp.bfloat16, jnp.float32
-    window, qblock = rows_all + min(256, rows_all), min(256, rows_all)
+    window, qblock = rows_all + 256, 256
     pl.run_scoped(
         forward_backward,
         pltpu.VMEM((rows_all, width), low),
@@ -1005,20 +1198,20 @@
         pltpu.VMEM((2, size, WIDE), low),
         pltpu.VMEM((n, size, WIDE), low),
         pltpu.VMEM((rows_all, WIDE), low),
-        pltpu.VMEM((rows_all, LANES), low),
-        pltpu.VMEM((rows_all, LANES), low),
+        pltpu.VMEM((2, rows_all, LANES), low),
         pltpu.VMEM((2, 2 * rows_all, LANES), wide),
+        pltpu.VMEM((2, 256, LANES), wide),
         pltpu.VMEM((2, rows_all, LANES), wide),
         pltpu.VMEM((window, qblock), wide),
-        pltpu.VMEM((2, n, half, WIDE), low),
-        pltpu.VMEM((n, half, WIDE), low),
+        pltpu.VMEM((2, n, HID, size), low),
+        pltpu.VMEM((n, HID, size), low),
     )
     pl.run_scoped(
         finals,
         pltpu.VMEM((max(units, 2 * peers + 1), rows_all, WIDE), low),
         pltpu.VMEM((2, units, size // 2, WIDE), low),
         pltpu.VMEM((2, peers - 1, rows_all, size), low),
-        pltpu.VMEM((n, half, WIDE), low),
+        pltpu.VMEM((n, HID, size), low),
         pltpu.VMEM((rows_all // 2, size), low),
     )
 
@@ -1042,12 +1235,12 @@
             def _():
                 hop(1, g, 0, z).wait_send()
 
-            @pl.when(g >= units - (LAG + 2))
+            @pl.when(g >= units - boxes)
             def _():
                 keep(g).wait()
-                share(g, mine).wait_send()
-
-            share(g, theirs).wait_recv()
+                share(g, my_part).wait_send()
+
+            share(g, their_part).wait_recv()
 
         @pl.when(z >= s)
         def _():
@@ -1082,9 +1275,8 @@
     size, cols_all = in_weight.shape[1:]
     steps = cols_all // LANES
     units = 3 * steps
-    half = size // 2
     rows, width = tokens.shape
-    assert width == n * size == peers * cols_all and size == cols_all and rows == n * half
+    assert width == n * size == peers * cols_all and size == cols_all and rows <= n * HID
     low, wide = jnp.bfloat16, jnp.float32
     anywhere = pl.BlockSpec(memory_space=pl.ANY)
     vm = pl.BlockSpec(memory_space=pltpu.VMEM)
@@ -1094,21 +1286,26 @@
         out_shape=(
             jax.ShapeDtypeStruct((units, n, size, WIDE), low),
             jax.ShapeDtypeStruct((units, rows, WIDE), low),
-            jax.ShapeDtypeStruct((units, size, WIDE), wide),
-            jax.ShapeDtypeStruct((units, n, half, WIDE), low),
+            jax.ShapeDtypeStruct((units, WIDE, size), wide),
+            jax.ShapeDtypeStruct((units, n, HID, size), low),
+            jax.ShapeDtypeStruct((units, n, HID, size), wide),
             jax.ShapeDtypeStruct((steps, 2, rows, LANES), wide),
             jax.ShapeDtypeStruct((2, peers - 1, rows, size), low),
             jax.ShapeDtypeStruct((rows, size), low),
-            jax.ShapeDtypeStruct((n, half, size), wide),
+            jax.ShapeDtypeStruct((rows // HID, HID, size), wide),
             jax.ShapeDtypeStruct((peers, 16, size), wide),
         ),
         in_specs=[anywhere] * 4 + [vm] * 5,
-        out_specs=[anywhere] * 8 + [vm],
+        out_specs=[anywhere] * 9 + [vm],
         scratch_shapes=[
             pltpu.VMEM((steps, 2, 2 * rows, LANES), low),
-            pltpu.VMEM((schedule(n)[-1], n, half, WIDE), wide),
-            pltpu.VMEM((units, n + 1, half, WIDE), low),
-            pltpu.VMEM((LAG + 2, half, WIDE), wide),
+            pltpu.VMEM((steps, 2, 256, LANES), low),
+            pltpu.VMEM((steps, 2, 256, LANES), wide),
+            pltpu.VMEM((steps, 2, 256, LANES), wide),
+            pltpu.VMEM((2, n, HID, size), wide),
+            pltpu.VMEM((2, 2, HID, size), wide),
+            pltpu.VMEM((units, n + 1, HID, size), low),
+            pltpu.VMEM((3, HID, size), wide),
             pltpu.VMEM((rows, LANES), wide),
             pltpu.VMEM((16, size), wide),
             pltpu.VMEM((16, size), wide),
@@ -1131,6 +1328,12 @@
             dma((steps,)),
             dma((steps,)),
             dma((steps,)),
+            dma((steps,)),
+            dma((steps,)),
+            dma((steps,)),
+            dma((steps,)),
+            dma((steps,)),
+            dma((steps,)),
             dma,
             dma,
             dma,
@@ -1138,6 +1341,9 @@
             dma((2,)),
             dma((2,)),
             dma,
+            dma((2,)),
+            dma((2, 2)),
+            dma((3,)),
             dma((2, 6 if peers == 4 else peers - 1)),
             dma((2, 6 if peers == 4 else peers - 1)),
             dma((peers - 1,)),
@@ -1163,7 +1369,7 @@
         for c, piece in enumerate(pieces):
             part = slice(c * LANES, (c + 1) * LANES)
             at = (0, part) if turned else (0, slice(None), part)
-            gradient = piece[0].T if turned else piece[0]
+            gradient = piece[0] if turned else piece[0].T
             new_w[at], new_m[at], new_v[at] = adamw(
                 w[at], gradient, m[at], v[at], rate_matrix, weight_decay
             )
@@ -1191,7 +1397,7 @@
         lane = jnp.where(
             group < lead, jnp.where(is_in, group, 3), c % 2 + jnp.where(is_in, 0, 2)
         )
-        return unit, 0, lane
+        return unit, lane, 0
 
     in_spec = pl.BlockSpec((1, size, cols_all), lambda g: (jnp.minimum(g, into - 1), 0, 0))
     out_spec = pl.BlockSpec((1, cols_all, size), lambda g: (jnp.maximum(g - into, 0), 0, 0))
@@ -1199,7 +1405,7 @@
         functools.partial(adam_kernel, into, chunks),
         grid=(into + outof,),
         out_shape=tuple(jax.ShapeDtypeStruct(v.shape, jnp.float32) for v in in_arrays + out_arrays),
-        in_specs=[pl.BlockSpec((1, size, LANES), functools.partial(place, c)) for c in range(chunks)]
+        in_specs=[pl.BlockSpec((1, LANES, size), functools.partial(place, c)) for c in range(chunks)]
         + [in_spec] * 3
         + [out_spec] * 3,
         out_specs=[in_spec] * 3 + [out_spec] * 3,
@@ -1270,8 +1476,8 @@
         1,
     ).reshape(3 * steps, 1, WIDE)
     by_group = jnp.transpose(in_weight, (1, 0, 2))
-    _, _, total, _, _, _, result, token_grad, vec_grad = run_block(
-        by_group, out_weight, tokens, cotangent, bias, vectors, tables[0], tables[1], begin[None]
+    _, _, total, _, _, _, _, result, token_grad, vec_grad = run_block(
+        by_group, out_weight, tokens, cotangent, bias, vectors, tables[0], tables[1], begin_all[None]
     )
     token_grad = token_grad.reshape(local_rows, slice_width)
     vector_grad = jnp.transpose(vec_grad, (1, 0, 2)).reshape(-1, model_width)[: NIN + 3]

time: 453 us -> 440 us (0.971)
  Pallas kernels: 440 us -> 426 us
    pallas_call x1, Pallas kernels: 407 us -> 393 us  [run_block(): pl.pallas_call(functools.partial(block_kernel, n, steps, peers), out_shap...]
where the time goes in v4:
time: 440 us; the launch traced here: 438 us
  Pallas kernels  426 us (97%)
  other arithmetic  5.57 us (1%)
  local copies, waits for them, and re-layouts  4.97 us (1%)
    pallas_call x1, Pallas kernels, run_block(): pl.pallas_call(functools.partial(block_kernel, n, steps, peers), out_shap...  393 us
    pallas_call x1, Pallas kernels, adam_weights(): pl.pallas_call(functools.partial(adam_kernel, into, chunks), grid=(into +...  33.1 us

profile of v4, /device:TPU:0, one launch (start us, length us, event | category | flops | bytes accessed | tf_op | source)
XLA Modules:
  0.0 437.7 jit_solution(6291195621374006491)
XLA Ops:
  0.6 0.8 reduce-window.4
  1.5 0.7 fusion.7
  2.2 0.1 convert_reduce_fusion
  2.3 0.1 select_reduce_fusion
  2.3 0.0 copy-start.5
  2.4 0.8 slice.21
  3.2 0.1 dynamic-slice
  3.4 0.6 reshape.84.bias_ref
  4.1 3.0 fusion.1
  7.1 0.0 copy-done.5
  7.1 0.0 copy-start.2
  7.1 0.0 copy-start.3
  7.2 0.0 copy-start.4
  7.2 392.9 %parallel_block.1 = (bf16[12,4,512,512]{3,2,1,0:T(8,128)(2,1)}, bf16[12,1024,512]{2,1,0:T(8,128)(2,1)}, f32[12,512,512]{2,1,0:T(8,128)}, bf16[12,4,256,512]{3,2,...) custom-call(f32[7,512,512]{2,1,0:T(8,128)} %bitcast.29, ...), custom_call_target="tpu_custom_call" | custom-call | tf_op jit(solution)/shard_map/parallel_block/pallas_call | solution.py:1284
  400.0 1.0 copy.32
  401.1 0.0 copy-done.2
  401.1 0.0 copy-done.3
  401.1 0.0 copy-done.4
  401.1 0.8 multiply_subtract_fusion
  401.9 33.1 %adam_weights.1 = (f32[7,512,512]{2,1,0:T(8,128)}, f32[7,512,512]{2,1,0:T(8,128)}, f32[7,512,512]{2,1,0:T(8,128)}, f32[5,512,512]{2,1,0:T(8,128)}, f32[5,512,512]{2,1,0:T(8,128)}, /*index=5*/f32[5,512,512]{2,1,0:T(8,128)}) custom-call(f32[12,512,512]{2,1,0:T(8,128)} %get-tuple-element.23.refs_0_.refs_1_.refs_2_.refs_3_, ...), custom_call_target="tpu_custom_call" | custom-call | tf_op jit(solution)/shard_map/adam_weights/pallas_call | solution.py:1404
  435.1 0.0 copy-done.1
  435.1 1.0 copy.36
  436.0 0.0 copy-done
  436.0 1.3 copy.37
  (17 shorter events, 0.2 us)
Async XLA Ops:
  2.3 4.8 %copy-start.5 = (s32[2048]{0:T(1024)}, s32[2048]{0:T(1024)S(1)}, u32[]{:S(2)}) copy-start(s32[2048]{0:T(1024)S(1)} %select_reduce_fusion) | copy-start | bytes 24580
  7.1 393.9 %copy-start.2 = (f32[10,2048]{1,0:T(8,128)S(1)}, f32[10,2048]{1,0:T(8,128)}, u32[]{:S(2)}) copy-start(f32[10,2048]{1,0:T(8,128)} %vec_ref.1) | copy-start | bytes 245764
  7.1 393.9 %copy-start.3 = (f32[10,2048]{1,0:T(8,128)S(1)}, f32[10,2048]{1,0:T(8,128)}, u32[]{:S(2)}) copy-start(f32[10,2048]{1,0:T(8,128)} %param.22) | copy-start | bytes 245764
  7.2 394.0 %copy-start.4 = (f32[10,2048]{1,0:T(8,128)S(1)}, f32[10,2048]{1,0:T(8,128)}, u32[]{:S(2)}) copy-start(f32[10,2048]{1,0:T(8,128)} %param.23) | copy-start | bytes 245764
  401.9 33.2 %copy-start.1 = (bf16[1024,512]{1,0:T(8,128)(2,1)S(1)}, bf16[1024,512]{1,0:T(8,128)(2,1)}, u32[]{:S(2)}) copy-start(bf16[1024,512]{1,0:T(8,128)(2,1)} %get-tuple-element.49) | copy-start | bytes 3145732
  401.9 34.1 %copy-start = (f32[4,256,512]{2,1,0:T(8,128)S(1)}, f32[4,256,512]{2,1,0:T(8,128)}, u32[]{:S(2)}) copy-start(f32[4,256,512]{2,1,0:T(8,128)} %get-tuple-element.22) | copy-start | bytes 6291460
